TPU v7x, 256 devices: a whole 4x4x8 slice. The times are simulated.
256 devices in a mesh: blk: 16 (over z, y_hi), exp: 16 (over x, y_lo, core).
Axes of the slice: x: 4, y: 4 (y_hi: 2, y_lo: 2; y = y_hi * 2 + y_lo), z: 8, core: 2. Of those that a mesh axis runs over, the one named last changes fastest.
Arguments:
- grad_block: bfloat16 [512, 256, 2048], P('exp', 'blk'), may hold values from -6 to 6
- momentum: float32 [512, 256, 2048], P('exp', 'blk'), may hold values from -6 to 6
- model_root: bfloat16 [2048, 2048], P('blk'), may hold values from -0.125 to 0.125
- expert_root: bfloat16 [512, 512], replicated, may hold values from -0.25 to 0.25
Outputs:
- momentum_new: float32 [512, 256, 2048], P('exp', 'blk')
All inputs are finite; a program needn't handle non-finite values.
Results may differ from a plain program's by a relative error of at most 0.0031.
Values may be sent and summed in bfloat16 or wider, within the bound.
No kernel may reach another device: no remote copies, remote signals or barrier semaphores. Data moves between devices by JAX's collectives and lax.ppermute only.
A program may use at most 64 MiB of HBM per device.

v0:
```python
import jax
import jax.numpy as jnp
from jax import lax
from jax.sharding import PartitionSpec as P


def per_device(grad_block, momentum, model_root, expert_root):
    local_experts, local_hidden, width = grad_block.shape
    flat_rows = grad_block.reshape(local_experts * local_hidden, width)
    products = lax.dot_general(
        flat_rows,
        lax.all_gather(model_root, "blk", axis=0, tiled=True),
        (((1,), (1,)), ((), ())),
        preferred_element_type=jnp.float32,
    )
    model_mode = products.astype(jnp.bfloat16).reshape(local_experts, local_hidden, width)
    swapped = lax.all_to_all(model_mode, "exp", split_axis=2, concat_axis=0, tiled=True)
    all_experts, items, columns = swapped.shape
    blended = jnp.dot(
        expert_root,
        swapped.reshape(all_experts, items * columns),
        preferred_element_type=jnp.float32,
    )
    blended = blended.astype(jnp.bfloat16).reshape(all_experts, items, columns)
    restored = lax.all_to_all(blended, "exp", split_axis=0, concat_axis=2, tiled=True)
    return 0.9 * momentum + restored.astype(jnp.float32)


def solution(mesh):
    placed = (P("exp", "blk", None), P("exp", "blk", None), P("blk", None), P())
    return jax.shard_map(
        per_device, mesh=mesh, in_specs=placed, out_specs=P("exp", "blk", None), check_vma=False
    )
```

profile of v0, /device:TPU:1, one launch (start us, length us, event | category | flops | bytes accessed | tf_op | source)
XLA Modules:
  0.0 291.2 jit_solution(11429465256965235366)
XLA Ops:
  6.5 0.0 copy-start
  6.5 0.0 all-gather.2.cloned.1.call-start
  6.5 0.7 all-gather.2.cloned.1.call-update
  7.3 142.0 %all-gather.2.cloned.1.call-done = bf16[2048,2048]{1,0:T(8,128)(2,1)} async-done(((bf16[128,2048]{1,0:T(8,128)(2,1)}), bf16[2048,2048]{1,0:T(8,128)(2,1)}) %all-gather.2.cloned.1.call-update) | async-done | bytes 8388624 | tf_op jit(solution)/shard_map/all_gather | solution.py:12
  149.2 0.0 copy-done
  149.2 9.1 %convolution_convert_fusion.1 = bf16[512,2048]{1,0:T(8,128)(2,1)} fusion(bf16[512,2048]{1,0:T(8,128)(2,1)S(1)} %bitcast.27, bf16[2048,2048]{1,0:T(8,128)(2,1)} %all-gather.2.cloned.1.call-done), kind=kOutput, calls=%fused_computation.3 | convolution fusion | flops 4296015872 | bytes 12582912 | tf_op jit(solution)/shard_map/dot_general | solution.py:10
  158.3 12.9 %copy.15 = bf16[32,16,2048]{0,1,2:T(8,128)(2,1)} copy(bf16[32,16,2048]{2,1,0:T(8,128)(2,1)} %bitcast.31) | data formatting | bytes 4194304 | tf_op jit(solution)/shard_map/reshape | solution.py:16
  171.2 14.5 %reshape.23 = bf16[16,2,32768]{2,1,0:T(2,128)(2,1)} reshape(bf16[2048,16,32]{2,1,0:T(8,128)(2,1)} %bitcast.28) | data formatting | bytes 4194304
  185.6 32.0 %all_to_all.24 = bf16[16,2,32768]{2,1,0:T(2,128)(2,1)} all-to-all(bf16[16,2,32768]{2,1,0:T(2,128)(2,1)} %reshape.23), channel_id=1, replica_groups=mesh['blk'=16,'exp'=16] {'exp'}, dimensions={0} | all-to-all | bytes 4194304 | tf_op jit(solution)/shard_map/all_to_all | solution.py:17
  217.6 12.9 %reshape.24 = bf16[2048,16,32]{2,1,0:T(8,128)(2,1)} reshape(bf16[16,2,32768]{2,1,0:T(2,128)(2,1)} %all_to_all.24) | data formatting | bytes 4194304
  230.5 0.0 copy-start.2
  230.5 10.8 %copy.17 = bf16[16,32,16,128]{3,2,1,0:T(8,128)(2,1)} copy(bf16[16,32,16,128]{1,2,3,0:T(8,128)(2,1)} %bitcast.29) | data formatting | bytes 4194304 | tf_op jit(solution)/shard_map/all_to_all | solution.py:17
  241.3 0.0 copy-done.2
  241.3 4.3 %convolution_convert_fusion = bf16[2048,512]{1,0:T(8,128)(2,1)} fusion(bf16[512,512]{1,0:T(8,128)(2,1)S(1)} %copy-done.2, bf16[64,8,16,128]{3,2,1,0:T(8,128)(2,1)} %bitcast.32), kind=kOutput, calls=%fused_computation.2 | convolution fusion | flops 1074790400 | bytes 4718592 | tf_op jit(solution)/shard_map/dot_general | solution.py:19
  245.6 4.5 %copy.18 = bf16[512,16,128]{2,1,0:T(8,128)(2,1)} copy(bf16[512,16,128]{0,2,1:T(8,128)(2,1)} %bitcast.33) | data formatting | bytes 4194304 | tf_op jit(solution)/shard_map/reshape | solution.py:24
  250.1 0.0 copy-start.1
  250.1 31.6 %all_to_all.25 = bf16[512,16,128]{2,1,0:T(8,128)(2,1)S(1)} all-to-all(bf16[512,16,128]{2,1,0:T(8,128)(2,1)} %copy.18), channel_id=1, replica_groups=mesh['blk'=16,'exp'=16] {'exp'}, dimensions={0} | all-to-all | bytes 4194304 | tf_op jit(solution)/shard_map/all_to_all | solution.py:25
  281.7 0.0 copy-done.1
  281.7 2.7 bitcast_add_fusion
Async XLA Ops:
  6.5 142.7 %copy-start = (bf16[32,16,2048]{2,1,0:T(8,128)(2,1)S(1)}, bf16[32,16,2048]{2,1,0:T(8,128)(2,1)}, u32[]{:S(2)}) copy-start(bf16[32,16,2048]{2,1,0:T(8,128)(2,1)} %param.4) | copy-start | bytes 6291460
  6.5 142.7 %all-gather.2.cloned.1.call-start = ((), (), s32[]{:S(2)}) async-start(), calls=%async_computation.2 | async-start | bytes 8912896 | tf_op jit(solution)/shard_map/all_gather | solution.py:12
  230.5 10.8 %copy-start.2 = (bf16[512,512]{1,0:T(8,128)(2,1)S(1)}, bf16[512,512]{1,0:T(8,128)(2,1)}, u32[]{:S(2)}) copy-start(bf16[512,512]{1,0:T(8,128)(2,1)} %param.7) | copy-start | bytes 1572868
  250.1 31.6 %copy-start.1 = (f32[32,16,2048]{2,1,0:T(8,128)S(1)}, f32[32,16,2048]{2,1,0:T(8,128)}, u32[]{:S(2)}) copy-start(f32[32,16,2048]{2,1,0:T(8,128)} %param.5) | copy-start | bytes 12582916
Sparse Core Ops, SparseCore 0:
  9.9 139.2 all-gather.1
where the time goes:
time: 292 us; the launch traced here: 291 us
  waiting for transfers between devices  143 us (49%)
  blocking collectives  63.6 us (22%)
  local copies, waits for them, and re-layouts  55.6 us (19%)
  matrix products  13.4 us (5%)
  between operations  13.4 us (5%)
    all_gather x1, waiting for transfers between devices, per_device(): lax.all_gather(model_root, 'blk', axis=0, tiled=True)  142 us
    all_to_all x1, blocking collectives, per_device(): lax.all_to_all(model_mode, 'exp', split_axis=2, concat_axis=0, tiled=True)  32 us
    all_to_all x1, blocking collectives, per_device(): lax.all_to_all(blended, 'exp', split_axis=0, concat_axis=2, tiled=True)  31.6 us
    unnamed x8, local copies, waits for them, and re-layouts  27.4 us
    reshape x1, local copies, waits for them, and re-layouts, per_device(): products.astype(jnp.bfloat16).reshape(local_experts, local_hidden, width)  12.9 us
    all_to_all x1, local copies, waits for them, and re-layouts, per_device(): lax.all_to_all(model_mode, 'exp', split_axis=2, concat_axis=0, tiled=True)  10.8 us
    dot_general x1, matrix products, per_device(): lax.dot_general(flat_rows, lax.all_gather(model_root, 'blk', axis=0, tile...  9.09 us
  transfers between devices with their start and end apart: 1, of which 1 were waited for; matrix products, arithmetic and copies ran while one was open for 0% of the time, Pallas kernels for 0%

commit v1 on v0

v1 whole, which is shorter than its diff:
```python
import jax
import jax.numpy as jnp
from jax import lax
from jax.experimental import pallas as pl
from jax.experimental.pallas import tpu as pltpu
from jax.sharding import Mesh, PartitionSpec as P

NAMES = ("z", "yh", "x", "yl", "core")
SIZES = (8, 2, 4, 2, 2)
EXP = ("x", "yl", "core")
BLK = ("z", "yh")
PARTS = 16
LANES = 128
MIB = 1024 * 1024


def order_matrix(rows, outer, inner, transposed=False):
    first = lax.broadcasted_iota(jnp.int32, (rows, rows), 1 if transposed else 0)
    second = lax.broadcasted_iota(jnp.int32, (rows, rows), 0 if transposed else 1)
    source = (first & (inner - 1)) * outer + lax.div(first, inner)
    return jnp.where(source == second, 1.0, 0.0).astype(jnp.bfloat16)


def slice_kernel(experts, hidden, grad_ref, out_ref, order):
    @pl.when(pl.program_id(0) == 0)
    def _():
        order[...] = order_matrix(experts * hidden, hidden, experts)

    moved = jnp.dot(order[...], grad_ref[...], preferred_element_type=jnp.float32)
    moved = moved.astype(jnp.bfloat16)
    out_ref[0] = moved[:, :LANES]
    out_ref[1] = moved[:, LANES:]


def sliced(grad, experts, hidden):
    rows, width = grad.shape
    return pl.pallas_call(
        lambda *refs: slice_kernel(experts, hidden, *refs),
        out_shape=jax.ShapeDtypeStruct((PARTS, rows, LANES), jnp.bfloat16),
        grid=(PARTS // 2,),
        in_specs=[pl.BlockSpec((rows, 2 * LANES), lambda s: (0, s))],
        out_specs=pl.BlockSpec((2, rows, LANES), lambda s: (s, 0, 0)),
        scratch_shapes=[pltpu.VMEM((rows, rows), jnp.bfloat16)],
        cost_estimate=pl.CostEstimate(
            flops=2 * rows * rows * width, bytes_accessed=4 * rows * width, transcendentals=0
        ),
        name="slice_columns",
    )(grad)


def mix_kernel(root_ref, in_ref, out_ref):
    groups, _, experts, lanes = in_ref.shape
    pair = jnp.concatenate(
        [in_ref[:, 0].reshape(groups * experts, lanes), in_ref[:, 1].reshape(groups * experts, lanes)], axis=1
    )
    mixed = jnp.dot(root_ref[...], pair, preferred_element_type=jnp.float32).astype(jnp.bfloat16)
    out_ref[:, 0] = mixed[:, :lanes].reshape(groups, experts, lanes)
    out_ref[:, 1] = mixed[:, lanes:].reshape(groups, experts, lanes)


def mixed_experts(expert_root, held):
    groups, hidden, experts, lanes = held.shape
    block = pl.BlockSpec((groups, 2, experts, lanes), lambda s: (0, s, 0, 0))
    total = groups * experts
    return pl.pallas_call(
        mix_kernel,
        out_shape=jax.ShapeDtypeStruct(held.shape, jnp.bfloat16),
        grid=(hidden // 2,),
        in_specs=[pl.BlockSpec((total, total), lambda s: (0, 0)), block],
        out_specs=block,
        cost_estimate=pl.CostEstimate(
            flops=2 * total * total * hidden * lanes, bytes_accessed=4 * total * hidden * lanes, transcendentals=0
        ),
        name="mix_experts",
    )(expert_root, held)


def finish_kernel(experts, hidden, yh_ref, held_ref, root_ref, momentum_ref, out_ref, rows_ref):
    half = root_ref.shape[-1]
    per_half = half // LANES
    rows = experts * hidden

    @pl.when(pl.program_id(0) == 0)
    def _():
        order = order_matrix(rows, hidden, experts, transposed=True)
        for part in range(0, PARTS, 2):
            pair = jnp.concatenate([held_ref[part], held_ref[part + 1]], axis=1)
            moved = jnp.dot(order, pair, preferred_element_type=jnp.float32).astype(jnp.bfloat16)
            at = (part % per_half) * LANES
            rows_ref[part // per_half, :, at : at + 2 * LANES] = moved

    yh = yh_ref[0]
    total = 0.9 * momentum_ref[...]
    for which in range(2):
        root = jnp.concatenate([root_ref[which, 0, yh], root_ref[which, 0, 1 - yh]], axis=0)
        total += lax.dot_general(
            rows_ref[which], root, (((1,), (1,)), ((), ())), preferred_element_type=jnp.float32
        )
    out_ref[...] = total


def finished(yh, held, root, momentum, experts, hidden):
    parts, rows, lanes = held.shape
    halves, steps, pair, block, half = root.shape
    columns = pair * block
    width = steps * columns
    out_spec = pl.BlockSpec((rows, columns), lambda s, yh: (0, s))
    return pl.pallas_call(
        lambda *refs: finish_kernel(experts, hidden, *refs),
        out_shape=jax.ShapeDtypeStruct(momentum.shape, jnp.float32),
        grid_spec=pltpu.PrefetchScalarGridSpec(
            num_scalar_prefetch=1,
            grid=(steps,),
            in_specs=[
                pl.BlockSpec((parts, rows, lanes), lambda s, yh: (0, 0, 0)),
                pl.BlockSpec((halves, 1, pair, block, half), lambda s, yh: (0, s, 0, 0, 0)),
                out_spec,
            ],
            out_specs=out_spec,
            scratch_shapes=[pltpu.VMEM((halves, rows, half), jnp.bfloat16)],
        ),
        compiler_params=pltpu.CompilerParams(vmem_limit_bytes=40 * MIB),
        cost_estimate=pl.CostEstimate(
            flops=2 * rows * width * (width + rows), bytes_accessed=2 * width * width + 10 * rows * width, transcendentals=0
        ),
        name="model_rows",
    )(yh, held, root, momentum)


def swap(value, axis):
    return lax.ppermute(value, axis, [(0, 1), (1, 0)])


def per_device(grad_block, momentum, model_root, expert_root):
    experts, hidden, width = grad_block.shape
    rows = experts * hidden
    half = width // 2
    yh, core = lax.axis_index("yh"), lax.axis_index("core")

    mine = lax.dynamic_slice_in_dim(model_root, core * half, half, axis=1)
    both = jnp.stack([mine, swap(mine, "yh")])
    root = lax.all_gather(both, ("core", "z"), axis=0).reshape(2, SIZES[0], 2, -1, half)

    sent = sliced(grad_block.reshape(rows, width), experts, hidden)
    held = lax.all_to_all(sent, EXP, split_axis=0, concat_axis=0, tiled=True)
    blended = mixed_experts(expert_root, held.reshape(PARTS, hidden, experts, LANES))
    back = lax.all_to_all(
        blended.reshape(PARTS, rows, LANES), EXP, split_axis=0, concat_axis=0, tiled=True
    )
    place = yh.astype(jnp.int32)[None]
    out = finished(place, back, root, momentum.reshape(rows, width), experts, hidden)
    return out.reshape(experts, hidden, width)


def solution(mesh):
    fine = Mesh(mesh.devices.reshape(SIZES), NAMES)
    placed = (P(EXP, BLK, None), P(EXP, BLK, None), P(BLK, None), P())
    return jax.shard_map(
        per_device, mesh=fine, in_specs=placed, out_specs=P(EXP, BLK, None), check_vma=False
    )
```

time: 292 us -> 119 us (0.41)
  waiting for transfers between devices: 143 us -> 32 us
  local copies, waits for them, and re-layouts: 55.6 us -> 3.26 us
  blocking collectives: 63.6 us -> 34.2 us
  Pallas kernels: 0 us -> 25.4 us
  matrix products: 13.4 us -> 0 us
  starting transfers between devices: 0.01 us -> 8.58 us
    all_gather x1, waiting for transfers between devices: 142 us -> 0.01 us  [per_device(): lax.all_gather(both, ('core', 'z'), axis=0)]
    all_to_all x2 -> x1, blocking collectives: 63.6 us -> 34.2 us  [per_device(): held = lax.all_to_all(sent, EXP, split_axis=0, concat_axis=0, tiled=True)]
    all_to_all x0 -> x1, waiting for transfers between devices: none -> 27 us  [per_device(): lax.all_to_all(blended.reshape(PARTS, rows, LANES), EXP, split_axis=0, co...]
    pallas_call x0 -> x3, Pallas kernels: none -> 25.4 us  [the longest x1 11.6 us: finished(): pl.pallas_call(lambda *refs: finish_kernel(experts, hidden, *refs), out_s...]
    unnamed x8 -> x4, local copies, waits for them, and re-layouts: 27.4 us -> 3.23 us
    reshape x2 -> x0, local copies, waits for them, and re-layouts: 17.3 us -> none  [the longest x1 12.9 us: per_device(): products.astype(jnp.bfloat16).reshape(local_experts, local_hidden, width)]
    dot_general x2 -> x0, matrix products: 13.4 us -> none  [the longest x1 9.09 us: per_device(): lax.dot_general(flat_rows, lax.all_gather(model_root, 'blk', axis=0, tile...]
    all_to_all x1 -> x0, local copies, waits for them, and re-layouts: 10.8 us -> none  [per_device(): lax.all_to_all(model_mode, 'exp', split_axis=2, concat_axis=0, tiled=True)]
  transfers between devices with their start and end apart: 1 -> 3, of which waited for: 1 -> 2; matrix products, arithmetic and copies ran while one was open for 0% -> 0% of each run, Pallas kernels for 0% -> 12%
where the time goes in v1:
time: 119 us; the launch traced here: 118 us
  blocking collectives  34.2 us (29%)
  waiting for transfers between devices  32 us (27%)
  Pallas kernels  25.4 us (21%)
  between operations  13.4 us (11%)
  starting transfers between devices  8.58 us (7%)
  local copies, waits for them, and re-layouts  3.26 us (3%)
    all_to_all x1, blocking collectives, per_device(): held = lax.all_to_all(sent, EXP, split_axis=0, concat_axis=0, tiled=True)  34.2 us
    all_to_all x1, waiting for transfers between devices, per_device(): lax.all_to_all(blended.reshape(PARTS, rows, LANES), EXP, split_axis=0, co...  27 us
    pallas_call x1, Pallas kernels, finished(): pl.pallas_call(lambda *refs: finish_kernel(experts, hidden, *refs), out_s...  11.6 us
    pallas_call x1, Pallas kernels, mixed_experts(): pl.pallas_call(mix_kernel, out_shape=jax.ShapeDtypeStruct(held.shape, jnp...  6.96 us
    pallas_call x1, Pallas kernels, sliced(): pl.pallas_call(lambda *refs: slice_kernel(experts, hidden, *refs), out_sh...  6.82 us
    ppermute x1, waiting for transfers between devices, swap(): return lax.ppermute(value, axis, [(0, 1), (1, 0)])  4.95 us
    all_to_all x1, starting transfers between devices, per_device(): lax.all_to_all(blended.reshape(PARTS, rows, LANES), EXP, split_axis=0, co...  4.75 us
    ppermute x1, starting transfers between devices, swap(): return lax.ppermute(value, axis, [(0, 1), (1, 0)])  3.83 us
  transfers between devices with their start and end apart: 3, of which 2 were waited for; matrix products, arithmetic and copies ran while one was open for 0% of the time, Pallas kernels for 12%

profile of v1, /device:TPU:1, one launch (start us, length us, event | category | flops | bytes accessed | tf_op | source)
XLA Modules:
  0.0 117.7 jit_solution(532849046469170819)
XLA Ops:
  6.5 0.0 copy-start
  6.5 0.0 all-gather.3.cloned.1.call-start
  6.5 1.0 copy-done
  7.6 3.8 %collective-permute-start = (bf16[128,1024]{1,0:T(8,128)(2,1)S(1)}, bf16[128,1024]{1,0:T(8,128)(2,1)S(1)}, u32[]{:S(2)}, u32[]{:S(2)}) collective-permute-start(bf16[128,1024]{1,0:T(8,128)(2,1)S(1)} %constant_dynamic-slice_fusion), channel_id=1, source_target_pairs={{0,16},{16,0},{1,17},{17,1},{2,18},{18,2},{3,19},{19,3},{4,20},{20... | collective-permute-start | bytes 786440 | tf_op jit(solution)/shard_map/ppermute | solution.py:131
  11.5 4.9 %collective-permute-done = bf16[128,1024]{1,0:T(8,128)(2,1)S(1)} collective-permute-done((bf16[128,1024]{1,0:T(8,128)(2,1)S(1)}, bf16[128,1024]{1,0:T(8,128)(2,1)S(1)}, u32[]{:S(2)}, u32[]{:S(2)}) %collective-permute-start) | collective-permute-done | bytes 262176 | tf_op jit(solution)/shard_map/ppermute | solution.py:131
  16.4 0.9 pad_maximum_fusion
  17.3 0.0 all-gather.3.cloned.1.call-update
  17.3 6.8 %slice_columns.1 = bf16[16,512,128]{2,1,0:T(8,128)(2,1)} custom-call(bf16[512,2048]{1,0:T(8,128)(2,1)} %bitcast.13), custom_call_target="tpu_custom_call" | custom-call | flops 1073741824 | bytes 4194304 | tf_op jit(solution)/shard_map/slice_columns/pallas_call | solution.py:37
  24.1 34.2 %all_to_all.10 = bf16[16,512,128]{2,1,0:T(8,128)(2,1)} all-to-all(bf16[16,512,128]{2,1,0:T(8,128)(2,1)} %slice_columns.1), channel_id=1, replica_groups=mesh['z'=8,'yh'=2,'x'=4,'yl'=2,'core'=2] {'x','yl','core'}, dimensions={0} | all-to-all | bytes 4194304 | tf_op jit(solution)/shard_map/all_to_all | solution.py:145
  58.3 7.0 %mix_experts.1 = bf16[16,16,32,128]{3,2,1,0:T(8,128)(2,1)} custom-call(bf16[512,512]{1,0:T(8,128)(2,1)} %root_ref.1, bf16[16,16,32,128]{3,2,1,0:T(8,128)(2,1)} %bitcast.12), custom_call_target="tpu_custom_call" | custom-call | flops 1073741824 | bytes 4194304 | tf_op jit(solution)/shard_map/mix_experts/pallas_call | solution.py:65
  65.3 4.7 %all-to-all-start.1 = ((bf16[16,512,128]{2,1,0:T(8,128)(2,1)}), bf16[16,512,128]{2,1,0:T(8,128)(2,1)S(1)}, u32[]{:S(2)}, u32[]{:S(2)}) async-start(bf16[16,512,128]{2,1,0:T(8,128)(2,1)} %bitcast.11), calls=%async_computation.1 | async-start | bytes 4194304 | tf_op jit(solution)/shard_map/all_to_all | solution.py:147
  70.1 27.0 %all-to-all-done.1.refs_1_ = bf16[16,512,128]{2,1,0:T(8,128)(2,1)S(1)} async-done(((bf16[16,512,128]{2,1,0:T(8,128)(2,1)}), bf16[16,512,128]{2,1,0:T(8,128)(2,1)S(1)}, u32[]{:S(2)}, u32[]{:S(2)}) %all-to-all-start.1) | async-done | bytes 2097184 | tf_op jit(solution)/shard_map/all_to_all | solution.py:147
  97.1 0.0 all-gather.3.cloned.1.call-done
  97.1 0.0 copy-start.1
  97.1 2.2 %copy-done.1 = f32[32,16,2048]{2,1,0:T(8,128)S(1)} copy-done((f32[32,16,2048]{2,1,0:T(8,128)S(1)}, f32[32,16,2048]{2,1,0:T(8,128)}, u32[]{:S(2)}) %copy-start.1) | copy-done | bytes 4194328
  99.3 11.6 %model_rows.1 = f32[512,2048]{1,0:T(8,128)} custom-call(s32[1]{0:T(128)} %bitcast.refs_0_, bf16[16,512,128]{2,1,0:T(8,128)(2,1)S(1)} %all-to-all-done.1.refs_1_, bf16[2,8,2,128,1024]{4,3,2,1,0:T(8,128)(2,1)} %bitcast.15, f32[512,2048]{1,0:T(8,128)S(1)} %bitcast.10), custom_call_target="tpu_custom_call" | custom-call | flops 5368709120 | bytes 18874368 | tf_op jit(solution)/shard_map/model_rows/pallas_call | solution.py:108
  (2 shorter events, 0.0 us)
Async XLA Ops:
  6.5 1.0 copy-start
  6.5 90.5 %all-gather.3.cloned.1.call-start = ((), (), s32[]{:S(2)}) async-start(), calls=%async_computation.2 | async-start | bytes 8912896 | tf_op jit(solution)/shard_map/all_gather | solution.py:142
  7.6 8.8 %collective-permute-start = (bf16[128,1024]{1,0:T(8,128)(2,1)S(1)}, bf16[128,1024]{1,0:T(8,128)(2,1)S(1)}, u32[]{:S(2)}, u32[]{:S(2)}) collective-permute-start(bf16[128,1024]{1,0:T(8,128)(2,1)S(1)} %constant_dynamic-slice_fusion), channel_id=1, source_target_pairs={{0,16},{16,0},{1,17},{17,1},{2,18},{18,2},{3,19},{19,3},{4,20},{20... | collective-permute-start | bytes 786440 | tf_op jit(solution)/shard_map/ppermute | solution.py:131
  65.3 31.8 %all-to-all-start.1 = ((bf16[16,512,128]{2,1,0:T(8,128)(2,1)}), bf16[16,512,128]{2,1,0:T(8,128)(2,1)S(1)}, u32[]{:S(2)}, u32[]{:S(2)}) async-start(bf16[16,512,128]{2,1,0:T(8,128)(2,1)} %bitcast.11), calls=%async_computation.1 | async-start | bytes 4194304 | tf_op jit(solution)/shard_map/all_to_all | solution.py:147
  97.1 2.2 %copy-start.1 = (f32[32,16,2048]{2,1,0:T(8,128)S(1)}, f32[32,16,2048]{2,1,0:T(8,128)}, u32[]{:S(2)}) copy-start(f32[32,16,2048]{2,1,0:T(8,128)} %param.5) | copy-start | bytes 12582916
Sparse Core Ops, SparseCore 0:
  17.4 60.9 all-gather.2

commit v2 on v0

v2 whole, which is shorter than its diff:
```python
import jax
import jax.numpy as jnp
from jax import lax
from jax.experimental import pallas as pl
from jax.experimental.pallas import tpu as pltpu
from jax.sharding import Mesh, PartitionSpec as P

NAMES = ("z", "yh", "x", "yl", "core")
SIZES = (8, 2, 4, 2, 2)
EXP = ("x", "yl", "core")
BLK = ("z", "yh")
PARTS = 16
LANES = 128
MIB = 1024 * 1024
OFFSETS = (0, 1, -1, 2, -2, 3, -3, 4)
VMEM = pl.BlockSpec(memory_space=pltpu.VMEM)
ANY = pl.BlockSpec(memory_space=pl.ANY)


def order_matrix(rows, outer, inner):
    row = lax.broadcasted_iota(jnp.int32, (rows, 1), 0)
    source = (row & (outer - 1)) * inner + lax.shift_right_logical(row, outer.bit_length() - 1)
    column = lax.broadcasted_iota(jnp.int32, (rows, rows), 1)
    return jnp.where(source == column, 1.0, 0.0).astype(jnp.bfloat16)


def slice_kernel(experts, hidden, grad_ref, out_ref, grad, parts, in_sems, out_sems):
    pairs = PARTS // 2

    def arrival(pair):
        columns = pl.ds(pair * 2 * LANES, 2 * LANES)
        return pltpu.make_async_copy(grad_ref.at[:, columns], grad.at[pair], in_sems.at[pair])

    def departure(pair):
        both = pl.ds(2 * pair, 2)
        return pltpu.make_async_copy(parts.at[both], out_ref.at[both], out_sems.at[pair])

    for pair in range(pairs):
        arrival(pair).start()
    order = order_matrix(experts * hidden, experts, hidden)
    for pair in range(pairs):
        arrival(pair).wait()
        moved = jnp.dot(order, grad[pair], preferred_element_type=jnp.float32).astype(jnp.bfloat16)
        parts[2 * pair] = moved[:, :LANES]
        parts[2 * pair + 1] = moved[:, LANES:]
        departure(pair).start()
    for pair in range(pairs):
        departure(pair).wait()


def sliced(grad, experts, hidden):
    rows, width = grad.shape
    pairs = PARTS // 2
    return pl.pallas_call(
        lambda *refs: slice_kernel(experts, hidden, *refs),
        out_shape=jax.ShapeDtypeStruct((PARTS, rows, LANES), jnp.bfloat16),
        in_specs=[ANY],
        out_specs=ANY,
        scratch_shapes=[
            pltpu.VMEM((pairs, rows, 2 * LANES), jnp.bfloat16),
            pltpu.VMEM((PARTS, rows, LANES), jnp.bfloat16),
            pltpu.SemaphoreType.DMA((pairs,)),
            pltpu.SemaphoreType.DMA((pairs,)),
        ],
        compiler_params=pltpu.CompilerParams(vmem_limit_bytes=58 * MIB),
        cost_estimate=pl.CostEstimate(
            flops=2 * rows * rows * width, bytes_accessed=4 * rows * width, transcendentals=0
        ),
        name="slice_columns",
    )(grad)


def mix_kernel(root_ref, in_ref, out_ref, root, mixed, in_sem, out_sems):
    groups, hidden, experts, lanes = in_ref.shape

    def departure(h):
        there = (slice(None), pl.ds(h, 2))
        return pltpu.make_async_copy(mixed.at[there], out_ref.at[there], out_sems.at[h // 2])

    arrival = pltpu.make_async_copy(root_ref, root, in_sem)
    arrival.start()
    arrival.wait()
    for h in range(0, hidden, 2):
        pair = jnp.concatenate(
            [in_ref[:, at].reshape(groups * experts, lanes) for at in (h, h + 1)], axis=1
        )
        sums = jnp.dot(root[...], pair, preferred_element_type=jnp.float32).astype(jnp.bfloat16)
        mixed[:, h] = sums[:, :lanes].reshape(groups, experts, lanes)
        mixed[:, h + 1] = sums[:, lanes:].reshape(groups, experts, lanes)
        departure(h).start()
    for h in range(0, hidden, 2):
        departure(h).wait()


def mixed_experts(expert_root, held):
    groups, hidden, experts, lanes = held.shape
    total = groups * experts
    return pl.pallas_call(
        mix_kernel,
        out_shape=jax.ShapeDtypeStruct(held.shape, jnp.bfloat16),
        in_specs=[ANY, VMEM],
        out_specs=ANY,
        scratch_shapes=[
            pltpu.VMEM((total, total), jnp.bfloat16),
            pltpu.VMEM(held.shape, jnp.bfloat16),
            pltpu.SemaphoreType.DMA,
            pltpu.SemaphoreType.DMA((hidden // 2,)),
        ],
        compiler_params=pltpu.CompilerParams(vmem_limit_bytes=24 * MIB),
        cost_estimate=pl.CostEstimate(
            flops=2 * total * total * hidden * lanes, bytes_accessed=4 * total * hidden * lanes, transcendentals=0
        ),
        name="mix_experts",
    )(expert_root, held)


def finish_kernel(experts, hidden, pieces, place_ref, held_ref, *refs):
    sources = refs[:pieces], refs[pieces : 2 * pieces]
    momentum_ref, out_ref, held_parts, roots, momentum, out, sums = refs[2 * pieces : 2 * pieces + 7]
    held_sem, root_sems, momentum_sems, out_sems = refs[2 * pieces + 7 :]
    steps, rows, columns = out.shape
    per_half = PARTS // 2
    yh, core = place_ref[0], place_ref[1]

    def block(ref, step):
        return ref.at[:, pl.ds(pl.multiple_of(place_ref[2 + step] * columns, columns), columns)]

    def root_arrivals(side, step):
        pieces_of, sem = sources[side], root_sems.at[side]
        if step < steps - 1:
            return [pltpu.make_async_copy(pieces_of[step], roots.at[side, step], sem.at[step])]
        return [
            pltpu.make_async_copy(pieces_of[step + k], roots.at[side, step, k], sem.at[step + k]) for k in range(2)
        ]

    def momentum_arrival(step):
        return pltpu.make_async_copy(block(momentum_ref, step), momentum.at[step], momentum_sems.at[step])

    def departure(step):
        return pltpu.make_async_copy(out.at[step], block(out_ref, step), out_sems.at[step])

    held_arrival = pltpu.make_async_copy(held_ref, held_parts, held_sem)
    held_arrival.start()
    for step in range(steps):
        for copy in (*root_arrivals(0, step), *root_arrivals(1, step), momentum_arrival(step)):
            copy.start()
    held_arrival.wait()
    for step in range(steps):
        total = None
        for side, which in ((0, core), (1, 1 - core)):
            for copy in root_arrivals(side, step):
                copy.wait()
            held = jnp.concatenate([held_parts[which * per_half + part] for part in range(per_half)], axis=1)
            root = roots[side, step].reshape(columns, per_half * LANES)
            term = lax.dot_general(held, root, (((1,), (1,)), ((), ())), preferred_element_type=jnp.float32)
            total = term if total is None else total + term
        sums[yh] = total[:, :LANES]
        sums[1 - yh] = total[:, LANES:]
        momentum_arrival(step).wait()
        for tile in range(columns // LANES):
            lanes = slice(tile * LANES, (tile + 1) * LANES)
            for expert in range(experts):
                there = slice(expert * hidden, (expert + 1) * hidden)
                change = sums[tile, pl.ds(expert, hidden, stride=experts), :]
                out[step, there, lanes] = 0.9 * momentum[step, there, lanes] + change
        departure(step).start()
    for step in range(steps):
        departure(step).wait()


def finished(place, held, own, other, momentum, experts, hidden):
    parts, rows, lanes = held.shape
    width = parts * lanes
    columns = 2 * LANES
    pieces, steps = len(own), len(OFFSETS)
    return pl.pallas_call(
        lambda *refs: finish_kernel(experts, hidden, pieces, *refs),
        out_shape=jax.ShapeDtypeStruct(momentum.shape, jnp.float32),
        in_specs=[pl.BlockSpec(memory_space=pltpu.SMEM), ANY, *[ANY] * (2 * pieces), ANY],
        out_specs=ANY,
        scratch_shapes=[
            pltpu.VMEM(held.shape, jnp.bfloat16),
            pltpu.VMEM((2, steps, *own[0].shape), jnp.bfloat16),
            pltpu.VMEM((steps, rows, columns), jnp.float32),
            pltpu.VMEM((steps, rows, columns), jnp.float32),
            pltpu.VMEM((2, rows, LANES), jnp.float32),
            pltpu.SemaphoreType.DMA,
            pltpu.SemaphoreType.DMA((2, pieces)),
            pltpu.SemaphoreType.DMA((steps,)),
            pltpu.SemaphoreType.DMA((steps,)),
        ],
        compiler_params=pltpu.CompilerParams(vmem_limit_bytes=52 * MIB),
        cost_estimate=pl.CostEstimate(
            flops=2 * rows * width * width, bytes_accessed=2 * width * width + 10 * rows * width, transcendentals=0
        ),
        name="model_rows",
    )(place, held, *own, *other, momentum)


def swap(value, axis):
    return lax.ppermute(value, axis, [(0, 1), (1, 0)])


def along_z(value, step):
    n = SIZES[0]
    return lax.ppermute(value, "z", [(i, (i + step) % n) for i in range(n)])


def exchange(value):
    return lax.all_to_all(value, EXP, split_axis=0, concat_axis=0, tiled=True)


def per_device(grad_block, momentum, model_root, expert_root):
    experts, hidden, width = grad_block.shape
    rows = experts * hidden
    half = width // 2
    z, yh, core = (lax.axis_index(axis) for axis in ("z", "yh", "core"))

    mine = lax.dynamic_slice_in_dim(model_root, core * half, half, axis=1)
    theirs = swap(mine, "yh")
    sent = sliced(grad_block.reshape(rows, width), experts, hidden)
    mine, theirs, sent = lax.optimization_barrier((mine, theirs, sent))

    held = exchange(sent)
    here = jnp.stack([mine, theirs])
    up1, down1 = along_z(here, 1), along_z(here, -1)
    up2, down2 = along_z(up1, 1), along_z(down1, -1)
    near = (here, down1, up1)
    others = tuple(swap(piece, "core") for piece in near)
    held, up2, down2, others = lax.optimization_barrier((held, up2, down2, others))

    blended = mixed_experts(expert_root, held.reshape(PARTS, hidden, experts, LANES))
    blended, up2, down2 = lax.optimization_barrier((blended, up2, down2))

    back = exchange(blended.reshape(PARTS, rows, LANES))
    up3, down3 = along_z(up2, 1), along_z(down2, -1)
    late = (down2, up2, down3, up3, along_z(up2[0], 2), along_z(down2[1], -2))
    own = near + late
    other = others + tuple(swap(piece, "core") for piece in late)

    order = [lax.rem(z + SIZES[0] + offset, SIZES[0]) for offset in OFFSETS]
    place = jnp.stack([yh, core, *order]).astype(jnp.int32)
    out = finished(place, back, own, other, momentum.reshape(rows, width), experts, hidden)
    return out.reshape(experts, hidden, width)


def solution(mesh):
    fine = Mesh(mesh.devices.reshape(SIZES), NAMES)
    placed = (P(EXP, BLK, None), P(EXP, BLK, None), P(BLK, None), P())
    return jax.shard_map(
        per_device, mesh=fine, in_specs=placed, out_specs=P(EXP, BLK, None), check_vma=False
    )
```

time: 292 us -> 113 us (0.39)
  waiting for transfers between devices: 143 us -> 45.3 us
  blocking collectives: 63.6 us -> 0 us
  local copies, waits for them, and re-layouts: 55.6 us -> 4.83 us
  starting transfers between devices: 0.01 us -> 37 us
  Pallas kernels: 0 us -> 24.3 us
  matrix products: 13.4 us -> 0 us
  between operations: 13.4 us -> 0.3 us
    all_gather x1 -> x0, waiting for transfers between devices: 142 us -> none  [per_device(): lax.all_gather(model_root, 'blk', axis=0, tiled=True)]
    all_to_all x2 -> x0, blocking collectives: 63.6 us -> none  [the longest x1 32 us: per_device(): lax.all_to_all(model_mode, 'exp', split_axis=2, concat_axis=0, tiled=True)]
    ppermute x0 -> x18, waiting for transfers between devices: none -> 45.3 us  [the longest x8 42.2 us: along_z(): return lax.ppermute(value, 'z', [(i, (i + step) % n) for i in range(n)])]
    pallas_call x0 -> x3, Pallas kernels: none -> 24.3 us  [the longest x1 16.9 us: finished(): pl.pallas_call(lambda *refs: finish_kernel(experts, hidden, pieces, *refs...]
    unnamed x8 -> x20, local copies, waits for them, and re-layouts: 27.4 us -> 3.71 us
    ppermute x0 -> x18, starting transfers between devices: none -> 23.1 us  [the longest x8 14.5 us: along_z(): return lax.ppermute(value, 'z', [(i, (i + step) % n) for i in range(n)])]
    reshape x2 -> x0, local copies, waits for them, and re-layouts: 17.3 us -> none  [the longest x1 12.9 us: per_device(): products.astype(jnp.bfloat16).reshape(local_experts, local_hidden, width)]
    all_to_all x0 -> x2, starting transfers between devices: none -> 14 us  [exchange(): return lax.all_to_all(value, EXP, split_axis=0, concat_axis=0, tiled=True)]
  transfers between devices with their start and end apart: 1 -> 20, of which waited for: 1 -> 7; matrix products, arithmetic and copies ran while one was open for 0% -> 2% of each run, Pallas kernels for 0% -> 5%
where the time goes in v2:
time: 113 us
  waiting for transfers between devices  45.3 us (40%)
  starting transfers between devices  37 us (33%)
  Pallas kernels  24.3 us (22%)
  local copies, waits for them, and re-layouts  4.83 us (4%)
    ppermute x8, waiting for transfers between devices, along_z(): return lax.ppermute(value, 'z', [(i, (i + step) % n) for i in range(n)])  42.2 us
    pallas_call x1, Pallas kernels, finished(): pl.pallas_call(lambda *refs: finish_kernel(experts, hidden, pieces, *refs...  16.9 us
    ppermute x8, starting transfers between devices, along_z(): return lax.ppermute(value, 'z', [(i, (i + step) % n) for i in range(n)])  14.5 us
    all_to_all x2, starting transfers between devices, exchange(): return lax.all_to_all(value, EXP, split_axis=0, concat_axis=0, tiled=True)  14 us
    ppermute x10, starting transfers between devices, swap(): return lax.ppermute(value, axis, [(0, 1), (1, 0)])  8.55 us
    pallas_call x1, Pallas kernels, sliced(): pl.pallas_call(lambda *refs: slice_kernel(experts, hidden, *refs), out_sh...  5.17 us
    unnamed x20, local copies, waits for them, and re-layouts  3.71 us
    ppermute x10, waiting for transfers between devices, swap(): return lax.ppermute(value, axis, [(0, 1), (1, 0)])  3.06 us
  transfers between devices with their start and end apart: 20, of which 7 were waited for; matrix products, arithmetic and copies ran while one was open for 2% of the time, Pallas kernels for 5%

profile of v2, /device:TPU:1, one launch (start us, length us, event | category | flops | bytes accessed | tf_op | source)
XLA Modules:
  0.0 112.8 jit_solution(363136814721858036)
XLA Ops:
  0.0 0.0 copy-start
  0.0 1.0 copy-done
  1.1 3.8 %collective-permute-start = (bf16[128,1024]{1,0:T(8,128)(2,1)S(1)}, bf16[128,1024]{1,0:T(8,128)(2,1)S(1)}, u32[]{:S(2)}, u32[]{:S(2)}) collective-permute-start(bf16[128,1024]{1,0:T(8,128)(2,1)S(1)} %constant_dynamic-slice_fusion), channel_id=1, source_target_pairs={{0,16},{16,0},{1,17},{17,1},{2,18},{18,2},{3,19},{19,3},{4,20},{20... | collective-permute-start | bytes 786440 | tf_op jit(solution)/shard_map/ppermute | solution.py:201
  4.9 5.2 %slice_columns.1 = bf16[16,512,128]{2,1,0:T(8,128)(2,1)} custom-call(bf16[512,2048]{1,0:T(8,128)(2,1)} %bitcast.23), custom_call_target="tpu_custom_call" | custom-call | flops 1073741824 | bytes 4194304 | tf_op jit(solution)/shard_map/slice_columns/pallas_call | solution.py:54
  10.1 0.0 collective-permute-done
  10.1 0.0 copy-start.9
  10.1 7.4 %all-to-all-start = ((bf16[16,512,128]{2,1,0:T(8,128)(2,1)}), bf16[16,512,128]{2,1,0:T(8,128)(2,1)S(1)}, u32[]{:S(2)}, u32[]{:S(2)}) async-start(bf16[16,512,128]{2,1,0:T(8,128)(2,1)} %slice_columns.1), calls=%async_computation | async-start | bytes 4194304 | tf_op jit(solution)/shard_map/all_to_all | solution.py:210
  17.5 0.0 copy-done.9
  17.5 1.0 pad_maximum_fusion.refs_2_
  18.5 5.7 %collective-permute-start.3 = (bf16[2,128,1024]{2,1,0:T(8,128)(2,1)S(1)}, bf16[2,128,1024]{2,1,0:T(8,128)(2,1)S(1)}, u32[]{:S(2)}, u32[]{:S(2)}) collective-permute-start(bf16[2,128,1024]{2,1,0:T(8,128)(2,1)S(1)} %pad_maximum_fusion.refs_2_), channel_id=1, source_target_pairs={{0,224},{32,0},{64,32},{96,64},{128,96},{160,128},{192,160},{224,1... | collective-permute-start | bytes 1572872 | tf_op jit(solution)/shard_map/ppermute | solution.py:206
  24.2 0.0 collective-permute-start.1
  24.2 0.4 collective-permute-start.5
  24.6 10.9 %collective-permute-done.3.refs_3_ = bf16[2,128,1024]{2,1,0:T(8,128)(2,1)S(1)} collective-permute-done((bf16[2,128,1024]{2,1,0:T(8,128)(2,1)S(1)}, bf16[2,128,1024]{2,1,0:T(8,128)(2,1)S(1)}, u32[]{:S(2)}, u32[]{:S(2)}) %collective-permute-start.3) | collective-permute-done | bytes 524320 | tf_op jit(solution)/shard_map/ppermute | solution.py:206
  35.5 0.0 copy-start.4
  35.5 0.9 collective-permute-start.6
  36.4 3.4 %collective-permute-start.4 = (bf16[2,128,1024]{2,1,0:T(8,128)(2,1)S(1)}, bf16[2,128,1024]{2,1,0:T(8,128)(2,1)S(1)}, u32[]{:S(2)}, u32[]{:S(2)}) collective-permute-start(bf16[2,128,1024]{2,1,0:T(8,128)(2,1)S(1)} %collective-permute-done.3.refs_3_), channel_id=1, source_target_pairs={{0,224},{32,0},{64,32},{96,64},{128,96},{160,128},{192,160},{224,1... | collective-permute-start | bytes 1572872 | tf_op jit(solution)/shard_map/ppermute | solution.py:206
  39.8 0.0 collective-permute-done.1.refs_4_
  39.8 0.0 copy-start.5
  39.8 0.3 collective-permute-start.7
  40.1 0.0 collective-permute-start.2
  40.1 0.0 collective-permute-done.5.refs_11_
  40.1 0.0 copy-start.6
  40.1 0.0 collective-permute-done.6.refs_12_
  40.1 0.0 copy-start.7
  40.1 11.0 %collective-permute-done.4.refs_5_ = bf16[2,128,1024]{2,1,0:T(8,128)(2,1)S(1)} collective-permute-done((bf16[2,128,1024]{2,1,0:T(8,128)(2,1)S(1)}, bf16[2,128,1024]{2,1,0:T(8,128)(2,1)S(1)}, u32[]{:S(2)}, u32[]{:S(2)}) %collective-permute-start.4) | collective-permute-done | bytes 524320 | tf_op jit(solution)/shard_map/ppermute | solution.py:206
  51.1 0.0 copy-start.2
  51.1 0.0 collective-permute-done.7.refs_13_
  51.1 0.0 copy-done.4
  51.1 0.0 copy-done.5
  51.1 0.0 copy-done.6
  51.2 0.0 copy-done.7
  51.2 0.8 copy-done.2
  51.9 0.8 copy-done.8
  52.8 1.9 %collective-permute-done.2.refs_6_ = bf16[2,128,1024]{2,1,0:T(8,128)(2,1)} collective-permute-done((bf16[2,128,1024]{2,1,0:T(8,128)(2,1)S(1)}, bf16[2,128,1024]{2,1,0:T(8,128)(2,1)}, u32[]{:S(2)}, u32[]{:S(2)}) %collective-permute-start.2) | collective-permute-done | bytes 524320 | tf_op jit(solution)/shard_map/ppermute | solution.py:206
  54.7 0.0 all-to-all-done
  54.7 1.0 copy-done.1
  55.7 2.2 %mix_experts.1 = bf16[16,16,32,128]{3,2,1,0:T(8,128)(2,1)} custom-call(bf16[512,512]{1,0:T(8,128)(2,1)S(1)} %copy-done.1, bf16[16,16,32,128]{3,2,1,0:T(8,128)(2,1)S(1)} %bitcast.21), custom_call_target="tpu_custom_call" | custom-call | flops 1073741824 | bytes 4194304 | tf_op jit(solution)/shard_map/mix_experts/pallas_call | solution.py:98
  58.0 0.0 copy-start.3
  58.0 6.5 %all-to-all-start.1 = ((bf16[16,512,128]{2,1,0:T(8,128)(2,1)}), bf16[16,512,128]{2,1,0:T(8,128)(2,1)}, u32[]{:S(2)}, u32[]{:S(2)}) async-start(bf16[16,512,128]{2,1,0:T(8,128)(2,1)} %bitcast.14), calls=%async_computation.1 | async-start | bytes 4194304 | tf_op jit(solution)/shard_map/all_to_all | solution.py:210
  64.5 0.0 copy-done.3
  64.5 1.3 %collective-permute-start.8 = (bf16[2,128,1024]{2,1,0:T(8,128)(2,1)S(1)}, bf16[2,128,1024]{2,1,0:T(8,128)(2,1)}, u32[]{:S(2)}, u32[]{:S(2)}) collective-permute-start(bf16[2,128,1024]{2,1,0:T(8,128)(2,1)S(1)} %copy-done.3), channel_id=1, source_target_pairs={{0,224},{32,0},{64,32},{96,64},{128,96},{160,128},{192,160},{224,1... | collective-permute-start | bytes 1572872 | tf_op jit(solution)/shard_map/ppermute | solution.py:206
  65.8 0.2 collective-permute-start.9
  66.0 1.0 slice_bitcast_fusion.1
  67.1 0.1 collective-permute-start.10
  67.2 3.8 %collective-permute-start.11 = (bf16[128,1024]{1,0:T(8,128)(2,1)S(1)}, bf16[128,1024]{1,0:T(8,128)(2,1)S(1)}, u32[]{:S(2)}, u32[]{:S(2)}) collective-permute-start(bf16[128,1024]{1,0:T(8,128)(2,1)S(1)} %slice_bitcast_fusion), channel_id=1, source_target_pairs={{0,192},{32,224},{64,0},{96,32},{128,64},{160,96},{192,128},{224,1... | collective-permute-start | bytes 786440 | tf_op jit(solution)/shard_map/ppermute | solution.py:206
  71.0 1.3 %collective-permute-start.12 = (bf16[2,128,1024]{2,1,0:T(8,128)(2,1)S(1)}, bf16[2,128,1024]{2,1,0:T(8,128)(2,1)}, u32[]{:S(2)}, u32[]{:S(2)}) collective-permute-start(bf16[2,128,1024]{2,1,0:T(8,128)(2,1)S(1)} %copy-done.3), channel_id=1, source_target_pairs={{0,1},{1,0},{2,3},{3,2},{4,5},{5,4},{6,7},{7,6},{8,9},{9,8},{10,11... | collective-permute-start | bytes 1572872 | tf_op jit(solution)/shard_map/ppermute | solution.py:201
  72.3 18.3 %collective-permute-done.10.refs_9_ = bf16[128,1024]{1,0:T(8,128)(2,1)S(1)} collective-permute-done((bf16[128,1024]{1,0:T(8,128)(2,1)S(1)}, bf16[128,1024]{1,0:T(8,128)(2,1)S(1)}, u32[]{:S(2)}, u32[]{:S(2)}) %collective-permute-start.10) | collective-permute-done | bytes 262176 | tf_op jit(solution)/shard_map/ppermute | solution.py:206
  90.6 1.0 collective-permute-start.16
  91.6 0.0 collective-permute-done.11.refs_10_
  91.6 0.0 collective-permute-start.13
  91.6 0.0 collective-permute-done.8.refs_7_
  91.6 0.5 collective-permute-start.14
  92.1 0.0 collective-permute-done.9.refs_8_
  92.1 0.1 collective-permute-start.15
  92.2 0.8 collective-permute-done.16.refs_18_
  93.0 0.4 collective-permute-start.17
  93.4 0.1 stack.52.refs_0_
  93.5 1.5 %collective-permute-done.17.refs_19_ = bf16[128,1024]{1,0:T(8,128)(2,1)S(1)} collective-permute-done((bf16[128,1024]{1,0:T(8,128)(2,1)S(1)}, bf16[128,1024]{1,0:T(8,128)(2,1)S(1)}, u32[]{:S(2)}, u32[]{:S(2)}) %collective-permute-start.17) | collective-permute-done | bytes 262176 | tf_op jit(solution)/shard_map/ppermute | solution.py:201
  95.0 0.0 collective-permute-done.12.refs_14_
  95.0 0.0 collective-permute-done.13.refs_15_
  95.0 0.0 collective-permute-done.14.refs_16_
  95.0 0.7 collective-permute-done.15.refs_17_
  95.7 0.0 all-to-all-done.1.refs_1_
  95.7 16.9 %model_rows.1 = f32[512,2048]{1,0:T(8,128)} custom-call(s32[10]{0:T(128)S(1)} %stack.52.refs_0_, bf16[16,512,128]{2,1,0:T(8,128)(2,1)} %all-to-all-done.1.refs_1_, bf16[2,128,1024]{2,1,0:T(8,128)(2,1)S(1)} %pad_maximum_fusion.refs_2_, bf16[2,128,1024]{2,1,0:T(8,128)(2,1)} %copy-done.4, bf16[2,128,1024]{2,1,0:T(8,128)(2,1)} %copy-done.5, ...), custom_call_target="tpu_custom_call" | custom-call | flops 4294967296 | bytes 18874368 | tf_op jit(solution)/shard_map/model_rows/pallas_call | solution.py:176
  (4 shorter events, 0.0 us)
Async XLA Ops:
  0.0 1.0 copy-start
  1.1 9.0 %collective-permute-start = (bf16[128,1024]{1,0:T(8,128)(2,1)S(1)}, bf16[128,1024]{1,0:T(8,128)(2,1)S(1)}, u32[]{:S(2)}, u32[]{:S(2)}) collective-permute-start(bf16[128,1024]{1,0:T(8,128)(2,1)S(1)} %constant_dynamic-slice_fusion), channel_id=1, source_target_pairs={{0,16},{16,0},{1,17},{17,1},{2,18},{18,2},{3,19},{19,3},{4,20},{20... | collective-permute-start | bytes 786440 | tf_op jit(solution)/shard_map/ppermute | solution.py:201
  10.1 7.5 %copy-start.9 = (bf16[128,1024]{1,0:T(8,128)(2,1)}, bf16[128,1024]{1,0:T(8,128)(2,1)S(1)}, u32[]{:S(2)}) copy-start(bf16[128,1024]{1,0:T(8,128)(2,1)S(1)} %collective-permute-done) | copy-start | bytes 786436
  10.1 44.6 %all-to-all-start = ((bf16[16,512,128]{2,1,0:T(8,128)(2,1)}), bf16[16,512,128]{2,1,0:T(8,128)(2,1)S(1)}, u32[]{:S(2)}, u32[]{:S(2)}) async-start(bf16[16,512,128]{2,1,0:T(8,128)(2,1)} %slice_columns.1), calls=%async_computation | async-start | bytes 4194304 | tf_op jit(solution)/shard_map/all_to_all | solution.py:210
  18.5 16.9 %collective-permute-start.3 = (bf16[2,128,1024]{2,1,0:T(8,128)(2,1)S(1)}, bf16[2,128,1024]{2,1,0:T(8,128)(2,1)S(1)}, u32[]{:S(2)}, u32[]{:S(2)}) collective-permute-start(bf16[2,128,1024]{2,1,0:T(8,128)(2,1)S(1)} %pad_maximum_fusion.refs_2_), channel_id=1, source_target_pairs={{0,224},{32,0},{64,32},{96,64},{128,96},{160,128},{192,160},{224,1... | collective-permute-start | bytes 1572872 | tf_op jit(solution)/shard_map/ppermute | solution.py:206
  24.2 15.6 %collective-permute-start.1 = (bf16[2,128,1024]{2,1,0:T(8,128)(2,1)S(1)}, bf16[2,128,1024]{2,1,0:T(8,128)(2,1)S(1)}, u32[]{:S(2)}, u32[]{:S(2)}) collective-permute-start(bf16[2,128,1024]{2,1,0:T(8,128)(2,1)S(1)} %pad_maximum_fusion.refs_2_), channel_id=1, source_target_pairs={{0,32},{32,64},{64,96},{96,128},{128,160},{160,192},{192,224},{224... | collective-permute-start | bytes 1572872 | tf_op jit(solution)/shard_map/ppermute | solution.py:206
  24.2 15.8 %collective-permute-start.5 = (bf16[2,128,1024]{2,1,0:T(8,128)(2,1)S(1)}, bf16[2,128,1024]{2,1,0:T(8,128)(2,1)S(1)}, u32[]{:S(2)}, u32[]{:S(2)}) collective-permute-start(bf16[2,128,1024]{2,1,0:T(8,128)(2,1)S(1)} %pad_maximum_fusion.refs_2_), channel_id=1, source_target_pairs={{0,1},{1,0},{2,3},{3,2},{4,5},{5,4},{6,7},{7,6},{8,9},{9,8},{10,11... | collective-permute-start | bytes 1572872 | tf_op jit(solution)/shard_map/ppermute | solution.py:201
  35.5 15.6 %copy-start.4 = (bf16[2,128,1024]{2,1,0:T(8,128)(2,1)}, bf16[2,128,1024]{2,1,0:T(8,128)(2,1)S(1)}, u32[]{:S(2)}) copy-start(bf16[2,128,1024]{2,1,0:T(8,128)(2,1)S(1)} %collective-permute-done.3.refs_3_) | copy-start | bytes 1572868
  35.5 4.6 %collective-permute-start.6 = (bf16[2,128,1024]{2,1,0:T(8,128)(2,1)S(1)}, bf16[2,128,1024]{2,1,0:T(8,128)(2,1)S(1)}, u32[]{:S(2)}, u32[]{:S(2)}) collective-permute-start(bf16[2,128,1024]{2,1,0:T(8,128)(2,1)S(1)} %collective-permute-done.3.refs_3_), channel_id=1, source_target_pairs={{0,1},{1,0},{2,3},{3,2},{4,5},{5,4},{6,7},{7,6},{8,9},{9,8},{10,11... | collective-permute-start | bytes 1572872 | tf_op jit(solution)/shard_map/ppermute | solution.py:201
  36.4 14.8 %collective-permute-start.4 = (bf16[2,128,1024]{2,1,0:T(8,128)(2,1)S(1)}, bf16[2,128,1024]{2,1,0:T(8,128)(2,1)S(1)}, u32[]{:S(2)}, u32[]{:S(2)}) collective-permute-start(bf16[2,128,1024]{2,1,0:T(8,128)(2,1)S(1)} %collective-permute-done.3.refs_3_), channel_id=1, source_target_pairs={{0,224},{32,0},{64,32},{96,64},{128,96},{160,128},{192,160},{224,1... | collective-permute-start | bytes 1572872 | tf_op jit(solution)/shard_map/ppermute | solution.py:206
  39.8 11.4 %copy-start.5 = (bf16[2,128,1024]{2,1,0:T(8,128)(2,1)}, bf16[2,128,1024]{2,1,0:T(8,128)(2,1)S(1)}, u32[]{:S(2)}) copy-start(bf16[2,128,1024]{2,1,0:T(8,128)(2,1)S(1)} %collective-permute-done.1.refs_4_) | copy-start | bytes 1572868
  39.8 11.4 %collective-permute-start.7 = (bf16[2,128,1024]{2,1,0:T(8,128)(2,1)S(1)}, bf16[2,128,1024]{2,1,0:T(8,128)(2,1)S(1)}, u32[]{:S(2)}, u32[]{:S(2)}) collective-permute-start(bf16[2,128,1024]{2,1,0:T(8,128)(2,1)S(1)} %collective-permute-done.1.refs_4_), channel_id=1, source_target_pairs={{0,1},{1,0},{2,3},{3,2},{4,5},{5,4},{6,7},{7,6},{8,9},{9,8},{10,11... | collective-permute-start | bytes 1572872 | tf_op jit(solution)/shard_map/ppermute | solution.py:201
  40.1 14.6 %collective-permute-start.2 = (bf16[2,128,1024]{2,1,0:T(8,128)(2,1)S(1)}, bf16[2,128,1024]{2,1,0:T(8,128)(2,1)}, u32[]{:S(2)}, u32[]{:S(2)}) collective-permute-start(bf16[2,128,1024]{2,1,0:T(8,128)(2,1)S(1)} %collective-permute-done.1.refs_4_), channel_id=1, source_target_pairs={{0,32},{32,64},{64,96},{96,128},{128,160},{160,192},{192,224},{224... | collective-permute-start | bytes 1572872 | tf_op jit(solution)/shard_map/ppermute | solution.py:206
  40.1 11.1 %copy-start.6 = (bf16[2,128,1024]{2,1,0:T(8,128)(2,1)}, bf16[2,128,1024]{2,1,0:T(8,128)(2,1)S(1)}, u32[]{:S(2)}) copy-start(bf16[2,128,1024]{2,1,0:T(8,128)(2,1)S(1)} %collective-permute-done.5.refs_11_) | copy-start | bytes 1572868
  40.1 11.1 %copy-start.7 = (bf16[2,128,1024]{2,1,0:T(8,128)(2,1)}, bf16[2,128,1024]{2,1,0:T(8,128)(2,1)S(1)}, u32[]{:S(2)}) copy-start(bf16[2,128,1024]{2,1,0:T(8,128)(2,1)S(1)} %collective-permute-done.6.refs_12_) | copy-start | bytes 1572868
  51.1 0.8 copy-start.2
  51.9 0.8 copy-start.8
  54.7 1.0 copy-start.1
  58.0 6.5 %copy-start.3 = (bf16[2,128,1024]{2,1,0:T(8,128)(2,1)S(1)}, bf16[2,128,1024]{2,1,0:T(8,128)(2,1)}, u32[]{:S(2)}) copy-start(bf16[2,128,1024]{2,1,0:T(8,128)(2,1)} %copy-done.2) | copy-start | bytes 1572868
  58.0 37.7 %all-to-all-start.1 = ((bf16[16,512,128]{2,1,0:T(8,128)(2,1)}), bf16[16,512,128]{2,1,0:T(8,128)(2,1)}, u32[]{:S(2)}, u32[]{:S(2)}) async-start(bf16[16,512,128]{2,1,0:T(8,128)(2,1)} %bitcast.14), calls=%async_computation.1 | async-start | bytes 4194304 | tf_op jit(solution)/shard_map/all_to_all | solution.py:210
  64.5 27.1 %collective-permute-start.8 = (bf16[2,128,1024]{2,1,0:T(8,128)(2,1)S(1)}, bf16[2,128,1024]{2,1,0:T(8,128)(2,1)}, u32[]{:S(2)}, u32[]{:S(2)}) collective-permute-start(bf16[2,128,1024]{2,1,0:T(8,128)(2,1)S(1)} %copy-done.3), channel_id=1, source_target_pairs={{0,224},{32,0},{64,32},{96,64},{128,96},{160,128},{192,160},{224,1... | collective-permute-start | bytes 1572872 | tf_op jit(solution)/shard_map/ppermute | solution.py:206
  65.8 26.3 %collective-permute-start.9 = (bf16[2,128,1024]{2,1,0:T(8,128)(2,1)}, bf16[2,128,1024]{2,1,0:T(8,128)(2,1)}, u32[]{:S(2)}, u32[]{:S(2)}) collective-permute-start(bf16[2,128,1024]{2,1,0:T(8,128)(2,1)} %collective-permute-done.2.refs_6_), channel_id=1, source_target_pairs={{0,32},{32,64},{64,96},{96,128},{128,160},{160,192},{192,224},{224... | collective-permute-start | bytes 1572872 | tf_op jit(solution)/shard_map/ppermute | solution.py:206
  67.1 23.6 %collective-permute-start.10 = (bf16[128,1024]{1,0:T(8,128)(2,1)S(1)}, bf16[128,1024]{1,0:T(8,128)(2,1)S(1)}, u32[]{:S(2)}, u32[]{:S(2)}) collective-permute-start(bf16[128,1024]{1,0:T(8,128)(2,1)S(1)} %slice_bitcast_fusion.1), channel_id=1, source_target_pairs={{0,64},{32,96},{64,128},{96,160},{128,192},{160,224},{192,0},{224,... | collective-permute-start | bytes 786440 | tf_op jit(solution)/shard_map/ppermute | solution.py:206
  67.2 24.4 %collective-permute-start.11 = (bf16[128,1024]{1,0:T(8,128)(2,1)S(1)}, bf16[128,1024]{1,0:T(8,128)(2,1)S(1)}, u32[]{:S(2)}, u32[]{:S(2)}) collective-permute-start(bf16[128,1024]{1,0:T(8,128)(2,1)S(1)} %slice_bitcast_fusion), channel_id=1, source_target_pairs={{0,192},{32,224},{64,0},{96,32},{128,64},{160,96},{192,128},{224,1... | collective-permute-start | bytes 786440 | tf_op jit(solution)/shard_map/ppermute | solution.py:206
  71.0 24.0 %collective-permute-start.12 = (bf16[2,128,1024]{2,1,0:T(8,128)(2,1)S(1)}, bf16[2,128,1024]{2,1,0:T(8,128)(2,1)}, u32[]{:S(2)}, u32[]{:S(2)}) collective-permute-start(bf16[2,128,1024]{2,1,0:T(8,128)(2,1)S(1)} %copy-done.3), channel_id=1, source_target_pairs={{0,1},{1,0},{2,3},{3,2},{4,5},{5,4},{6,7},{7,6},{8,9},{9,8},{10,11... | collective-permute-start | bytes 1572872 | tf_op jit(solution)/shard_map/ppermute | solution.py:201
  90.6 2.4 %collective-permute-start.16 = (bf16[128,1024]{1,0:T(8,128)(2,1)S(1)}, bf16[128,1024]{1,0:T(8,128)(2,1)S(1)}, u32[]{:S(2)}, u32[]{:S(2)}) collective-permute-start(bf16[128,1024]{1,0:T(8,128)(2,1)S(1)} %collective-permute-done.10.refs_9_), channel_id=1, source_target_pairs={{0,1},{1,0},{2,3},{3,2},{4,5},{5,4},{6,7},{7,6},{8,9},{9,8},{10,11... | collective-permute-start | bytes 786440 | tf_op jit(solution)/shard_map/ppermute | solution.py:201
  91.6 3.4 %collective-permute-start.13 = (bf16[2,128,1024]{2,1,0:T(8,128)(2,1)}, bf16[2,128,1024]{2,1,0:T(8,128)(2,1)}, u32[]{:S(2)}, u32[]{:S(2)}) collective-permute-start(bf16[2,128,1024]{2,1,0:T(8,128)(2,1)} %collective-permute-done.2.refs_6_), channel_id=1, source_target_pairs={{0,1},{1,0},{2,3},{3,2},{4,5},{5,4},{6,7},{7,6},{8,9},{9,8},{10,11... | collective-permute-start | bytes 1572872 | tf_op jit(solution)/shard_map/ppermute | solution.py:201
  91.6 3.4 %collective-permute-start.14 = (bf16[2,128,1024]{2,1,0:T(8,128)(2,1)}, bf16[2,128,1024]{2,1,0:T(8,128)(2,1)}, u32[]{:S(2)}, u32[]{:S(2)}) collective-permute-start(bf16[2,128,1024]{2,1,0:T(8,128)(2,1)} %collective-permute-done.8.refs_7_), channel_id=1, source_target_pairs={{0,1},{1,0},{2,3},{3,2},{4,5},{5,4},{6,7},{7,6},{8,9},{9,8},{10,11... | collective-permute-start | bytes 1572872 | tf_op jit(solution)/shard_map/ppermute | solution.py:201
  92.1 3.6 %collective-permute-start.15 = (bf16[2,128,1024]{2,1,0:T(8,128)(2,1)}, bf16[2,128,1024]{2,1,0:T(8,128)(2,1)}, u32[]{:S(2)}, u32[]{:S(2)}) collective-permute-start(bf16[2,128,1024]{2,1,0:T(8,128)(2,1)} %collective-permute-done.9.refs_8_), channel_id=1, source_target_pairs={{0,1},{1,0},{2,3},{3,2},{4,5},{5,4},{6,7},{7,6},{8,9},{9,8},{10,11... | collective-permute-start | bytes 1572872 | tf_op jit(solution)/shard_map/ppermute | solution.py:201
  93.0 2.0 %collective-permute-start.17 = (bf16[128,1024]{1,0:T(8,128)(2,1)S(1)}, bf16[128,1024]{1,0:T(8,128)(2,1)S(1)}, u32[]{:S(2)}, u32[]{:S(2)}) collective-permute-start(bf16[128,1024]{1,0:T(8,128)(2,1)S(1)} %collective-permute-done.11.refs_10_), channel_id=1, source_target_pairs={{0,1},{1,0},{2,3},{3,2},{4,5},{5,4},{6,7},{7,6},{8,9},{9,8},{10,11... | collective-permute-start | bytes 786440 | tf_op jit(solution)/shard_map/ppermute | solution.py:201

commit v3 on v2

v3 whole, which is shorter than its diff:
```python
import jax
import jax.numpy as jnp
from jax import lax
from jax.experimental import pallas as pl
from jax.experimental.pallas import tpu as pltpu
from jax.sharding import Mesh, PartitionSpec as P

NAMES = ("z", "yh", "x", "yl", "core")
SIZES = (8, 2, 4, 2, 2)
EXP = ("x", "yl", "core")
BLK = ("z", "yh")
PARTS = 16
GROUP = 4
LANES = 128
MIB = 1024 * 1024
OFFSETS = (0, 1, -1, 2, -2, 3, -3, 4)
VMEM = pl.BlockSpec(memory_space=pltpu.VMEM)
ANY = pl.BlockSpec(memory_space=pl.ANY)


def order_matrix(rows, outer, inner):
    row = lax.broadcasted_iota(jnp.int32, (rows, 1), 0)
    source = (row & (outer - 1)) * inner + lax.shift_right_logical(row, outer.bit_length() - 1)
    column = lax.broadcasted_iota(jnp.int32, (rows, rows), 1)
    return jnp.where(source == column, 1.0, 0.0).astype(jnp.bfloat16)


def slice_kernel(grad_ref, out_ref, parts, in_sems, out_sems):
    def arrival(part):
        return pltpu.make_async_copy(grad_ref.at[:, pl.ds(part * LANES, LANES)], parts.at[part], in_sems.at[part])

    def departure(part):
        return pltpu.make_async_copy(parts.at[part], out_ref.at[part], out_sems.at[part])

    for part in range(PARTS):
        arrival(part).start()
    for part in range(PARTS):
        arrival(part).wait()
        departure(part).start()
    for part in range(PARTS):
        departure(part).wait()


def sliced(grad):
    rows, width = grad.shape
    shape = (PARTS, rows, LANES)
    return pl.pallas_call(
        slice_kernel,
        out_shape=jax.ShapeDtypeStruct(shape, jnp.bfloat16),
        in_specs=[ANY],
        out_specs=ANY,
        scratch_shapes=[
            pltpu.VMEM(shape, jnp.bfloat16),
            pltpu.SemaphoreType.DMA((PARTS,)),
            pltpu.SemaphoreType.DMA((PARTS,)),
        ],
        compiler_params=pltpu.CompilerParams(vmem_limit_bytes=58 * MIB),
        cost_estimate=pl.CostEstimate(flops=0, bytes_accessed=4 * rows * width, transcendentals=0),
        name="slice_columns",
    )(grad)


def mix_kernel(experts, hidden, root_ref, in_ref, out_ref, root, turned, mixed, in_sem, out_sems):
    groups, rows, lanes = in_ref.shape

    def departure(h):
        there = (slice(None), pl.ds(h, GROUP))
        return pltpu.make_async_copy(mixed.at[there], out_ref.at[there], out_sems.at[h // GROUP])

    arrival = pltpu.make_async_copy(root_ref, root, in_sem)
    arrival.start()
    order = order_matrix(rows, experts, hidden)
    for group in range(0, groups, GROUP):
        some = jnp.concatenate([in_ref[group + k] for k in range(GROUP)], axis=1)
        moved = jnp.dot(order, some, preferred_element_type=jnp.float32).astype(jnp.bfloat16)
        for k in range(GROUP):
            at = slice((group + k) * experts, (group + k + 1) * experts)
            turned[:, at] = moved[:, k * lanes : (k + 1) * lanes].reshape(hidden, experts, lanes)
    arrival.wait()
    for h in range(0, hidden, GROUP):
        some = jnp.concatenate([turned[h + k] for k in range(GROUP)], axis=1)
        sums = jnp.dot(root[...], some, preferred_element_type=jnp.float32).astype(jnp.bfloat16)
        for k in range(GROUP):
            mixed[:, h + k] = sums[:, k * lanes : (k + 1) * lanes].reshape(groups, experts, lanes)
        departure(h).start()
    for h in range(0, hidden, GROUP):
        departure(h).wait()


def mixed_experts(expert_root, held, experts, hidden):
    groups, rows, lanes = held.shape
    total = groups * experts
    shape = (groups, hidden, experts, lanes)
    return pl.pallas_call(
        lambda *refs: mix_kernel(experts, hidden, *refs),
        out_shape=jax.ShapeDtypeStruct(shape, jnp.bfloat16),
        in_specs=[ANY, VMEM],
        out_specs=ANY,
        scratch_shapes=[
            pltpu.VMEM((total, total), jnp.bfloat16),
            pltpu.VMEM((hidden, total, lanes), jnp.bfloat16),
            pltpu.VMEM(shape, jnp.bfloat16),
            pltpu.SemaphoreType.DMA,
            pltpu.SemaphoreType.DMA((hidden // GROUP,)),
        ],
        compiler_params=pltpu.CompilerParams(vmem_limit_bytes=24 * MIB),
        cost_estimate=pl.CostEstimate(flops=0, bytes_accessed=0, transcendentals=0),
        name="mix_experts",
    )(expert_root, held)


def finish_kernel(experts, hidden, pieces, place_ref, held_ref, *refs):
    sources = refs[:pieces], refs[pieces : 2 * pieces]
    momentum_ref, out_ref, held, rows_of, roots, momentum, out = refs[2 * pieces : 2 * pieces + 7]
    held_sem, root_sems, momentum_sems, out_sems = refs[2 * pieces + 7 :]
    steps, rows, columns = out.shape
    per_half = PARTS // 2
    yh, core = place_ref[0], place_ref[1]

    def block(ref, step):
        return ref.at[:, pl.ds(pl.multiple_of(place_ref[2 + step] * columns, columns), columns)]

    def root_arrivals(side, step):
        pieces_of, sem = sources[side], root_sems.at[side]
        if step < steps - 1:
            return [pltpu.make_async_copy(pieces_of[step], roots.at[side, step], sem.at[step])]
        return [
            pltpu.make_async_copy(pieces_of[step + k], roots.at[side, step, k], sem.at[step + k]) for k in range(2)
        ]

    def momentum_arrival(step):
        return pltpu.make_async_copy(block(momentum_ref, step), momentum.at[step], momentum_sems.at[step])

    def departure(step):
        return pltpu.make_async_copy(out.at[step], block(out_ref, step), out_sems.at[step])

    held_arrival = pltpu.make_async_copy(held_ref, held, held_sem)
    held_arrival.start()
    for step in range(steps):
        for copy in (*root_arrivals(0, step), *root_arrivals(1, step), momentum_arrival(step)):
            copy.start()
    order = order_matrix(rows, hidden, experts)
    held_arrival.wait()
    for part in range(0, PARTS, GROUP):
        some = jnp.concatenate([held[part + k] for k in range(GROUP)], axis=1)
        moved = jnp.dot(order, some, preferred_element_type=jnp.float32).astype(jnp.bfloat16)
        at = (part % per_half) * LANES
        rows_of[part // per_half, :, at : at + GROUP * LANES] = moved
    for first in range(0, steps, 2):
        both = (first, first + 1)
        total = None
        for side, which in ((0, core), (1, 1 - core)):
            for step in both:
                for copy in root_arrivals(side, step):
                    copy.wait()
            root = jnp.concatenate([roots[side, step, k] for step in both for k in range(2)], axis=1)
            term = jnp.dot(rows_of[which], root, preferred_element_type=jnp.float32)
            total = term if total is None else total + term
        for step in both:
            momentum_arrival(step).wait()
            for k, block_at in ((0, yh), (1, 1 - yh)):
                lanes = pl.ds(pl.multiple_of(block_at * LANES, LANES), LANES)
                at = ((step - first) * 2 + k) * LANES
                out[step, :, lanes] = 0.9 * momentum[step, :, lanes] + total[:, at : at + LANES]
            departure(step).start()
    for step in range(steps):
        departure(step).wait()


def finished(place, held, own, other, momentum, experts, hidden):
    parts, rows, lanes = held.shape
    width = parts * lanes
    columns = 2 * LANES
    pieces, steps = len(own), len(OFFSETS)
    return pl.pallas_call(
        lambda *refs: finish_kernel(experts, hidden, pieces, *refs),
        out_shape=jax.ShapeDtypeStruct(momentum.shape, jnp.float32),
        in_specs=[pl.BlockSpec(memory_space=pltpu.SMEM), ANY, *[ANY] * (2 * pieces), ANY],
        out_specs=ANY,
        scratch_shapes=[
            pltpu.VMEM(held.shape, jnp.bfloat16),
            pltpu.VMEM((2, rows, width // 2), jnp.bfloat16),
            pltpu.VMEM((2, steps, *own[0].shape), jnp.bfloat16),
            pltpu.VMEM((steps, rows, columns), jnp.float32),
            pltpu.VMEM((steps, rows, columns), jnp.float32),
            pltpu.SemaphoreType.DMA,
            pltpu.SemaphoreType.DMA((2, pieces)),
            pltpu.SemaphoreType.DMA((steps,)),
            pltpu.SemaphoreType.DMA((steps,)),
        ],
        compiler_params=pltpu.CompilerParams(vmem_limit_bytes=52 * MIB),
        cost_estimate=pl.CostEstimate(
            flops=2 * rows * width * width, bytes_accessed=2 * width * width + 10 * rows * width, transcendentals=0
        ),
        name="model_rows",
    )(place, held, *own, *other, momentum)


def swap(value, axis):
    return lax.ppermute(value, axis, [(0, 1), (1, 0)])


def along_z(value, step):
    n = SIZES[0]
    return lax.ppermute(value, "z", [(i, (i + step) % n) for i in range(n)])


def exchange(value):
    return lax.all_to_all(value, EXP, split_axis=0, concat_axis=0, tiled=True)


def per_device(grad_block, momentum, model_root, expert_root):
    experts, hidden, width = grad_block.shape
    rows = experts * hidden
    half = width // 2
    z, yh, core = (lax.axis_index(axis) for axis in ("z", "yh", "core"))

    mine = lax.dynamic_slice_in_dim(model_root, core * half, half, axis=1).T
    theirs = swap(mine, "yh")
    here = jnp.stack([mine, theirs])
    sent = sliced(grad_block.reshape(rows, width))
    here, sent = lax.optimization_barrier((here, sent))

    held = exchange(sent)
    up1, down1 = along_z(here, 1), along_z(here, -1)
    first = (swap(here, "core"),)
    held, first, _, _ = lax.optimization_barrier((held, first, up1, down1))

    up2, down2 = along_z(up1, 1), along_z(down1, -1)
    blended = mixed_experts(expert_root, held, experts, hidden)
    second = (swap(down1, "core"), swap(up1, "core"))
    blended, up2, down2, second = lax.optimization_barrier((blended, up2, down2, second))

    back = exchange(blended.reshape(PARTS, rows, LANES))
    up3, down3 = along_z(up2, 1), along_z(down2, -1)
    own = (here, down1, up1, down2, up2, down3, up3, along_z(up3[0], 1), along_z(down3[1], -1))
    other = first + second + tuple(swap(piece, "core") for piece in own[3:])

    order = [lax.rem(z + SIZES[0] + offset, SIZES[0]) for offset in OFFSETS]
    place = jnp.stack([yh, core, *order]).astype(jnp.int32)
    out = finished(place, back, own, other, momentum.reshape(rows, width), experts, hidden)
    return out.reshape(experts, hidden, width)


def solution(mesh):
    fine = Mesh(mesh.devices.reshape(SIZES), NAMES)
    placed = (P(EXP, BLK, None), P(EXP, BLK, None), P(BLK, None), P())
    return jax.shard_map(
        per_device, mesh=fine, in_specs=placed, out_specs=P(EXP, BLK, None), check_vma=False
    )
```

time: 113 us -> 99.8 us (0.88)
  Pallas kernels: 24.3 us -> 16.8 us
  waiting for transfers between devices: 45.3 us -> 39.6 us
  starting transfers between devices: 37 us -> 38.2 us
    ppermute x8, waiting for transfers between devices: 42.2 us -> 30.8 us  [along_z(): return lax.ppermute(value, 'z', [(i, (i + step) % n) for i in range(n)])]
    pallas_call x1, Pallas kernels: 16.9 us -> 10.8 us  [finished(): pl.pallas_call(lambda *refs: finish_kernel(experts, hidden, pieces, *refs...]
    all_to_all x2, waiting for transfers between devices: 0.01 us -> 5.42 us  [exchange(): return lax.all_to_all(value, EXP, split_axis=0, concat_axis=0, tiled=True)]
    ppermute x10, starting transfers between devices: 8.55 us -> 11.7 us  [swap(): return lax.ppermute(value, axis, [(0, 1), (1, 0)])]
    ppermute x8, starting transfers between devices: 14.5 us -> 12.4 us  [along_z(): return lax.ppermute(value, 'z', [(i, (i + step) % n) for i in range(n)])]
    pallas_call x2, Pallas kernels: 7.4 us -> 5.98 us  [the longest x1 3.39 us: mixed_experts(): pl.pallas_call(lambda *refs: mix_kernel(experts, hidden, *refs), out_shap...]
    unnamed x20 -> x9, local copies, waits for them, and re-layouts: 3.71 us -> 2.96 us
  transfers between devices with their start and end apart: 20 -> 20, of which waited for: 7 -> 9; matrix products, arithmetic and copies ran while one was open for 2% -> 1% of each run, Pallas kernels for 5% -> 6%
where the time goes in v3:
time: 99.8 us; the launch traced here: 98.9 us
  waiting for transfers between devices  39.6 us (40%)
  starting transfers between devices  38.2 us (38%)
  Pallas kernels  16.8 us (17%)
  local copies, waits for them, and re-layouts  4.05 us (4%)
    ppermute x8, waiting for transfers between devices, along_z(): return lax.ppermute(value, 'z', [(i, (i + step) % n) for i in range(n)])  30.8 us
    all_to_all x2, starting transfers between devices, exchange(): return lax.all_to_all(value, EXP, split_axis=0, concat_axis=0, tiled=True)  14.1 us
    ppermute x8, starting transfers between devices, along_z(): return lax.ppermute(value, 'z', [(i, (i + step) % n) for i in range(n)])  12.4 us
    ppermute x10, starting transfers between devices, swap(): return lax.ppermute(value, axis, [(0, 1), (1, 0)])  11.7 us
    pallas_call x1, Pallas kernels, finished(): pl.pallas_call(lambda *refs: finish_kernel(experts, hidden, pieces, *refs...  10.8 us
    all_to_all x2, waiting for transfers between devices, exchange(): return lax.all_to_all(value, EXP, split_axis=0, concat_axis=0, tiled=True)  5.42 us
    ppermute x10, waiting for transfers between devices, swap(): return lax.ppermute(value, axis, [(0, 1), (1, 0)])  3.44 us
    pallas_call x1, Pallas kernels, mixed_experts(): pl.pallas_call(lambda *refs: mix_kernel(experts, hidden, *refs), out_shap...  3.39 us
  transfers between devices with their start and end apart: 20, of which 9 were waited for; matrix products, arithmetic and copies ran while one was open for 1% of the time, Pallas kernels for 6%

profile of v3, /device:TPU:1, one launch (start us, length us, event | category | flops | bytes accessed | tf_op | source)
XLA Modules:
  0.0 98.9 jit_solution(9900155213330790028)
XLA Ops:
  0.0 0.0 copy-start
  0.0 1.0 %copy-done = bf16[128,2048]{1,0:T(8,128)(2,1)S(1)} copy-done((bf16[128,2048]{1,0:T(8,128)(2,1)S(1)}, bf16[128,2048]{1,0:T(8,128)(2,1)}, u32[]{:S(2)}) %copy-start) | copy-done | bytes 524312
  1.1 0.2 copy.6
  1.2 3.8 %collective-permute-start = (bf16[1024,128]{1,0:T(8,128)(2,1)S(1)}, bf16[1024,128]{1,0:T(8,128)(2,1)S(1)}, u32[]{:S(2)}, u32[]{:S(2)}) collective-permute-start(bf16[1024,128]{1,0:T(8,128)(2,1)S(1)} %bitcast.24), channel_id=1, source_target_pairs={{0,16},{16,0},{1,17},{17,1},{2,18},{18,2},{3,19},{19,3},{4,20},{20... | collective-permute-start | bytes 786440 | tf_op jit(solution)/shard_map/ppermute | solution.py:200
  5.1 2.6 %slice_columns.1 = bf16[16,512,128]{2,1,0:T(8,128)(2,1)} custom-call(bf16[512,2048]{1,0:T(8,128)(2,1)} %bitcast.23), custom_call_target="tpu_custom_call" | custom-call | bytes 4194304 | tf_op jit(solution)/shard_map/slice_columns/pallas_call | solution.py:47
  7.7 2.4 %collective-permute-done = bf16[1024,128]{1,0:T(8,128)(2,1)S(1)} collective-permute-done((bf16[1024,128]{1,0:T(8,128)(2,1)S(1)}, bf16[1024,128]{1,0:T(8,128)(2,1)S(1)}, u32[]{:S(2)}, u32[]{:S(2)}) %collective-permute-start) | collective-permute-done | bytes 262176 | tf_op jit(solution)/shard_map/ppermute | solution.py:200
  10.0 0.1 pad_maximum_fusion.refs_2_
  10.1 7.7 %all-to-all-start = ((bf16[16,512,128]{2,1,0:T(8,128)(2,1)}), bf16[16,512,128]{2,1,0:T(8,128)(2,1)S(1)}, u32[]{:S(2)}, u32[]{:S(2)}) async-start(bf16[16,512,128]{2,1,0:T(8,128)(2,1)} %slice_columns.1), calls=%async_computation | async-start | bytes 4194304 | tf_op jit(solution)/shard_map/all_to_all | solution.py:209
  17.8 5.6 %collective-permute-start.3 = (bf16[2,1024,128]{2,1,0:T(8,128)(2,1)S(1)}, bf16[2,1024,128]{2,1,0:T(8,128)(2,1)}, u32[]{:S(2)}, u32[]{:S(2)}) collective-permute-start(bf16[2,1024,128]{2,1,0:T(8,128)(2,1)S(1)} %pad_maximum_fusion.refs_2_), channel_id=1, source_target_pairs={{0,224},{32,0},{64,32},{96,64},{128,96},{160,128},{192,160},{224,1... | collective-permute-start | bytes 1572872 | tf_op jit(solution)/shard_map/ppermute | solution.py:205
  23.3 0.0 collective-permute-start.2
  23.4 0.5 collective-permute-start.1
  23.8 10.7 %collective-permute-done.3.refs_3_ = bf16[2,1024,128]{2,1,0:T(8,128)(2,1)} collective-permute-done((bf16[2,1024,128]{2,1,0:T(8,128)(2,1)S(1)}, bf16[2,1024,128]{2,1,0:T(8,128)(2,1)}, u32[]{:S(2)}, u32[]{:S(2)}) %collective-permute-start.3) | collective-permute-done | bytes 524320 | tf_op jit(solution)/shard_map/ppermute | solution.py:205
  34.5 1.0 collective-permute-start.6
  35.5 3.5 %collective-permute-start.5 = (bf16[2,1024,128]{2,1,0:T(8,128)(2,1)}, bf16[2,1024,128]{2,1,0:T(8,128)(2,1)}, u32[]{:S(2)}, u32[]{:S(2)}) collective-permute-start(bf16[2,1024,128]{2,1,0:T(8,128)(2,1)} %collective-permute-done.3.refs_3_), channel_id=1, source_target_pairs={{0,224},{32,0},{64,32},{96,64},{128,96},{160,128},{192,160},{224,1... | collective-permute-start | bytes 1572872 | tf_op jit(solution)/shard_map/ppermute | solution.py:205
  39.0 0.0 collective-permute-done.2.refs_4_
  39.0 0.3 collective-permute-start.7
  39.3 0.0 collective-permute-start.4
  39.3 0.0 collective-permute-done.1.refs_11_
  39.3 5.4 %all-to-all-done.refs_1_ = bf16[16,512,128]{2,1,0:T(8,128)(2,1)S(1)} async-done(((bf16[16,512,128]{2,1,0:T(8,128)(2,1)}), bf16[16,512,128]{2,1,0:T(8,128)(2,1)S(1)}, u32[]{:S(2)}, u32[]{:S(2)}) %all-to-all-start) | async-done | bytes 2097184 | tf_op jit(solution)/shard_map/all_to_all | solution.py:209
  44.7 0.0 copy-start.1
  44.7 1.0 %copy-done.1 = bf16[512,512]{1,0:T(8,128)(2,1)S(1)} copy-done((bf16[512,512]{1,0:T(8,128)(2,1)S(1)}, bf16[512,512]{1,0:T(8,128)(2,1)}, u32[]{:S(2)}) %copy-start.1) | copy-done | bytes 524312
  45.8 3.4 %mix_experts.1 = bf16[16,16,32,128]{3,2,1,0:T(8,128)(2,1)} custom-call(bf16[512,512]{1,0:T(8,128)(2,1)S(1)} %copy-done.1, bf16[16,512,128]{2,1,0:T(8,128)(2,1)S(1)} %all-to-all-done.refs_1_), custom_call_target="tpu_custom_call" | custom-call | tf_op jit(solution)/shard_map/mix_experts/pallas_call | solution.py:94
  49.2 0.0 collective-permute-done.6.refs_12_
  49.2 1.5 %collective-permute-done.5.refs_5_ = bf16[2,1024,128]{2,1,0:T(8,128)(2,1)} collective-permute-done((bf16[2,1024,128]{2,1,0:T(8,128)(2,1)}, bf16[2,1024,128]{2,1,0:T(8,128)(2,1)}, u32[]{:S(2)}, u32[]{:S(2)}) %collective-permute-start.5) | collective-permute-done | bytes 524320 | tf_op jit(solution)/shard_map/ppermute | solution.py:205
  50.7 0.0 collective-permute-done.7.refs_13_
  50.7 3.4 %collective-permute-done.4.refs_6_ = bf16[2,1024,128]{2,1,0:T(8,128)(2,1)} collective-permute-done((bf16[2,1024,128]{2,1,0:T(8,128)(2,1)}, bf16[2,1024,128]{2,1,0:T(8,128)(2,1)}, u32[]{:S(2)}, u32[]{:S(2)}) %collective-permute-start.4) | collective-permute-done | bytes 524320 | tf_op jit(solution)/shard_map/ppermute | solution.py:205
  54.1 6.4 %all-to-all-start.1 = ((bf16[16,512,128]{2,1,0:T(8,128)(2,1)}), bf16[16,512,128]{2,1,0:T(8,128)(2,1)}, u32[]{:S(2)}, u32[]{:S(2)}) async-start(bf16[16,512,128]{2,1,0:T(8,128)(2,1)} %bitcast.14), calls=%async_computation.1 | async-start | bytes 4194304 | tf_op jit(solution)/shard_map/all_to_all | solution.py:209
  60.5 0.2 collective-permute-start.8
  60.7 1.3 %collective-permute-start.9 = (bf16[2,1024,128]{2,1,0:T(8,128)(2,1)}, bf16[2,1024,128]{2,1,0:T(8,128)(2,1)}, u32[]{:S(2)}, u32[]{:S(2)}) collective-permute-start(bf16[2,1024,128]{2,1,0:T(8,128)(2,1)} %collective-permute-done.4.refs_6_), channel_id=1, source_target_pairs={{0,32},{32,64},{64,96},{96,128},{128,160},{160,192},{192,224},{224... | collective-permute-start | bytes 1572872 | tf_op jit(solution)/shard_map/ppermute | solution.py:205
  62.0 0.8 collective-permute-start.12
  62.8 0.0 collective-permute-start.13
  62.8 11.4 %collective-permute-done.8.refs_7_ = bf16[2,1024,128]{2,1,0:T(8,128)(2,1)S(1)} collective-permute-done((bf16[2,1024,128]{2,1,0:T(8,128)(2,1)}, bf16[2,1024,128]{2,1,0:T(8,128)(2,1)S(1)}, u32[]{:S(2)}, u32[]{:S(2)}) %collective-permute-start.8) | collective-permute-done | bytes 524320 | tf_op jit(solution)/shard_map/ppermute | solution.py:205
  74.1 0.0 copy-start.2
  74.2 1.5 %collective-permute-start.11 = (bf16[1024,128]{1,0:T(8,128)(2,1)S(1)}, bf16[1024,128]{1,0:T(8,128)(2,1)S(1)}, u32[]{:S(2)}, u32[]{:S(2)}) collective-permute-start(bf16[1024,128]{1,0:T(8,128)(2,1)S(1)} %slice_bitcast_fusion), channel_id=1, source_target_pairs={{0,224},{32,0},{64,32},{96,64},{128,96},{160,128},{192,160},{224,1... | collective-permute-start | bytes 786440 | tf_op jit(solution)/shard_map/ppermute | solution.py:205
  75.6 0.0 collective-permute-done.9.refs_8_
  75.6 1.0 slice_bitcast_fusion.1
  76.6 0.3 collective-permute-start.10
  76.9 1.5 %collective-permute-start.14 = (bf16[2,1024,128]{2,1,0:T(8,128)(2,1)S(1)}, bf16[2,1024,128]{2,1,0:T(8,128)(2,1)}, u32[]{:S(2)}, u32[]{:S(2)}) collective-permute-start(bf16[2,1024,128]{2,1,0:T(8,128)(2,1)S(1)} %collective-permute-done.8.refs_7_), channel_id=1, source_target_pairs={{0,1},{1,0},{2,3},{3,2},{4,5},{5,4},{6,7},{7,6},{8,9},{9,8},{10,11... | collective-permute-start | bytes 1572872 | tf_op jit(solution)/shard_map/ppermute | solution.py:200
  78.4 0.0 collective-permute-done.12.refs_14_
  78.4 0.0 copy-start.3
  78.4 0.1 collective-permute-start.15
  78.5 0.7 copy-done.3
  79.2 2.0 %collective-permute-done.11.refs_10_ = bf16[1024,128]{1,0:T(8,128)(2,1)S(1)} collective-permute-done((bf16[1024,128]{1,0:T(8,128)(2,1)S(1)}, bf16[1024,128]{1,0:T(8,128)(2,1)S(1)}, u32[]{:S(2)}, u32[]{:S(2)}) %collective-permute-start.11) | collective-permute-done | bytes 262176 | tf_op jit(solution)/shard_map/ppermute | solution.py:205
  81.2 1.7 %collective-permute-start.17 = (bf16[1024,128]{1,0:T(8,128)(2,1)S(1)}, bf16[1024,128]{1,0:T(8,128)(2,1)S(1)}, u32[]{:S(2)}, u32[]{:S(2)}) collective-permute-start(bf16[1024,128]{1,0:T(8,128)(2,1)S(1)} %collective-permute-done.11.refs_10_), channel_id=1, source_target_pairs={{0,1},{1,0},{2,3},{3,2},{4,5},{5,4},{6,7},{7,6},{8,9},{9,8},{10,11... | collective-permute-start | bytes 786440 | tf_op jit(solution)/shard_map/ppermute | solution.py:200
  83.0 1.8 %collective-permute-done.10.refs_9_ = bf16[1024,128]{1,0:T(8,128)(2,1)S(1)} collective-permute-done((bf16[1024,128]{1,0:T(8,128)(2,1)S(1)}, bf16[1024,128]{1,0:T(8,128)(2,1)S(1)}, u32[]{:S(2)}, u32[]{:S(2)}) %collective-permute-start.10) | collective-permute-done | bytes 262176 | tf_op jit(solution)/shard_map/ppermute | solution.py:205
  84.8 2.0 %collective-permute-start.16 = (bf16[1024,128]{1,0:T(8,128)(2,1)S(1)}, bf16[1024,128]{1,0:T(8,128)(2,1)S(1)}, u32[]{:S(2)}, u32[]{:S(2)}) collective-permute-start(bf16[1024,128]{1,0:T(8,128)(2,1)S(1)} %collective-permute-done.10.refs_9_), channel_id=1, source_target_pairs={{0,1},{1,0},{2,3},{3,2},{4,5},{5,4},{6,7},{7,6},{8,9},{9,8},{10,11... | collective-permute-start | bytes 786440 | tf_op jit(solution)/shard_map/ppermute | solution.py:200
  86.8 0.1 stack.52.refs_0_
  86.9 0.0 collective-permute-done.13.refs_15_
  86.9 0.0 collective-permute-done.17.refs_19_
  86.9 0.0 collective-permute-done.14.refs_16_
  86.9 1.1 %collective-permute-done.16.refs_18_ = bf16[1024,128]{1,0:T(8,128)(2,1)S(1)} collective-permute-done((bf16[1024,128]{1,0:T(8,128)(2,1)S(1)}, bf16[1024,128]{1,0:T(8,128)(2,1)S(1)}, u32[]{:S(2)}, u32[]{:S(2)}) %collective-permute-start.16) | collective-permute-done | bytes 262176 | tf_op jit(solution)/shard_map/ppermute | solution.py:200
  88.0 0.0 collective-permute-done.15.refs_17_
  88.0 0.0 all-to-all-done.1.refs_1_
  88.0 0.0 copy-done.2
  88.0 10.8 %model_rows.1 = f32[512,2048]{1,0:T(8,128)} custom-call(s32[10]{0:T(128)S(1)} %stack.52.refs_0_, bf16[16,512,128]{2,1,0:T(8,128)(2,1)} %all-to-all-done.1.refs_1_, bf16[2,1024,128]{2,1,0:T(8,128)(2,1)S(1)} %pad_maximum_fusion.refs_2_, bf16[2,1024,128]{2,1,0:T(8,128)(2,1)} %collective-permute-done.3.refs_3_, ...), custom_call_target="tpu_custom_call" | custom-call | flops 4294967296 | bytes 18874368 | tf_op jit(solution)/shard_map/model_rows/pallas_call | solution.py:175
  (2 shorter events, 0.0 us)
Async XLA Ops:
  0.0 1.0 %copy-start = (bf16[128,2048]{1,0:T(8,128)(2,1)S(1)}, bf16[128,2048]{1,0:T(8,128)(2,1)}, u32[]{:S(2)}) copy-start(bf16[128,2048]{1,0:T(8,128)(2,1)} %param.6) | copy-start | bytes 1572868
  1.2 8.8 %collective-permute-start = (bf16[1024,128]{1,0:T(8,128)(2,1)S(1)}, bf16[1024,128]{1,0:T(8,128)(2,1)S(1)}, u32[]{:S(2)}, u32[]{:S(2)}) collective-permute-start(bf16[1024,128]{1,0:T(8,128)(2,1)S(1)} %bitcast.24), channel_id=1, source_target_pairs={{0,16},{16,0},{1,17},{17,1},{2,18},{18,2},{3,19},{19,3},{4,20},{20... | collective-permute-start | bytes 786440 | tf_op jit(solution)/shard_map/ppermute | solution.py:200
  10.1 34.6 %all-to-all-start = ((bf16[16,512,128]{2,1,0:T(8,128)(2,1)}), bf16[16,512,128]{2,1,0:T(8,128)(2,1)S(1)}, u32[]{:S(2)}, u32[]{:S(2)}) async-start(bf16[16,512,128]{2,1,0:T(8,128)(2,1)} %slice_columns.1), calls=%async_computation | async-start | bytes 4194304 | tf_op jit(solution)/shard_map/all_to_all | solution.py:209
  17.8 16.7 %collective-permute-start.3 = (bf16[2,1024,128]{2,1,0:T(8,128)(2,1)S(1)}, bf16[2,1024,128]{2,1,0:T(8,128)(2,1)}, u32[]{:S(2)}, u32[]{:S(2)}) collective-permute-start(bf16[2,1024,128]{2,1,0:T(8,128)(2,1)S(1)} %pad_maximum_fusion.refs_2_), channel_id=1, source_target_pairs={{0,224},{32,0},{64,32},{96,64},{128,96},{160,128},{192,160},{224,1... | collective-permute-start | bytes 1572872 | tf_op jit(solution)/shard_map/ppermute | solution.py:205
  23.3 15.7 %collective-permute-start.2 = (bf16[2,1024,128]{2,1,0:T(8,128)(2,1)S(1)}, bf16[2,1024,128]{2,1,0:T(8,128)(2,1)}, u32[]{:S(2)}, u32[]{:S(2)}) collective-permute-start(bf16[2,1024,128]{2,1,0:T(8,128)(2,1)S(1)} %pad_maximum_fusion.refs_2_), channel_id=1, source_target_pairs={{0,32},{32,64},{64,96},{96,128},{128,160},{160,192},{192,224},{224... | collective-permute-start | bytes 1572872 | tf_op jit(solution)/shard_map/ppermute | solution.py:205
  23.4 15.9 %collective-permute-start.1 = (bf16[2,1024,128]{2,1,0:T(8,128)(2,1)S(1)}, bf16[2,1024,128]{2,1,0:T(8,128)(2,1)}, u32[]{:S(2)}, u32[]{:S(2)}) collective-permute-start(bf16[2,1024,128]{2,1,0:T(8,128)(2,1)S(1)} %pad_maximum_fusion.refs_2_), channel_id=1, source_target_pairs={{0,1},{1,0},{2,3},{3,2},{4,5},{5,4},{6,7},{7,6},{8,9},{9,8},{10,11... | collective-permute-start | bytes 1572872 | tf_op jit(solution)/shard_map/ppermute | solution.py:200
  34.5 14.6 %collective-permute-start.6 = (bf16[2,1024,128]{2,1,0:T(8,128)(2,1)}, bf16[2,1024,128]{2,1,0:T(8,128)(2,1)}, u32[]{:S(2)}, u32[]{:S(2)}) collective-permute-start(bf16[2,1024,128]{2,1,0:T(8,128)(2,1)} %collective-permute-done.3.refs_3_), channel_id=1, source_target_pairs={{0,1},{1,0},{2,3},{3,2},{4,5},{5,4},{6,7},{7,6},{8,9},{9,8},{10,11... | collective-permute-start | bytes 1572872 | tf_op jit(solution)/shard_map/ppermute | solution.py:200
  35.5 15.2 %collective-permute-start.5 = (bf16[2,1024,128]{2,1,0:T(8,128)(2,1)}, bf16[2,1024,128]{2,1,0:T(8,128)(2,1)}, u32[]{:S(2)}, u32[]{:S(2)}) collective-permute-start(bf16[2,1024,128]{2,1,0:T(8,128)(2,1)} %collective-permute-done.3.refs_3_), channel_id=1, source_target_pairs={{0,224},{32,0},{64,32},{96,64},{128,96},{160,128},{192,160},{224,1... | collective-permute-start | bytes 1572872 | tf_op jit(solution)/shard_map/ppermute | solution.py:205
  39.0 11.7 %collective-permute-start.7 = (bf16[2,1024,128]{2,1,0:T(8,128)(2,1)}, bf16[2,1024,128]{2,1,0:T(8,128)(2,1)}, u32[]{:S(2)}, u32[]{:S(2)}) collective-permute-start(bf16[2,1024,128]{2,1,0:T(8,128)(2,1)} %collective-permute-done.2.refs_4_), channel_id=1, source_target_pairs={{0,1},{1,0},{2,3},{3,2},{4,5},{5,4},{6,7},{7,6},{8,9},{9,8},{10,11... | collective-permute-start | bytes 1572872 | tf_op jit(solution)/shard_map/ppermute | solution.py:200
  39.3 14.8 %collective-permute-start.4 = (bf16[2,1024,128]{2,1,0:T(8,128)(2,1)}, bf16[2,1024,128]{2,1,0:T(8,128)(2,1)}, u32[]{:S(2)}, u32[]{:S(2)}) collective-permute-start(bf16[2,1024,128]{2,1,0:T(8,128)(2,1)} %collective-permute-done.2.refs_4_), channel_id=1, source_target_pairs={{0,32},{32,64},{64,96},{96,128},{128,160},{160,192},{192,224},{224... | collective-permute-start | bytes 1572872 | tf_op jit(solution)/shard_map/ppermute | solution.py:205
  44.7 1.0 %copy-start.1 = (bf16[512,512]{1,0:T(8,128)(2,1)S(1)}, bf16[512,512]{1,0:T(8,128)(2,1)}, u32[]{:S(2)}) copy-start(bf16[512,512]{1,0:T(8,128)(2,1)} %refs_0_.1) | copy-start | bytes 1572868
  54.1 33.8 %all-to-all-start.1 = ((bf16[16,512,128]{2,1,0:T(8,128)(2,1)}), bf16[16,512,128]{2,1,0:T(8,128)(2,1)}, u32[]{:S(2)}, u32[]{:S(2)}) async-start(bf16[16,512,128]{2,1,0:T(8,128)(2,1)} %bitcast.14), calls=%async_computation.1 | async-start | bytes 4194304 | tf_op jit(solution)/shard_map/all_to_all | solution.py:209
  60.5 13.6 %collective-permute-start.8 = (bf16[2,1024,128]{2,1,0:T(8,128)(2,1)}, bf16[2,1024,128]{2,1,0:T(8,128)(2,1)S(1)}, u32[]{:S(2)}, u32[]{:S(2)}) collective-permute-start(bf16[2,1024,128]{2,1,0:T(8,128)(2,1)} %collective-permute-done.5.refs_5_), channel_id=1, source_target_pairs={{0,224},{32,0},{64,32},{96,64},{128,96},{160,128},{192,160},{224,1... | collective-permute-start | bytes 1572872 | tf_op jit(solution)/shard_map/ppermute | solution.py:205
  60.7 14.9 %collective-permute-start.9 = (bf16[2,1024,128]{2,1,0:T(8,128)(2,1)}, bf16[2,1024,128]{2,1,0:T(8,128)(2,1)}, u32[]{:S(2)}, u32[]{:S(2)}) collective-permute-start(bf16[2,1024,128]{2,1,0:T(8,128)(2,1)} %collective-permute-done.4.refs_6_), channel_id=1, source_target_pairs={{0,32},{32,64},{64,96},{96,128},{128,160},{160,192},{192,224},{224... | collective-permute-start | bytes 1572872 | tf_op jit(solution)/shard_map/ppermute | solution.py:205
  62.0 16.4 %collective-permute-start.12 = (bf16[2,1024,128]{2,1,0:T(8,128)(2,1)}, bf16[2,1024,128]{2,1,0:T(8,128)(2,1)S(1)}, u32[]{:S(2)}, u32[]{:S(2)}) collective-permute-start(bf16[2,1024,128]{2,1,0:T(8,128)(2,1)} %collective-permute-done.5.refs_5_), channel_id=1, source_target_pairs={{0,1},{1,0},{2,3},{3,2},{4,5},{5,4},{6,7},{7,6},{8,9},{9,8},{10,11... | collective-permute-start | bytes 1572872 | tf_op jit(solution)/shard_map/ppermute | solution.py:200
  62.8 24.1 %collective-permute-start.13 = (bf16[2,1024,128]{2,1,0:T(8,128)(2,1)}, bf16[2,1024,128]{2,1,0:T(8,128)(2,1)}, u32[]{:S(2)}, u32[]{:S(2)}) collective-permute-start(bf16[2,1024,128]{2,1,0:T(8,128)(2,1)} %collective-permute-done.4.refs_6_), channel_id=1, source_target_pairs={{0,1},{1,0},{2,3},{3,2},{4,5},{5,4},{6,7},{7,6},{8,9},{9,8},{10,11... | collective-permute-start | bytes 1572872 | tf_op jit(solution)/shard_map/ppermute | solution.py:200
  74.1 13.8 %copy-start.2 = (bf16[2,1024,128]{2,1,0:T(8,128)(2,1)}, bf16[2,1024,128]{2,1,0:T(8,128)(2,1)S(1)}, u32[]{:S(2)}) copy-start(bf16[2,1024,128]{2,1,0:T(8,128)(2,1)S(1)} %collective-permute-done.8.refs_7_) | copy-start | bytes 1572868
  74.2 7.1 %collective-permute-start.11 = (bf16[1024,128]{1,0:T(8,128)(2,1)S(1)}, bf16[1024,128]{1,0:T(8,128)(2,1)S(1)}, u32[]{:S(2)}, u32[]{:S(2)}) collective-permute-start(bf16[1024,128]{1,0:T(8,128)(2,1)S(1)} %slice_bitcast_fusion), channel_id=1, source_target_pairs={{0,224},{32,0},{64,32},{96,64},{128,96},{160,128},{192,160},{224,1... | collective-permute-start | bytes 786440 | tf_op jit(solution)/shard_map/ppermute | solution.py:205
  76.6 8.2 %collective-permute-start.10 = (bf16[1024,128]{1,0:T(8,128)(2,1)S(1)}, bf16[1024,128]{1,0:T(8,128)(2,1)S(1)}, u32[]{:S(2)}, u32[]{:S(2)}) collective-permute-start(bf16[1024,128]{1,0:T(8,128)(2,1)S(1)} %slice_bitcast_fusion.1), channel_id=1, source_target_pairs={{0,32},{32,64},{64,96},{96,128},{128,160},{160,192},{192,224},{224... | collective-permute-start | bytes 786440 | tf_op jit(solution)/shard_map/ppermute | solution.py:205
  76.9 10.0 %collective-permute-start.14 = (bf16[2,1024,128]{2,1,0:T(8,128)(2,1)S(1)}, bf16[2,1024,128]{2,1,0:T(8,128)(2,1)}, u32[]{:S(2)}, u32[]{:S(2)}) collective-permute-start(bf16[2,1024,128]{2,1,0:T(8,128)(2,1)S(1)} %collective-permute-done.8.refs_7_), channel_id=1, source_target_pairs={{0,1},{1,0},{2,3},{3,2},{4,5},{5,4},{6,7},{7,6},{8,9},{9,8},{10,11... | collective-permute-start | bytes 1572872 | tf_op jit(solution)/shard_map/ppermute | solution.py:200
  78.4 0.8 copy-start.3
  78.4 9.5 %collective-permute-start.15 = (bf16[2,1024,128]{2,1,0:T(8,128)(2,1)}, bf16[2,1024,128]{2,1,0:T(8,128)(2,1)}, u32[]{:S(2)}, u32[]{:S(2)}) collective-permute-start(bf16[2,1024,128]{2,1,0:T(8,128)(2,1)} %collective-permute-done.9.refs_8_), channel_id=1, source_target_pairs={{0,1},{1,0},{2,3},{3,2},{4,5},{5,4},{6,7},{7,6},{8,9},{9,8},{10,11... | collective-permute-start | bytes 1572872 | tf_op jit(solution)/shard_map/ppermute | solution.py:200
  81.2 5.7 %collective-permute-start.17 = (bf16[1024,128]{1,0:T(8,128)(2,1)S(1)}, bf16[1024,128]{1,0:T(8,128)(2,1)S(1)}, u32[]{:S(2)}, u32[]{:S(2)}) collective-permute-start(bf16[1024,128]{1,0:T(8,128)(2,1)S(1)} %collective-permute-done.11.refs_10_), channel_id=1, source_target_pairs={{0,1},{1,0},{2,3},{3,2},{4,5},{5,4},{6,7},{7,6},{8,9},{9,8},{10,11... | collective-permute-start | bytes 786440 | tf_op jit(solution)/shard_map/ppermute | solution.py:200
  84.8 3.2 %collective-permute-start.16 = (bf16[1024,128]{1,0:T(8,128)(2,1)S(1)}, bf16[1024,128]{1,0:T(8,128)(2,1)S(1)}, u32[]{:S(2)}, u32[]{:S(2)}) collective-permute-start(bf16[1024,128]{1,0:T(8,128)(2,1)S(1)} %collective-permute-done.10.refs_9_), channel_id=1, source_target_pairs={{0,1},{1,0},{2,3},{3,2},{4,5},{5,4},{6,7},{7,6},{8,9},{9,8},{10,11... | collective-permute-start | bytes 786440 | tf_op jit(solution)/shard_map/ppermute | solution.py:200

commit v4 on v3

--- a/solution.py
+++ b/solution.py
@@ -25,43 +25,55 @@
     return jnp.where(source == column, 1.0, 0.0).astype(jnp.bfloat16)
 
 
-def slice_kernel(grad_ref, out_ref, parts, in_sems, out_sems):
-    def arrival(part):
-        return pltpu.make_async_copy(grad_ref.at[:, pl.ds(part * LANES, LANES)], parts.at[part], in_sems.at[part])
-
-    def departure(part):
-        return pltpu.make_async_copy(parts.at[part], out_ref.at[part], out_sems.at[part])
-
-    for part in range(PARTS):
-        arrival(part).start()
-    for part in range(PARTS):
-        arrival(part).wait()
-        departure(part).start()
-    for part in range(PARTS):
-        departure(part).wait()
-
-
-def sliced(grad):
+def slice_kernel(experts, hidden, grad_ref, out_ref, grad, parts, in_sems, out_sems):
+    groups, rows, columns = grad.shape
+
+    def arrival(group):
+        lanes = pl.ds(group * columns, columns)
+        return pltpu.make_async_copy(grad_ref.at[:, lanes], grad.at[group], in_sems.at[group])
+
+    def departure(group):
+        there = pl.ds(group * GROUP, GROUP)
+        return pltpu.make_async_copy(parts.at[there], out_ref.at[there], out_sems.at[group])
+
+    for group in range(groups):
+        arrival(group).start()
+    order = order_matrix(rows, experts, hidden)
+    for group in range(groups):
+        arrival(group).wait()
+        moved = jnp.dot(order, grad[group], preferred_element_type=jnp.float32).astype(jnp.bfloat16)
+        for k in range(GROUP):
+            parts[group * GROUP + k] = moved[:, k * LANES : (k + 1) * LANES]
+        departure(group).start()
+    for group in range(groups):
+        departure(group).wait()
+
+
+def sliced(grad, experts, hidden):
     rows, width = grad.shape
+    groups = PARTS // GROUP
     shape = (PARTS, rows, LANES)
     return pl.pallas_call(
-        slice_kernel,
+        lambda *refs: slice_kernel(experts, hidden, *refs),
         out_shape=jax.ShapeDtypeStruct(shape, jnp.bfloat16),
         in_specs=[ANY],
         out_specs=ANY,
         scratch_shapes=[
+            pltpu.VMEM((groups, rows, GROUP * LANES), jnp.bfloat16),
             pltpu.VMEM(shape, jnp.bfloat16),
-            pltpu.SemaphoreType.DMA((PARTS,)),
-            pltpu.SemaphoreType.DMA((PARTS,)),
+            pltpu.SemaphoreType.DMA((groups,)),
+            pltpu.SemaphoreType.DMA((groups,)),
         ],
         compiler_params=pltpu.CompilerParams(vmem_limit_bytes=58 * MIB),
-        cost_estimate=pl.CostEstimate(flops=0, bytes_accessed=4 * rows * width, transcendentals=0),
+        cost_estimate=pl.CostEstimate(
+            flops=2 * rows * rows * width, bytes_accessed=4 * rows * width, transcendentals=0
+        ),
         name="slice_columns",
     )(grad)
 
 
-def mix_kernel(experts, hidden, root_ref, in_ref, out_ref, root, turned, mixed, in_sem, out_sems):
-    groups, rows, lanes = in_ref.shape
+def mix_kernel(root_ref, in_ref, out_ref, root, mixed, in_sem, out_sems):
+    groups, hidden, experts, lanes = in_ref.shape
 
     def departure(h):
         there = (slice(None), pl.ds(h, GROUP))
@@ -69,16 +81,9 @@
 
     arrival = pltpu.make_async_copy(root_ref, root, in_sem)
     arrival.start()
-    order = order_matrix(rows, experts, hidden)
-    for group in range(0, groups, GROUP):
-        some = jnp.concatenate([in_ref[group + k] for k in range(GROUP)], axis=1)
-        moved = jnp.dot(order, some, preferred_element_type=jnp.float32).astype(jnp.bfloat16)
-        for k in range(GROUP):
-            at = slice((group + k) * experts, (group + k + 1) * experts)
-            turned[:, at] = moved[:, k * lanes : (k + 1) * lanes].reshape(hidden, experts, lanes)
     arrival.wait()
     for h in range(0, hidden, GROUP):
-        some = jnp.concatenate([turned[h + k] for k in range(GROUP)], axis=1)
+        some = jnp.concatenate([in_ref[:, h + k].reshape(groups * experts, lanes) for k in range(GROUP)], axis=1)
         sums = jnp.dot(root[...], some, preferred_element_type=jnp.float32).astype(jnp.bfloat16)
         for k in range(GROUP):
             mixed[:, h + k] = sums[:, k * lanes : (k + 1) * lanes].reshape(groups, experts, lanes)
@@ -87,19 +92,17 @@
         departure(h).wait()
 
 
-def mixed_experts(expert_root, held, experts, hidden):
-    groups, rows, lanes = held.shape
+def mixed_experts(expert_root, held):
+    groups, hidden, experts, lanes = held.shape
     total = groups * experts
-    shape = (groups, hidden, experts, lanes)
     return pl.pallas_call(
-        lambda *refs: mix_kernel(experts, hidden, *refs),
-        out_shape=jax.ShapeDtypeStruct(shape, jnp.bfloat16),
+        mix_kernel,
+        out_shape=jax.ShapeDtypeStruct(held.shape, jnp.bfloat16),
         in_specs=[ANY, VMEM],
         out_specs=ANY,
         scratch_shapes=[
             pltpu.VMEM((total, total), jnp.bfloat16),
-            pltpu.VMEM((hidden, total, lanes), jnp.bfloat16),
-            pltpu.VMEM(shape, jnp.bfloat16),
+            pltpu.VMEM(held.shape, jnp.bfloat16),
             pltpu.SemaphoreType.DMA,
             pltpu.SemaphoreType.DMA((hidden // GROUP,)),
         ],
@@ -122,10 +125,9 @@
 
     def root_arrivals(side, step):
         pieces_of, sem = sources[side], root_sems.at[side]
-        if step < steps - 1:
-            return [pltpu.make_async_copy(pieces_of[step], roots.at[side, step], sem.at[step])]
         return [
-            pltpu.make_async_copy(pieces_of[step + k], roots.at[side, step, k], sem.at[step + k]) for k in range(2)
+            pltpu.make_async_copy(pieces_of[2 * step + k], roots.at[side, step, k], sem.at[2 * step + k])
+            for k in range(2)
         ]
 
     def momentum_arrival(step):
@@ -180,7 +182,7 @@
         scratch_shapes=[
             pltpu.VMEM(held.shape, jnp.bfloat16),
             pltpu.VMEM((2, rows, width // 2), jnp.bfloat16),
-            pltpu.VMEM((2, steps, *own[0].shape), jnp.bfloat16),
+            pltpu.VMEM((2, steps, 2, *own[0].shape), jnp.bfloat16),
             pltpu.VMEM((steps, rows, columns), jnp.float32),
             pltpu.VMEM((steps, rows, columns), jnp.float32),
             pltpu.SemaphoreType.DMA,
@@ -200,6 +202,10 @@
     return lax.ppermute(value, axis, [(0, 1), (1, 0)])
 
 
+def across(value):
+    return lax.ppermute(value, ("yh", "yl"), [(place, 3 - place) for place in range(4)])
+
+
 def along_z(value, step):
     n = SIZES[0]
     return lax.ppermute(value, "z", [(i, (i + step) % n) for i in range(n)])
@@ -216,25 +222,45 @@
     z, yh, core = (lax.axis_index(axis) for axis in ("z", "yh", "core"))
 
     mine = lax.dynamic_slice_in_dim(model_root, core * half, half, axis=1).T
-    theirs = swap(mine, "yh")
-    here = jnp.stack([mine, theirs])
-    sent = sliced(grad_block.reshape(rows, width))
-    here, sent = lax.optimization_barrier((here, sent))
+    sent = sliced(grad_block.reshape(rows, width), experts, hidden)
+    mine, sent = lax.optimization_barrier((mine, sent))
+    near, far = {0: mine}, {}
+
+    def spread(shares, distance):
+        shares[distance] = along_z(shares[distance - 1], -1)
+        shares[-distance] = along_z(shares[1 - distance], 1)
+
+    def cross(*places):
+        for place in places:
+            far[place] = across(near[place])
 
     held = exchange(sent)
-    up1, down1 = along_z(here, 1), along_z(here, -1)
-    first = (swap(here, "core"),)
-    held, first, _, _ = lax.optimization_barrier((held, first, up1, down1))
-
-    up2, down2 = along_z(up1, 1), along_z(down1, -1)
-    blended = mixed_experts(expert_root, held, experts, hidden)
-    second = (swap(down1, "core"), swap(up1, "core"))
-    blended, up2, down2, second = lax.optimization_barrier((blended, up2, down2, second))
+    spread(near, 1)
+    cross(0)
+    spread(near, 2)
+    cross(1, -1)
+    others = {0: [swap(near[0], "core"), swap(far[0], "core")]}
+    held, others, near[2], near[-2], far[1], far[-1] = lax.optimization_barrier(
+        (held, others, near[2], near[-2], far[1], far[-1])
+    )
+
+    blended = mixed_experts(expert_root, held.reshape(PARTS, hidden, experts, LANES))
+    blended, near[2], near[-2] = lax.optimization_barrier((blended, near[2], near[-2]))
 
     back = exchange(blended.reshape(PARTS, rows, LANES))
-    up3, down3 = along_z(up2, 1), along_z(down2, -1)
-    own = (here, down1, up1, down2, up2, down3, up3, along_z(up3[0], 1), along_z(down3[1], -1))
-    other = first + second + tuple(swap(piece, "core") for piece in own[3:])
+    spread(near, 3)
+    cross(2, -2)
+    early = [shares[place] for place in OFFSETS[1:5] for shares in (near, far)]
+    near[4] = along_z(near[-3], 1)
+    spread(far, 3)
+    cross(4)
+    early, near[3], near[-3] = lax.optimization_barrier((early, near[3], near[-3]))
+    for index, place in enumerate(OFFSETS[1:5]):
+        others[place] = [swap(piece, "core") for piece in early[2 * index : 2 * index + 2]]
+    for place in OFFSETS[5:]:
+        others[place] = [swap(shares[place], "core") for shares in (near, far)]
+    own = [shares[place] for place in OFFSETS for shares in (near, far)]
+    other = [piece for place in OFFSETS for piece in others[place]]
 
     order = [lax.rem(z + SIZES[0] + offset, SIZES[0]) for offset in OFFSETS]
     place = jnp.stack([yh, core, *order]).astype(jnp.int32)

time: 99.8 us -> 97.5 us (0.977)
  waiting for transfers between devices: 39.6 us -> 21.7 us
  starting transfers between devices: 38.2 us -> 54.9 us
    ppermute x8 -> x9, waiting for transfers between devices: 30.8 us -> 11.9 us  [along_z(): return lax.ppermute(value, 'z', [(i, (i + step) % n) for i in range(n)])]
    ppermute x0 -> x6, starting transfers between devices: none -> 11.9 us  [across(): lax.ppermute(value, ('yh', 'yl'), [(place, 3 - place) for place in range(...]
    ppermute x0 -> x6, waiting for transfers between devices: none -> 7.83 us  [across(): lax.ppermute(value, ('yh', 'yl'), [(place, 3 - place) for place in range(...]
    all_to_all x2, waiting for transfers between devices: 5.42 us -> 0.01 us  [exchange(): return lax.all_to_all(value, EXP, split_axis=0, concat_axis=0, tiled=True)]
    ppermute x8 -> x9, starting transfers between devices: 12.4 us -> 17 us  [along_z(): return lax.ppermute(value, 'z', [(i, (i + step) % n) for i in range(n)])]
    ppermute x10 -> x16, waiting for transfers between devices: 3.44 us -> 1.9 us  [swap(): return lax.ppermute(value, axis, [(0, 1), (1, 0)])]
    ppermute x10 -> x16, starting transfers between devices: 11.7 us -> 13.1 us  [swap(): return lax.ppermute(value, axis, [(0, 1), (1, 0)])]
    all_to_all x2, starting transfers between devices: 14.1 us -> 12.9 us  [exchange(): return lax.all_to_all(value, EXP, split_axis=0, concat_axis=0, tiled=True)]
  transfers between devices with their start and end apart: 20 -> 33, of which waited for: 9 -> 13; matrix products, arithmetic and copies ran while one was open for 1% -> 0% of each run, Pallas kernels for 6% -> 0%
where the time goes in v4:
time: 97.5 us; the launch traced here: 97.3 us
  starting transfers between devices  54.9 us (56%)
  waiting for transfers between devices  21.7 us (22%)
  Pallas kernels  16.8 us (17%)
  local copies, waits for them, and re-layouts  3.48 us (4%)
    ppermute x9, starting transfers between devices, along_z(): return lax.ppermute(value, 'z', [(i, (i + step) % n) for i in range(n)])  17 us
    ppermute x16, starting transfers between devices, swap(): return lax.ppermute(value, axis, [(0, 1), (1, 0)])  13.1 us
    all_to_all x2, starting transfers between devices, exchange(): return lax.all_to_all(value, EXP, split_axis=0, concat_axis=0, tiled=True)  12.9 us
    ppermute x9, waiting for transfers between devices, along_z(): return lax.ppermute(value, 'z', [(i, (i + step) % n) for i in range(n)])  11.9 us
    ppermute x6, starting transfers between devices, across(): lax.ppermute(value, ('yh', 'yl'), [(place, 3 - place) for place in range(...  11.9 us
    pallas_call x1, Pallas kernels, finished(): pl.pallas_call(lambda *refs: finish_kernel(experts, hidden, pieces, *refs...  11 us
    ppermute x6, waiting for transfers between devices, across(): lax.ppermute(value, ('yh', 'yl'), [(place, 3 - place) for place in range(...  7.83 us
    pallas_call x1, Pallas kernels, sliced(): pl.pallas_call(lambda *refs: slice_kernel(experts, hidden, *refs), out_sh...  3.67 us
  transfers between devices with their start and end apart: 33, of which 13 were waited for; matrix products, arithmetic and copies ran while one was open for 0% of the time, Pallas kernels for 0%

profile of v4, /device:TPU:1, one launch (start us, length us, event | category | flops | bytes accessed | tf_op | source)
XLA Modules:
  0.0 97.3 jit_solution(7149951389325893494)
XLA Ops:
  0.0 1.0 %copy-done = bf16[128,2048]{1,0:T(8,128)(2,1)S(1)} copy-done((bf16[128,2048]{1,0:T(8,128)(2,1)S(1)}, bf16[128,2048]{1,0:T(8,128)(2,1)}, u32[]{:S(2)}) %copy-start) | copy-done | bytes 524312
  1.1 0.2 copy.6
  1.2 3.7 %slice_columns.1 = bf16[16,512,128]{2,1,0:T(8,128)(2,1)} custom-call(bf16[512,2048]{1,0:T(8,128)(2,1)} %bitcast.23), custom_call_target="tpu_custom_call" | custom-call | flops 1073741824 | bytes 4194304 | tf_op jit(solution)/shard_map/slice_columns/pallas_call | solution.py:56
  4.9 0.0 copy-start.1
  4.9 7.0 %all-to-all-start = ((bf16[16,512,128]{2,1,0:T(8,128)(2,1)}), bf16[16,512,128]{2,1,0:T(8,128)(2,1)S(1)}, u32[]{:S(2)}, u32[]{:S(2)}) async-start(bf16[16,512,128]{2,1,0:T(8,128)(2,1)} %slice_columns.1), calls=%async_computation | async-start | bytes 4194304 | tf_op jit(solution)/shard_map/all_to_all | solution.py:215
  11.9 1.6 %collective-permute-start.5 = (bf16[1024,128]{1,0:T(8,128)(2,1)S(1)}, bf16[1024,128]{1,0:T(8,128)(2,1)S(1)}, u32[]{:S(2)}, u32[]{:S(2)}) collective-permute-start(bf16[1024,128]{1,0:T(8,128)(2,1)S(1)} %bitcast.17), channel_id=1, source_target_pairs={{0,32},{32,64},{64,96},{96,128},{128,160},{160,192},{192,224},{224... | collective-permute-start | bytes 786440 | tf_op jit(solution)/shard_map/ppermute | solution.py:211
  13.5 4.0 %collective-permute-start.3 = (bf16[1024,128]{1,0:T(8,128)(2,1)S(1)}, bf16[1024,128]{1,0:T(8,128)(2,1)S(1)}, u32[]{:S(2)}, u32[]{:S(2)}) collective-permute-start(bf16[1024,128]{1,0:T(8,128)(2,1)S(1)} %bitcast.18), channel_id=1, source_target_pairs={{0,224},{32,0},{64,32},{96,64},{128,96},{160,128},{192,160},{224,1... | collective-permute-start | bytes 786440 | tf_op jit(solution)/shard_map/ppermute | solution.py:211
  17.6 2.8 %collective-permute-start.1 = (bf16[1024,128]{1,0:T(8,128)(2,1)S(1)}, bf16[1024,128]{1,0:T(8,128)(2,1)S(1)}, u32[]{:S(2)}, u32[]{:S(2)}) collective-permute-start(bf16[1024,128]{1,0:T(8,128)(2,1)S(1)} %bitcast.19), channel_id=1, source_target_pairs={{0,18},{2,16},{16,2},{18,0},{1,19},{3,17},{17,3},{19,1},{4,22},{6,... | collective-permute-start | bytes 786440 | tf_op jit(solution)/shard_map/ppermute | solution.py:206
  20.4 0.9 collective-permute-start
  21.3 2.8 %collective-permute-done.5.refs_6_ = bf16[1024,128]{1,0:T(8,128)(2,1)S(1)} collective-permute-done((bf16[1024,128]{1,0:T(8,128)(2,1)S(1)}, bf16[1024,128]{1,0:T(8,128)(2,1)S(1)}, u32[]{:S(2)}, u32[]{:S(2)}) %collective-permute-start.5) | collective-permute-done | bytes 262176 | tf_op jit(solution)/shard_map/ppermute | solution.py:211
  24.1 2.6 %collective-permute-start.8 = (bf16[1024,128]{1,0:T(8,128)(2,1)S(1)}, bf16[1024,128]{1,0:T(8,128)(2,1)S(1)}, u32[]{:S(2)}, u32[]{:S(2)}) collective-permute-start(bf16[1024,128]{1,0:T(8,128)(2,1)S(1)} %collective-permute-done.5.refs_6_), channel_id=1, source_target_pairs={{0,18},{2,16},{16,2},{18,0},{1,19},{3,17},{17,3},{19,1},{4,22},{6,... | collective-permute-start | bytes 786440 | tf_op jit(solution)/shard_map/ppermute | solution.py:206
  26.7 0.0 collective-permute-start.6
  26.7 0.0 collective-permute-done.3.refs_4_
  26.7 0.2 collective-permute-start.7
  26.9 0.0 collective-permute-done.1.refs_3_
  26.9 2.6 %collective-permute-start.4 = (bf16[1024,128]{1,0:T(8,128)(2,1)S(1)}, bf16[1024,128]{1,0:T(8,128)(2,1)S(1)}, u32[]{:S(2)}, u32[]{:S(2)}) collective-permute-start(bf16[1024,128]{1,0:T(8,128)(2,1)S(1)} %collective-permute-done.3.refs_4_), channel_id=1, source_target_pairs={{0,224},{32,0},{64,32},{96,64},{128,96},{160,128},{192,160},{224,1... | collective-permute-start | bytes 786440 | tf_op jit(solution)/shard_map/ppermute | solution.py:211
  29.5 0.0 collective-permute-done.refs_18_
  29.5 1.8 %collective-permute-start.2 = (bf16[1024,128]{1,0:T(8,128)(2,1)S(1)}, bf16[1024,128]{1,0:T(8,128)(2,1)}, u32[]{:S(2)}, u32[]{:S(2)}) collective-permute-start(bf16[1024,128]{1,0:T(8,128)(2,1)S(1)} %collective-permute-done.1.refs_3_), channel_id=1, source_target_pairs={{0,1},{1,0},{2,3},{3,2},{4,5},{5,4},{6,7},{7,6},{8,9},{9,8},{10,11... | collective-permute-start | bytes 786440 | tf_op jit(solution)/shard_map/ppermute | solution.py:202
  31.2 0.7 copy-done.6
  31.9 0.5 collective-permute-done.8.refs_7_
  32.5 2.1 %collective-permute-done.6.refs_10_ = bf16[1024,128]{1,0:T(8,128)(2,1)S(1)} collective-permute-done((bf16[1024,128]{1,0:T(8,128)(2,1)S(1)}, bf16[1024,128]{1,0:T(8,128)(2,1)S(1)}, u32[]{:S(2)}, u32[]{:S(2)}) %collective-permute-start.6) | collective-permute-done | bytes 262176 | tf_op jit(solution)/shard_map/ppermute | solution.py:211
  34.6 3.5 %collective-permute-done.7.refs_5_ = bf16[1024,128]{1,0:T(8,128)(2,1)S(1)} collective-permute-done((bf16[1024,128]{1,0:T(8,128)(2,1)S(1)}, bf16[1024,128]{1,0:T(8,128)(2,1)S(1)}, u32[]{:S(2)}, u32[]{:S(2)}) %collective-permute-start.7) | collective-permute-done | bytes 262176 | tf_op jit(solution)/shard_map/ppermute | solution.py:206
  38.1 0.0 collective-permute-done.4.refs_8_
  38.2 0.7 copy-done.10
  38.8 0.7 copy-done.12
  39.5 2.1 %mix_experts.1 = bf16[16,16,32,128]{3,2,1,0:T(8,128)(2,1)} custom-call(bf16[512,512]{1,0:T(8,128)(2,1)S(1)} %copy-done.1, bf16[16,16,32,128]{3,2,1,0:T(8,128)(2,1)S(1)} %bitcast.16), custom_call_target="tpu_custom_call" | custom-call | tf_op jit(solution)/shard_map/mix_experts/pallas_call | solution.py:98
  41.7 5.9 %all-to-all-start.1 = ((bf16[16,512,128]{2,1,0:T(8,128)(2,1)}), bf16[16,512,128]{2,1,0:T(8,128)(2,1)}, u32[]{:S(2)}, u32[]{:S(2)}) async-start(bf16[16,512,128]{2,1,0:T(8,128)(2,1)} %bitcast.13), calls=%async_computation.1 | async-start | bytes 4194304 | tf_op jit(solution)/shard_map/all_to_all | solution.py:215
  47.7 3.8 %collective-permute-start.9 = (bf16[1024,128]{1,0:T(8,128)(2,1)S(1)}, bf16[1024,128]{1,0:T(8,128)(2,1)S(1)}, u32[]{:S(2)}, u32[]{:S(2)}) collective-permute-start(bf16[1024,128]{1,0:T(8,128)(2,1)S(1)} %copy-done.13), channel_id=1, source_target_pairs={{0,18},{2,16},{16,2},{18,0},{1,19},{3,17},{17,3},{19,1},{4,22},{6,... | collective-permute-start | bytes 786440 | tf_op jit(solution)/shard_map/ppermute | solution.py:206
  51.5 0.3 collective-permute-start.12
  51.8 3.9 %collective-permute-start.11 = (bf16[1024,128]{1,0:T(8,128)(2,1)S(1)}, bf16[1024,128]{1,0:T(8,128)(2,1)S(1)}, u32[]{:S(2)}, u32[]{:S(2)}) collective-permute-start(bf16[1024,128]{1,0:T(8,128)(2,1)S(1)} %copy-done.13), channel_id=1, source_target_pairs={{0,224},{32,0},{64,32},{96,64},{128,96},{160,128},{192,160},{224,1... | collective-permute-start | bytes 786440 | tf_op jit(solution)/shard_map/ppermute | solution.py:211
  55.7 0.2 collective-permute-start.10
  55.9 2.1 %collective-permute-done.9.refs_9_ = bf16[1024,128]{1,0:T(8,128)(2,1)S(1)} collective-permute-done((bf16[1024,128]{1,0:T(8,128)(2,1)S(1)}, bf16[1024,128]{1,0:T(8,128)(2,1)S(1)}, u32[]{:S(2)}, u32[]{:S(2)}) %collective-permute-start.9) | collective-permute-done | bytes 262176 | tf_op jit(solution)/shard_map/ppermute | solution.py:206
  58.0 4.4 %collective-permute-start.13 = (bf16[1024,128]{1,0:T(8,128)(2,1)S(1)}, bf16[1024,128]{1,0:T(8,128)(2,1)}, u32[]{:S(2)}, u32[]{:S(2)}) collective-permute-start(bf16[1024,128]{1,0:T(8,128)(2,1)S(1)} %collective-permute-done.9.refs_9_), channel_id=1, source_target_pairs={{0,224},{32,0},{64,32},{96,64},{128,96},{160,128},{192,160},{224,1... | collective-permute-start | bytes 786440 | tf_op jit(solution)/shard_map/ppermute | solution.py:211
  62.4 0.0 collective-permute-start.15
  62.4 1.7 %collective-permute-done.10.refs_11_ = bf16[1024,128]{1,0:T(8,128)(2,1)S(1)} collective-permute-done((bf16[1024,128]{1,0:T(8,128)(2,1)S(1)}, bf16[1024,128]{1,0:T(8,128)(2,1)S(1)}, u32[]{:S(2)}, u32[]{:S(2)}) %collective-permute-start.10) | collective-permute-done | bytes 262176 | tf_op jit(solution)/shard_map/ppermute | solution.py:206
  64.1 1.6 %collective-permute-start.17 = (bf16[1024,128]{1,0:T(8,128)(2,1)S(1)}, bf16[1024,128]{1,0:T(8,128)(2,1)S(1)}, u32[]{:S(2)}, u32[]{:S(2)}) collective-permute-start(bf16[1024,128]{1,0:T(8,128)(2,1)S(1)} %copy-done.5), channel_id=1, source_target_pairs={{0,1},{1,0},{2,3},{3,2},{4,5},{5,4},{6,7},{7,6},{8,9},{9,8},{10,11... | collective-permute-start | bytes 786440 | tf_op jit(solution)/shard_map/ppermute | solution.py:202
  65.7 0.1 collective-permute-start.18
  65.8 0.4 collective-permute-start.19
  66.2 0.9 collective-permute-done.13.refs_13_
  67.1 1.8 %collective-permute-start.20 = (bf16[1024,128]{1,0:T(8,128)(2,1)S(1)}, bf16[1024,128]{1,0:T(8,128)(2,1)S(1)}, u32[]{:S(2)}, u32[]{:S(2)}) collective-permute-start(bf16[1024,128]{1,0:T(8,128)(2,1)S(1)} %copy-done.9), channel_id=1, source_target_pairs={{0,1},{1,0},{2,3},{3,2},{4,5},{5,4},{6,7},{7,6},{8,9},{9,8},{10,11... | collective-permute-start | bytes 786440 | tf_op jit(solution)/shard_map/ppermute | solution.py:202
  68.9 1.4 %collective-permute-done.15.refs_16_ = bf16[1024,128]{1,0:T(8,128)(2,1)} collective-permute-done((bf16[1024,128]{1,0:T(8,128)(2,1)S(1)}, bf16[1024,128]{1,0:T(8,128)(2,1)}, u32[]{:S(2)}, u32[]{:S(2)}) %collective-permute-start.15) | collective-permute-done | bytes 262176 | tf_op jit(solution)/shard_map/ppermute | solution.py:211
  70.3 2.1 %collective-permute-start.21 = (bf16[1024,128]{1,0:T(8,128)(2,1)S(1)}, bf16[1024,128]{1,0:T(8,128)(2,1)S(1)}, u32[]{:S(2)}, u32[]{:S(2)}) collective-permute-start(bf16[1024,128]{1,0:T(8,128)(2,1)S(1)} %copy-done.13), channel_id=1, source_target_pairs={{0,1},{1,0},{2,3},{3,2},{4,5},{5,4},{6,7},{7,6},{8,9},{9,8},{10,11... | collective-permute-start | bytes 786440 | tf_op jit(solution)/shard_map/ppermute | solution.py:202
  72.4 0.0 collective-permute-done.17.refs_20_
  72.4 0.1 collective-permute-start.22
  72.5 0.4 collective-permute-start.23
  73.0 0.1 collective-permute-start.24
  73.1 0.0 collective-permute-done.20.refs_23_
  73.1 0.4 collective-permute-start.25
  73.5 0.1 collective-permute-done.21.refs_24_
  73.6 0.0 collective-permute-start.14
  73.6 0.4 collective-permute-done.22.refs_25_
  74.0 2.4 %collective-permute-start.16 = (bf16[1024,128]{1,0:T(8,128)(2,1)}, bf16[1024,128]{1,0:T(8,128)(2,1)}, u32[]{:S(2)}, u32[]{:S(2)}) collective-permute-start(bf16[1024,128]{1,0:T(8,128)(2,1)} %collective-permute-done.15.refs_16_), channel_id=1, source_target_pairs={{0,18},{2,16},{16,2},{18,0},{1,19},{3,17},{17,3},{19,1},{4,22},{6,... | collective-permute-start | bytes 786440 | tf_op jit(solution)/shard_map/ppermute | solution.py:206
  76.3 0.0 collective-permute-done.23.refs_26_
  76.3 0.7 collective-permute-start.27
  77.1 0.1 collective-permute-start.29
  77.2 0.0 collective-permute-done.25.refs_28_
  77.2 0.5 collective-permute-start.26
  77.7 4.8 %collective-permute-done.14.refs_15_ = bf16[1024,128]{1,0:T(8,128)(2,1)} collective-permute-done((bf16[1024,128]{1,0:T(8,128)(2,1)S(1)}, bf16[1024,128]{1,0:T(8,128)(2,1)}, u32[]{:S(2)}, u32[]{:S(2)}) %collective-permute-start.14) | collective-permute-done | bytes 262176 | tf_op jit(solution)/shard_map/ppermute | solution.py:211
  82.4 1.2 %collective-permute-start.28 = (bf16[1024,128]{1,0:T(8,128)(2,1)}, bf16[1024,128]{1,0:T(8,128)(2,1)}, u32[]{:S(2)}, u32[]{:S(2)}) collective-permute-start(bf16[1024,128]{1,0:T(8,128)(2,1)} %collective-permute-done.14.refs_15_), channel_id=1, source_target_pairs={{0,1},{1,0},{2,3},{3,2},{4,5},{5,4},{6,7},{7,6},{8,9},{9,8},{10,11... | collective-permute-start | bytes 786440 | tf_op jit(solution)/shard_map/ppermute | solution.py:202
  83.7 0.9 collective-permute-start.30
  84.6 0.1 stack.43.refs_0_
  84.7 0.4 collective-permute-done.28.refs_31_
  85.1 0.9 collective-permute-done.30.refs_33_
  86.1 11.0 %model_rows.1 = f32[512,2048]{1,0:T(8,128)} custom-call(s32[10]{0:T(128)S(1)} %stack.43.refs_0_, bf16[16,512,128]{2,1,0:T(8,128)(2,1)} %all-to-all-done.1.refs_1_, bf16[1024,128]{1,0:T(8,128)(2,1)S(1)} %bitcast.21, bf16[1024,128]{1,0:T(8,128)(2,1)S(1)} %copy-done.7, bf16[1024,128]{1,0:T(8,128)(2,1)S(1)} %copy-done.5, bf16[1024,128]{1,0:T(8,128)(2,1)S(1)} %copy-done.11, ...), custom_call_target="tpu_custom_call" | custom-call | flops 4294967296 | bytes 18874368 | tf_op jit(solution)/shard_map/model_rows/pallas_call | solution.py:177
  (70 shorter events, 0.2 us)
Async XLA Ops:
  0.0 1.0 %copy-start = (bf16[128,2048]{1,0:T(8,128)(2,1)S(1)}, bf16[128,2048]{1,0:T(8,128)(2,1)}, u32[]{:S(2)}) copy-start(bf16[128,2048]{1,0:T(8,128)(2,1)} %param.6) | copy-start | bytes 1572868
  4.9 34.6 %copy-start.1 = (bf16[512,512]{1,0:T(8,128)(2,1)S(1)}, bf16[512,512]{1,0:T(8,128)(2,1)}, u32[]{:S(2)}) copy-start(bf16[512,512]{1,0:T(8,128)(2,1)} %root_ref.1) | copy-start | bytes 1572868
  4.9 34.6 %all-to-all-start = ((bf16[16,512,128]{2,1,0:T(8,128)(2,1)}), bf16[16,512,128]{2,1,0:T(8,128)(2,1)S(1)}, u32[]{:S(2)}, u32[]{:S(2)}) async-start(bf16[16,512,128]{2,1,0:T(8,128)(2,1)} %slice_columns.1), calls=%async_computation | async-start | bytes 4194304 | tf_op jit(solution)/shard_map/all_to_all | solution.py:215
  11.9 12.2 %collective-permute-start.5 = (bf16[1024,128]{1,0:T(8,128)(2,1)S(1)}, bf16[1024,128]{1,0:T(8,128)(2,1)S(1)}, u32[]{:S(2)}, u32[]{:S(2)}) collective-permute-start(bf16[1024,128]{1,0:T(8,128)(2,1)S(1)} %bitcast.17), channel_id=1, source_target_pairs={{0,32},{32,64},{64,96},{96,128},{128,160},{160,192},{192,224},{224... | collective-permute-start | bytes 786440 | tf_op jit(solution)/shard_map/ppermute | solution.py:211
  13.5 13.2 %collective-permute-start.3 = (bf16[1024,128]{1,0:T(8,128)(2,1)S(1)}, bf16[1024,128]{1,0:T(8,128)(2,1)S(1)}, u32[]{:S(2)}, u32[]{:S(2)}) collective-permute-start(bf16[1024,128]{1,0:T(8,128)(2,1)S(1)} %bitcast.18), channel_id=1, source_target_pairs={{0,224},{32,0},{64,32},{96,64},{128,96},{160,128},{192,160},{224,1... | collective-permute-start | bytes 786440 | tf_op jit(solution)/shard_map/ppermute | solution.py:211
  17.6 9.3 %collective-permute-start.1 = (bf16[1024,128]{1,0:T(8,128)(2,1)S(1)}, bf16[1024,128]{1,0:T(8,128)(2,1)S(1)}, u32[]{:S(2)}, u32[]{:S(2)}) collective-permute-start(bf16[1024,128]{1,0:T(8,128)(2,1)S(1)} %bitcast.19), channel_id=1, source_target_pairs={{0,18},{2,16},{16,2},{18,0},{1,19},{3,17},{17,3},{19,1},{4,22},{6,... | collective-permute-start | bytes 786440 | tf_op jit(solution)/shard_map/ppermute | solution.py:206
  20.4 9.1 %collective-permute-start = (bf16[1024,128]{1,0:T(8,128)(2,1)S(1)}, bf16[1024,128]{1,0:T(8,128)(2,1)S(1)}, u32[]{:S(2)}, u32[]{:S(2)}) collective-permute-start(bf16[1024,128]{1,0:T(8,128)(2,1)S(1)} %bitcast.20), channel_id=1, source_target_pairs={{0,1},{1,0},{2,3},{3,2},{4,5},{5,4},{6,7},{7,6},{8,9},{9,8},{10,11... | collective-permute-start | bytes 786440 | tf_op jit(solution)/shard_map/ppermute | solution.py:202
  24.1 14.0 %copy-start.2 = (bf16[1024,128]{1,0:T(8,128)(2,1)}, bf16[1024,128]{1,0:T(8,128)(2,1)S(1)}, u32[]{:S(2)}) copy-start(bf16[1024,128]{1,0:T(8,128)(2,1)S(1)} %collective-permute-done.5.refs_6_) | copy-start | bytes 786436
  24.1 8.4 %collective-permute-start.8 = (bf16[1024,128]{1,0:T(8,128)(2,1)S(1)}, bf16[1024,128]{1,0:T(8,128)(2,1)S(1)}, u32[]{:S(2)}, u32[]{:S(2)}) collective-permute-start(bf16[1024,128]{1,0:T(8,128)(2,1)S(1)} %collective-permute-done.5.refs_6_), channel_id=1, source_target_pairs={{0,18},{2,16},{16,2},{18,0},{1,19},{3,17},{17,3},{19,1},{4,22},{6,... | collective-permute-start | bytes 786440 | tf_op jit(solution)/shard_map/ppermute | solution.py:206
  26.7 7.9 %collective-permute-start.6 = (bf16[1024,128]{1,0:T(8,128)(2,1)S(1)}, bf16[1024,128]{1,0:T(8,128)(2,1)S(1)}, u32[]{:S(2)}, u32[]{:S(2)}) collective-permute-start(bf16[1024,128]{1,0:T(8,128)(2,1)S(1)} %collective-permute-done.5.refs_6_), channel_id=1, source_target_pairs={{0,32},{32,64},{64,96},{96,128},{128,160},{160,192},{192,224},{224... | collective-permute-start | bytes 786440 | tf_op jit(solution)/shard_map/ppermute | solution.py:211
  26.7 11.4 %copy-start.4 = (bf16[1024,128]{1,0:T(8,128)(2,1)}, bf16[1024,128]{1,0:T(8,128)(2,1)S(1)}, u32[]{:S(2)}) copy-start(bf16[1024,128]{1,0:T(8,128)(2,1)S(1)} %collective-permute-done.3.refs_4_) | copy-start | bytes 786436
  26.7 11.4 %collective-permute-start.7 = (bf16[1024,128]{1,0:T(8,128)(2,1)S(1)}, bf16[1024,128]{1,0:T(8,128)(2,1)S(1)}, u32[]{:S(2)}, u32[]{:S(2)}) collective-permute-start(bf16[1024,128]{1,0:T(8,128)(2,1)S(1)} %collective-permute-done.3.refs_4_), channel_id=1, source_target_pairs={{0,18},{2,16},{16,2},{18,0},{1,19},{3,17},{17,3},{19,1},{4,22},{6,... | collective-permute-start | bytes 786440 | tf_op jit(solution)/shard_map/ppermute | solution.py:206
  26.9 11.2 %collective-permute-start.4 = (bf16[1024,128]{1,0:T(8,128)(2,1)S(1)}, bf16[1024,128]{1,0:T(8,128)(2,1)S(1)}, u32[]{:S(2)}, u32[]{:S(2)}) collective-permute-start(bf16[1024,128]{1,0:T(8,128)(2,1)S(1)} %collective-permute-done.3.refs_4_), channel_id=1, source_target_pairs={{0,224},{32,0},{64,32},{96,64},{128,96},{160,128},{192,160},{224,1... | collective-permute-start | bytes 786440 | tf_op jit(solution)/shard_map/ppermute | solution.py:211
  29.5 8.7 %copy-start.14 = (bf16[1024,128]{1,0:T(8,128)(2,1)}, bf16[1024,128]{1,0:T(8,128)(2,1)S(1)}, u32[]{:S(2)}) copy-start(bf16[1024,128]{1,0:T(8,128)(2,1)S(1)} %collective-permute-done.refs_18_) | copy-start | bytes 786436
  29.5 10.0 %collective-permute-start.2 = (bf16[1024,128]{1,0:T(8,128)(2,1)S(1)}, bf16[1024,128]{1,0:T(8,128)(2,1)}, u32[]{:S(2)}, u32[]{:S(2)}) collective-permute-start(bf16[1024,128]{1,0:T(8,128)(2,1)S(1)} %collective-permute-done.1.refs_3_), channel_id=1, source_target_pairs={{0,1},{1,0},{2,3},{3,2},{4,5},{5,4},{6,7},{7,6},{8,9},{9,8},{10,11... | collective-permute-start | bytes 786440 | tf_op jit(solution)/shard_map/ppermute | solution.py:202
  31.2 0.7 copy-start.6
  32.5 5.7 %copy-start.8 = (bf16[1024,128]{1,0:T(8,128)(2,1)}, bf16[1024,128]{1,0:T(8,128)(2,1)S(1)}, u32[]{:S(2)}) copy-start(bf16[1024,128]{1,0:T(8,128)(2,1)S(1)} %collective-permute-done.8.refs_7_) | copy-start | bytes 786436
  34.6 3.6 %copy-start.15 = (bf16[1024,128]{1,0:T(8,128)(2,1)}, bf16[1024,128]{1,0:T(8,128)(2,1)S(1)}, u32[]{:S(2)}) copy-start(bf16[1024,128]{1,0:T(8,128)(2,1)S(1)} %collective-permute-done.6.refs_10_) | copy-start | bytes 786436
  38.1 0.7 copy-start.10
  38.8 0.7 copy-start.12
  41.7 6.0 %copy-start.13 = (bf16[1024,128]{1,0:T(8,128)(2,1)S(1)}, bf16[1024,128]{1,0:T(8,128)(2,1)}, u32[]{:S(2)}) copy-start(bf16[1024,128]{1,0:T(8,128)(2,1)} %copy-done.12) | copy-start | bytes 786436
  41.7 9.8 %copy-start.16 = (bf16[1024,128]{1,0:T(8,128)(2,1)S(1)}, bf16[1024,128]{1,0:T(8,128)(2,1)}, u32[]{:S(2)}) copy-start(bf16[1024,128]{1,0:T(8,128)(2,1)} %copy-done.15) | copy-start | bytes 786436
  41.7 22.4 %copy-start.5 = (bf16[1024,128]{1,0:T(8,128)(2,1)S(1)}, bf16[1024,128]{1,0:T(8,128)(2,1)}, u32[]{:S(2)}) copy-start(bf16[1024,128]{1,0:T(8,128)(2,1)} %copy-done.4) | copy-start | bytes 786436
  41.7 24.0 %copy-start.11 = (bf16[1024,128]{1,0:T(8,128)(2,1)S(1)}, bf16[1024,128]{1,0:T(8,128)(2,1)}, u32[]{:S(2)}) copy-start(bf16[1024,128]{1,0:T(8,128)(2,1)} %copy-done.10) | copy-start | bytes 786436
  41.7 24.1 %copy-start.3 = (bf16[1024,128]{1,0:T(8,128)(2,1)S(1)}, bf16[1024,128]{1,0:T(8,128)(2,1)}, u32[]{:S(2)}) copy-start(bf16[1024,128]{1,0:T(8,128)(2,1)} %copy-done.2) | copy-start | bytes 786436
  41.7 25.4 %copy-start.9 = (bf16[1024,128]{1,0:T(8,128)(2,1)S(1)}, bf16[1024,128]{1,0:T(8,128)(2,1)}, u32[]{:S(2)}) copy-start(bf16[1024,128]{1,0:T(8,128)(2,1)} %copy-done.8) | copy-start | bytes 786436
  41.7 44.4 %copy-start.7 = (bf16[1024,128]{1,0:T(8,128)(2,1)S(1)}, bf16[1024,128]{1,0:T(8,128)(2,1)}, u32[]{:S(2)}) copy-start(bf16[1024,128]{1,0:T(8,128)(2,1)} %copy-done.6) | copy-start | bytes 786436
  41.7 44.4 %all-to-all-start.1 = ((bf16[16,512,128]{2,1,0:T(8,128)(2,1)}), bf16[16,512,128]{2,1,0:T(8,128)(2,1)}, u32[]{:S(2)}, u32[]{:S(2)}) async-start(bf16[16,512,128]{2,1,0:T(8,128)(2,1)} %bitcast.13), calls=%async_computation.1 | async-start | bytes 4194304 | tf_op jit(solution)/shard_map/all_to_all | solution.py:215
  47.7 10.3 %collective-permute-start.9 = (bf16[1024,128]{1,0:T(8,128)(2,1)S(1)}, bf16[1024,128]{1,0:T(8,128)(2,1)S(1)}, u32[]{:S(2)}, u32[]{:S(2)}) collective-permute-start(bf16[1024,128]{1,0:T(8,128)(2,1)S(1)} %copy-done.13), channel_id=1, source_target_pairs={{0,18},{2,16},{16,2},{18,0},{1,19},{3,17},{17,3},{19,1},{4,22},{6,... | collective-permute-start | bytes 786440 | tf_op jit(solution)/shard_map/ppermute | solution.py:206
  51.5 10.9 %collective-permute-start.12 = (bf16[1024,128]{1,0:T(8,128)(2,1)S(1)}, bf16[1024,128]{1,0:T(8,128)(2,1)S(1)}, u32[]{:S(2)}, u32[]{:S(2)}) collective-permute-start(bf16[1024,128]{1,0:T(8,128)(2,1)S(1)} %copy-done.16), channel_id=1, source_target_pairs={{0,32},{32,64},{64,96},{96,128},{128,160},{160,192},{192,224},{224... | collective-permute-start | bytes 786440 | tf_op jit(solution)/shard_map/ppermute | solution.py:211
  51.8 10.6 %collective-permute-start.11 = (bf16[1024,128]{1,0:T(8,128)(2,1)S(1)}, bf16[1024,128]{1,0:T(8,128)(2,1)S(1)}, u32[]{:S(2)}, u32[]{:S(2)}) collective-permute-start(bf16[1024,128]{1,0:T(8,128)(2,1)S(1)} %copy-done.13), channel_id=1, source_target_pairs={{0,224},{32,0},{64,32},{96,64},{128,96},{160,128},{192,160},{224,1... | collective-permute-start | bytes 786440 | tf_op jit(solution)/shard_map/ppermute | solution.py:211
  55.7 8.4 %collective-permute-start.10 = (bf16[1024,128]{1,0:T(8,128)(2,1)S(1)}, bf16[1024,128]{1,0:T(8,128)(2,1)S(1)}, u32[]{:S(2)}, u32[]{:S(2)}) collective-permute-start(bf16[1024,128]{1,0:T(8,128)(2,1)S(1)} %copy-done.16), channel_id=1, source_target_pairs={{0,18},{2,16},{16,2},{18,0},{1,19},{3,17},{17,3},{19,1},{4,22},{6,... | collective-permute-start | bytes 786440 | tf_op jit(solution)/shard_map/ppermute | solution.py:206
  58.0 28.1 %copy-start.17 = (bf16[1024,128]{1,0:T(8,128)(2,1)}, bf16[1024,128]{1,0:T(8,128)(2,1)S(1)}, u32[]{:S(2)}) copy-start(bf16[1024,128]{1,0:T(8,128)(2,1)S(1)} %collective-permute-done.9.refs_9_) | copy-start | bytes 786436
  58.0 9.1 %collective-permute-start.13 = (bf16[1024,128]{1,0:T(8,128)(2,1)S(1)}, bf16[1024,128]{1,0:T(8,128)(2,1)}, u32[]{:S(2)}, u32[]{:S(2)}) collective-permute-start(bf16[1024,128]{1,0:T(8,128)(2,1)S(1)} %collective-permute-done.9.refs_9_), channel_id=1, source_target_pairs={{0,224},{32,0},{64,32},{96,64},{128,96},{160,128},{192,160},{224,1... | collective-permute-start | bytes 786440 | tf_op jit(solution)/shard_map/ppermute | solution.py:211
  62.4 23.7 %copy-start.18 = (bf16[1024,128]{1,0:T(8,128)(2,1)}, bf16[1024,128]{1,0:T(8,128)(2,1)S(1)}, u32[]{:S(2)}) copy-start(bf16[1024,128]{1,0:T(8,128)(2,1)S(1)} %collective-permute-done.12.refs_14_) | copy-start | bytes 786436
  62.4 7.9 %collective-permute-start.15 = (bf16[1024,128]{1,0:T(8,128)(2,1)S(1)}, bf16[1024,128]{1,0:T(8,128)(2,1)}, u32[]{:S(2)}, u32[]{:S(2)}) collective-permute-start(bf16[1024,128]{1,0:T(8,128)(2,1)S(1)} %collective-permute-done.12.refs_14_), channel_id=1, source_target_pairs={{0,32},{32,64},{64,96},{96,128},{128,160},{160,192},{192,224},{224... | collective-permute-start | bytes 786440 | tf_op jit(solution)/shard_map/ppermute | solution.py:211
  62.4 13.9 %copy-start.19 = (bf16[1024,128]{1,0:T(8,128)(2,1)}, bf16[1024,128]{1,0:T(8,128)(2,1)S(1)}, u32[]{:S(2)}) copy-start(bf16[1024,128]{1,0:T(8,128)(2,1)S(1)} %collective-permute-done.11.refs_12_) | copy-start | bytes 786436
  64.1 13.1 %copy-start.20 = (bf16[1024,128]{1,0:T(8,128)(2,1)}, bf16[1024,128]{1,0:T(8,128)(2,1)S(1)}, u32[]{:S(2)}) copy-start(bf16[1024,128]{1,0:T(8,128)(2,1)S(1)} %collective-permute-done.10.refs_11_) | copy-start | bytes 786436
  64.1 8.3 %collective-permute-start.17 = (bf16[1024,128]{1,0:T(8,128)(2,1)S(1)}, bf16[1024,128]{1,0:T(8,128)(2,1)S(1)}, u32[]{:S(2)}, u32[]{:S(2)}) collective-permute-start(bf16[1024,128]{1,0:T(8,128)(2,1)S(1)} %copy-done.5), channel_id=1, source_target_pairs={{0,1},{1,0},{2,3},{3,2},{4,5},{5,4},{6,7},{7,6},{8,9},{9,8},{10,11... | collective-permute-start | bytes 786440 | tf_op jit(solution)/shard_map/ppermute | solution.py:202
  65.7 6.9 %collective-permute-start.18 = (bf16[1024,128]{1,0:T(8,128)(2,1)S(1)}, bf16[1024,128]{1,0:T(8,128)(2,1)S(1)}, u32[]{:S(2)}, u32[]{:S(2)}) collective-permute-start(bf16[1024,128]{1,0:T(8,128)(2,1)S(1)} %copy-done.11), channel_id=1, source_target_pairs={{0,1},{1,0},{2,3},{3,2},{4,5},{5,4},{6,7},{7,6},{8,9},{9,8},{10,11... | collective-permute-start | bytes 786440 | tf_op jit(solution)/shard_map/ppermute | solution.py:202
  65.8 7.2 %collective-permute-start.19 = (bf16[1024,128]{1,0:T(8,128)(2,1)S(1)}, bf16[1024,128]{1,0:T(8,128)(2,1)S(1)}, u32[]{:S(2)}, u32[]{:S(2)}) collective-permute-start(bf16[1024,128]{1,0:T(8,128)(2,1)S(1)} %copy-done.3), channel_id=1, source_target_pairs={{0,1},{1,0},{2,3},{3,2},{4,5},{5,4},{6,7},{7,6},{8,9},{9,8},{10,11... | collective-permute-start | bytes 786440 | tf_op jit(solution)/shard_map/ppermute | solution.py:202
  67.1 6.0 %collective-permute-start.20 = (bf16[1024,128]{1,0:T(8,128)(2,1)S(1)}, bf16[1024,128]{1,0:T(8,128)(2,1)S(1)}, u32[]{:S(2)}, u32[]{:S(2)}) collective-permute-start(bf16[1024,128]{1,0:T(8,128)(2,1)S(1)} %copy-done.9), channel_id=1, source_target_pairs={{0,1},{1,0},{2,3},{3,2},{4,5},{5,4},{6,7},{7,6},{8,9},{9,8},{10,11... | collective-permute-start | bytes 786440 | tf_op jit(solution)/shard_map/ppermute | solution.py:202
  70.3 3.3 %collective-permute-start.21 = (bf16[1024,128]{1,0:T(8,128)(2,1)S(1)}, bf16[1024,128]{1,0:T(8,128)(2,1)S(1)}, u32[]{:S(2)}, u32[]{:S(2)}) collective-permute-start(bf16[1024,128]{1,0:T(8,128)(2,1)S(1)} %copy-done.13), channel_id=1, source_target_pairs={{0,1},{1,0},{2,3},{3,2},{4,5},{5,4},{6,7},{7,6},{8,9},{9,8},{10,11... | collective-permute-start | bytes 786440 | tf_op jit(solution)/shard_map/ppermute | solution.py:202
  72.4 10.0 %copy-start.21 = (bf16[1024,128]{1,0:T(8,128)(2,1)}, bf16[1024,128]{1,0:T(8,128)(2,1)S(1)}, u32[]{:S(2)}) copy-start(bf16[1024,128]{1,0:T(8,128)(2,1)S(1)} %collective-permute-done.17.refs_20_) | copy-start | bytes 786436
  72.4 1.5 %collective-permute-start.22 = (bf16[1024,128]{1,0:T(8,128)(2,1)S(1)}, bf16[1024,128]{1,0:T(8,128)(2,1)S(1)}, u32[]{:S(2)}, u32[]{:S(2)}) collective-permute-start(bf16[1024,128]{1,0:T(8,128)(2,1)S(1)} %collective-permute-done.9.refs_9_), channel_id=1, source_target_pairs={{0,1},{1,0},{2,3},{3,2},{4,5},{5,4},{6,7},{7,6},{8,9},{9,8},{10,11... | collective-permute-start | bytes 786440 | tf_op jit(solution)/shard_map/ppermute | solution.py:202
  72.5 11.1 %copy-start.22 = (bf16[1024,128]{1,0:T(8,128)(2,1)}, bf16[1024,128]{1,0:T(8,128)(2,1)S(1)}, u32[]{:S(2)}) copy-start(bf16[1024,128]{1,0:T(8,128)(2,1)S(1)} %collective-permute-done.18.refs_21_) | copy-start | bytes 786436
  72.5 3.8 %collective-permute-start.23 = (bf16[1024,128]{1,0:T(8,128)(2,1)S(1)}, bf16[1024,128]{1,0:T(8,128)(2,1)S(1)}, u32[]{:S(2)}, u32[]{:S(2)}) collective-permute-start(bf16[1024,128]{1,0:T(8,128)(2,1)S(1)} %copy-done.16), channel_id=1, source_target_pairs={{0,1},{1,0},{2,3},{3,2},{4,5},{5,4},{6,7},{7,6},{8,9},{9,8},{10,11... | collective-permute-start | bytes 786440 | tf_op jit(solution)/shard_map/ppermute | solution.py:202
  73.0 10.7 %copy-start.23 = (bf16[1024,128]{1,0:T(8,128)(2,1)}, bf16[1024,128]{1,0:T(8,128)(2,1)S(1)}, u32[]{:S(2)}) copy-start(bf16[1024,128]{1,0:T(8,128)(2,1)S(1)} %collective-permute-done.19.refs_22_) | copy-start | bytes 786436
  73.0 4.1 %collective-permute-start.24 = (bf16[1024,128]{1,0:T(8,128)(2,1)S(1)}, bf16[1024,128]{1,0:T(8,128)(2,1)S(1)}, u32[]{:S(2)}, u32[]{:S(2)}) collective-permute-start(bf16[1024,128]{1,0:T(8,128)(2,1)S(1)} %collective-permute-done.10.refs_11_), channel_id=1, source_target_pairs={{0,1},{1,0},{2,3},{3,2},{4,5},{5,4},{6,7},{7,6},{8,9},{9,8},{10,11... | collective-permute-start | bytes 786440 | tf_op jit(solution)/shard_map/ppermute | solution.py:202
  73.1 10.6 %copy-start.24 = (bf16[1024,128]{1,0:T(8,128)(2,1)}, bf16[1024,128]{1,0:T(8,128)(2,1)S(1)}, u32[]{:S(2)}) copy-start(bf16[1024,128]{1,0:T(8,128)(2,1)S(1)} %collective-permute-done.20.refs_23_) | copy-start | bytes 786436
  73.1 4.1 %collective-permute-start.25 = (bf16[1024,128]{1,0:T(8,128)(2,1)S(1)}, bf16[1024,128]{1,0:T(8,128)(2,1)S(1)}, u32[]{:S(2)}, u32[]{:S(2)}) collective-permute-start(bf16[1024,128]{1,0:T(8,128)(2,1)S(1)} %collective-permute-done.11.refs_12_), channel_id=1, source_target_pairs={{0,1},{1,0},{2,3},{3,2},{4,5},{5,4},{6,7},{7,6},{8,9},{9,8},{10,11... | collective-permute-start | bytes 786440 | tf_op jit(solution)/shard_map/ppermute | solution.py:202
  73.6 10.1 %copy-start.25 = (bf16[1024,128]{1,0:T(8,128)(2,1)}, bf16[1024,128]{1,0:T(8,128)(2,1)S(1)}, u32[]{:S(2)}) copy-start(bf16[1024,128]{1,0:T(8,128)(2,1)S(1)} %collective-permute-done.21.refs_24_) | copy-start | bytes 786436
  73.6 8.8 %collective-permute-start.14 = (bf16[1024,128]{1,0:T(8,128)(2,1)S(1)}, bf16[1024,128]{1,0:T(8,128)(2,1)}, u32[]{:S(2)}, u32[]{:S(2)}) collective-permute-start(bf16[1024,128]{1,0:T(8,128)(2,1)S(1)} %collective-permute-done.10.refs_11_), channel_id=1, source_target_pairs={{0,32},{32,64},{64,96},{96,128},{128,160},{160,192},{192,224},{224... | collective-permute-start | bytes 786440 | tf_op jit(solution)/shard_map/ppermute | solution.py:211
  74.0 9.7 %copy-start.26 = (bf16[1024,128]{1,0:T(8,128)(2,1)}, bf16[1024,128]{1,0:T(8,128)(2,1)S(1)}, u32[]{:S(2)}) copy-start(bf16[1024,128]{1,0:T(8,128)(2,1)S(1)} %collective-permute-done.22.refs_25_) | copy-start | bytes 786436
  74.0 9.7 %collective-permute-start.16 = (bf16[1024,128]{1,0:T(8,128)(2,1)}, bf16[1024,128]{1,0:T(8,128)(2,1)}, u32[]{:S(2)}, u32[]{:S(2)}) collective-permute-start(bf16[1024,128]{1,0:T(8,128)(2,1)} %collective-permute-done.15.refs_16_), channel_id=1, source_target_pairs={{0,18},{2,16},{16,2},{18,0},{1,19},{3,17},{17,3},{19,1},{4,22},{6,... | collective-permute-start | bytes 786440 | tf_op jit(solution)/shard_map/ppermute | solution.py:206
  76.3 7.3 %copy-start.27 = (bf16[1024,128]{1,0:T(8,128)(2,1)}, bf16[1024,128]{1,0:T(8,128)(2,1)S(1)}, u32[]{:S(2)}) copy-start(bf16[1024,128]{1,0:T(8,128)(2,1)S(1)} %collective-permute-done.23.refs_26_) | copy-start | bytes 786436
  76.3 8.3 %collective-permute-start.27 = (bf16[1024,128]{1,0:T(8,128)(2,1)S(1)}, bf16[1024,128]{1,0:T(8,128)(2,1)S(1)}, u32[]{:S(2)}, u32[]{:S(2)}) collective-permute-start(bf16[1024,128]{1,0:T(8,128)(2,1)S(1)} %collective-permute-done.12.refs_14_), channel_id=1, source_target_pairs={{0,1},{1,0},{2,3},{3,2},{4,5},{5,4},{6,7},{7,6},{8,9},{9,8},{10,11... | collective-permute-start | bytes 786440 | tf_op jit(solution)/shard_map/ppermute | solution.py:202
  77.1 6.6 %copy-start.28 = (bf16[1024,128]{1,0:T(8,128)(2,1)}, bf16[1024,128]{1,0:T(8,128)(2,1)S(1)}, u32[]{:S(2)}) copy-start(bf16[1024,128]{1,0:T(8,128)(2,1)S(1)} %collective-permute-done.24.refs_27_) | copy-start | bytes 786436
  77.1 7.6 %collective-permute-start.29 = (bf16[1024,128]{1,0:T(8,128)(2,1)}, bf16[1024,128]{1,0:T(8,128)(2,1)}, u32[]{:S(2)}, u32[]{:S(2)}) collective-permute-start(bf16[1024,128]{1,0:T(8,128)(2,1)} %collective-permute-done.15.refs_16_), channel_id=1, source_target_pairs={{0,1},{1,0},{2,3},{3,2},{4,5},{5,4},{6,7},{7,6},{8,9},{9,8},{10,11... | collective-permute-start | bytes 786440 | tf_op jit(solution)/shard_map/ppermute | solution.py:202
  77.2 6.5 %copy-start.29 = (bf16[1024,128]{1,0:T(8,128)(2,1)}, bf16[1024,128]{1,0:T(8,128)(2,1)S(1)}, u32[]{:S(2)}) copy-start(bf16[1024,128]{1,0:T(8,128)(2,1)S(1)} %collective-permute-done.25.refs_28_) | copy-start | bytes 786436
  77.2 7.5 %collective-permute-start.26 = (bf16[1024,128]{1,0:T(8,128)(2,1)}, bf16[1024,128]{1,0:T(8,128)(2,1)}, u32[]{:S(2)}, u32[]{:S(2)}) collective-permute-start(bf16[1024,128]{1,0:T(8,128)(2,1)} %collective-permute-done.13.refs_13_), channel_id=1, source_target_pairs={{0,1},{1,0},{2,3},{3,2},{4,5},{5,4},{6,7},{7,6},{8,9},{9,8},{10,11... | collective-permute-start | bytes 786440 | tf_op jit(solution)/shard_map/ppermute | solution.py:202
  82.4 2.7 %collective-permute-start.28 = (bf16[1024,128]{1,0:T(8,128)(2,1)}, bf16[1024,128]{1,0:T(8,128)(2,1)}, u32[]{:S(2)}, u32[]{:S(2)}) collective-permute-start(bf16[1024,128]{1,0:T(8,128)(2,1)} %collective-permute-done.14.refs_15_), channel_id=1, source_target_pairs={{0,1},{1,0},{2,3},{3,2},{4,5},{5,4},{6,7},{7,6},{8,9},{9,8},{10,11... | collective-permute-start | bytes 786440 | tf_op jit(solution)/shard_map/ppermute | solution.py:202
  83.7 2.4 %collective-permute-start.30 = (bf16[1024,128]{1,0:T(8,128)(2,1)}, bf16[1024,128]{1,0:T(8,128)(2,1)}, u32[]{:S(2)}, u32[]{:S(2)}) collective-permute-start(bf16[1024,128]{1,0:T(8,128)(2,1)} %collective-permute-done.16.refs_17_), channel_id=1, source_target_pairs={{0,1},{1,0},{2,3},{3,2},{4,5},{5,4},{6,7},{7,6},{8,9},{9,8},{10,11... | collective-permute-start | bytes 786440 | tf_op jit(solution)/shard_map/ppermute | solution.py:202
  84.7 1.4 %copy-start.30 = (bf16[1024,128]{1,0:T(8,128)(2,1)}, bf16[1024,128]{1,0:T(8,128)(2,1)S(1)}, u32[]{:S(2)}) copy-start(bf16[1024,128]{1,0:T(8,128)(2,1)S(1)} %collective-permute-done.27.refs_30_) | copy-start | bytes 786436

commit v5 on v4

--- a/solution.py
+++ b/solution.py
@@ -148,23 +148,32 @@
         moved = jnp.dot(order, some, preferred_element_type=jnp.float32).astype(jnp.bfloat16)
         at = (part % per_half) * LANES
         rows_of[part // per_half, :, at : at + GROUP * LANES] = moved
-    for first in range(0, steps, 2):
+    def product(first):
         both = (first, first + 1)
         total = None
+        for step in both:
+            for copy in (*root_arrivals(0, step), *root_arrivals(1, step), momentum_arrival(step)):
+                copy.wait()
         for side, which in ((0, core), (1, 1 - core)):
-            for step in both:
-                for copy in root_arrivals(side, step):
-                    copy.wait()
             root = jnp.concatenate([roots[side, step, k] for step in both for k in range(2)], axis=1)
             term = jnp.dot(rows_of[which], root, preferred_element_type=jnp.float32)
             total = term if total is None else total + term
-        for step in both:
-            momentum_arrival(step).wait()
+        return total
+
+    def put(first, total):
+        for step in (first, first + 1):
             for k, block_at in ((0, yh), (1, 1 - yh)):
                 lanes = pl.ds(pl.multiple_of(block_at * LANES, LANES), LANES)
                 at = ((step - first) * 2 + k) * LANES
                 out[step, :, lanes] = 0.9 * momentum[step, :, lanes] + total[:, at : at + LANES]
             departure(step).start()
+
+    total = product(0)
+    for first in range(2, steps, 2):
+        later = product(first)
+        put(first - 2, total)
+        total = later
+    put(steps - 2, total)
     for step in range(steps):
         departure(step).wait()
 

time: 97.5 us -> 96.8 us (level)
  no operation moved by 1% of the time
where the time goes in v5:
time: 96.8 us; the launch traced here: 96.6 us
  starting transfers between devices  54.9 us (57%)
  waiting for transfers between devices  21.7 us (22%)
  Pallas kernels  16.1 us (17%)
  local copies, waits for them, and re-layouts  3.48 us (4%)
    ppermute x9, starting transfers between devices, along_z(): return lax.ppermute(value, 'z', [(i, (i + step) % n) for i in range(n)])  17 us
    ppermute x16, starting transfers between devices, swap(): return lax.ppermute(value, axis, [(0, 1), (1, 0)])  13.1 us
    all_to_all x2, starting transfers between devices, exchange(): return lax.all_to_all(value, EXP, split_axis=0, concat_axis=0, tiled=True)  12.9 us
    ppermute x9, waiting for transfers between devices, along_z(): return lax.ppermute(value, 'z', [(i, (i + step) % n) for i in range(n)])  11.9 us
    ppermute x6, starting transfers between devices, across(): lax.ppermute(value, ('yh', 'yl'), [(place, 3 - place) for place in range(...  11.9 us
    pallas_call x1, Pallas kernels, finished(): pl.pallas_call(lambda *refs: finish_kernel(experts, hidden, pieces, *refs...  10.3 us
    ppermute x6, waiting for transfers between devices, across(): lax.ppermute(value, ('yh', 'yl'), [(place, 3 - place) for place in range(...  7.83 us
    pallas_call x1, Pallas kernels, sliced(): pl.pallas_call(lambda *refs: slice_kernel(experts, hidden, *refs), out_sh...  3.67 us
  transfers between devices with their start and end apart: 33, of which 13 were waited for; matrix products, arithmetic and copies ran while one was open for 0% of the time, Pallas kernels for 0%

profile of v5, /device:TPU:1, one launch (start us, length us, event | category | flops | bytes accessed | tf_op | source)
XLA Modules:
  0.0 96.6 jit_solution(5554993571206883305)
XLA Ops:
  0.0 1.0 %copy-done = bf16[128,2048]{1,0:T(8,128)(2,1)S(1)} copy-done((bf16[128,2048]{1,0:T(8,128)(2,1)S(1)}, bf16[128,2048]{1,0:T(8,128)(2,1)}, u32[]{:S(2)}) %copy-start) | copy-done | bytes 524312
  1.1 0.2 copy.6
  1.2 3.7 %slice_columns.1 = bf16[16,512,128]{2,1,0:T(8,128)(2,1)} custom-call(bf16[512,2048]{1,0:T(8,128)(2,1)} %bitcast.23), custom_call_target="tpu_custom_call" | custom-call | flops 1073741824 | bytes 4194304 | tf_op jit(solution)/shard_map/slice_columns/pallas_call | solution.py:56
  4.9 0.0 copy-start.1
  4.9 7.0 %all-to-all-start = ((bf16[16,512,128]{2,1,0:T(8,128)(2,1)}), bf16[16,512,128]{2,1,0:T(8,128)(2,1)S(1)}, u32[]{:S(2)}, u32[]{:S(2)}) async-start(bf16[16,512,128]{2,1,0:T(8,128)(2,1)} %slice_columns.1), calls=%async_computation | async-start | bytes 4194304 | tf_op jit(solution)/shard_map/all_to_all | solution.py:224
  11.9 1.6 %collective-permute-start.5 = (bf16[1024,128]{1,0:T(8,128)(2,1)S(1)}, bf16[1024,128]{1,0:T(8,128)(2,1)S(1)}, u32[]{:S(2)}, u32[]{:S(2)}) collective-permute-start(bf16[1024,128]{1,0:T(8,128)(2,1)S(1)} %bitcast.17), channel_id=1, source_target_pairs={{0,32},{32,64},{64,96},{96,128},{128,160},{160,192},{192,224},{224... | collective-permute-start | bytes 786440 | tf_op jit(solution)/shard_map/ppermute | solution.py:220
  13.5 4.0 %collective-permute-start.3 = (bf16[1024,128]{1,0:T(8,128)(2,1)S(1)}, bf16[1024,128]{1,0:T(8,128)(2,1)S(1)}, u32[]{:S(2)}, u32[]{:S(2)}) collective-permute-start(bf16[1024,128]{1,0:T(8,128)(2,1)S(1)} %bitcast.18), channel_id=1, source_target_pairs={{0,224},{32,0},{64,32},{96,64},{128,96},{160,128},{192,160},{224,1... | collective-permute-start | bytes 786440 | tf_op jit(solution)/shard_map/ppermute | solution.py:220
  17.6 2.8 %collective-permute-start.1 = (bf16[1024,128]{1,0:T(8,128)(2,1)S(1)}, bf16[1024,128]{1,0:T(8,128)(2,1)S(1)}, u32[]{:S(2)}, u32[]{:S(2)}) collective-permute-start(bf16[1024,128]{1,0:T(8,128)(2,1)S(1)} %bitcast.19), channel_id=1, source_target_pairs={{0,18},{2,16},{16,2},{18,0},{1,19},{3,17},{17,3},{19,1},{4,22},{6,... | collective-permute-start | bytes 786440 | tf_op jit(solution)/shard_map/ppermute | solution.py:215
  20.4 0.9 collective-permute-start
  21.3 2.8 %collective-permute-done.5.refs_6_ = bf16[1024,128]{1,0:T(8,128)(2,1)S(1)} collective-permute-done((bf16[1024,128]{1,0:T(8,128)(2,1)S(1)}, bf16[1024,128]{1,0:T(8,128)(2,1)S(1)}, u32[]{:S(2)}, u32[]{:S(2)}) %collective-permute-start.5) | collective-permute-done | bytes 262176 | tf_op jit(solution)/shard_map/ppermute | solution.py:220
  24.1 2.6 %collective-permute-start.8 = (bf16[1024,128]{1,0:T(8,128)(2,1)S(1)}, bf16[1024,128]{1,0:T(8,128)(2,1)S(1)}, u32[]{:S(2)}, u32[]{:S(2)}) collective-permute-start(bf16[1024,128]{1,0:T(8,128)(2,1)S(1)} %collective-permute-done.5.refs_6_), channel_id=1, source_target_pairs={{0,18},{2,16},{16,2},{18,0},{1,19},{3,17},{17,3},{19,1},{4,22},{6,... | collective-permute-start | bytes 786440 | tf_op jit(solution)/shard_map/ppermute | solution.py:215
  26.7 0.0 collective-permute-start.6
  26.7 0.0 collective-permute-done.3.refs_4_
  26.7 0.2 collective-permute-start.7
  26.9 0.0 collective-permute-done.1.refs_3_
  26.9 2.6 %collective-permute-start.4 = (bf16[1024,128]{1,0:T(8,128)(2,1)S(1)}, bf16[1024,128]{1,0:T(8,128)(2,1)S(1)}, u32[]{:S(2)}, u32[]{:S(2)}) collective-permute-start(bf16[1024,128]{1,0:T(8,128)(2,1)S(1)} %collective-permute-done.3.refs_4_), channel_id=1, source_target_pairs={{0,224},{32,0},{64,32},{96,64},{128,96},{160,128},{192,160},{224,1... | collective-permute-start | bytes 786440 | tf_op jit(solution)/shard_map/ppermute | solution.py:220
  29.5 1.8 %collective-permute-start.2 = (bf16[1024,128]{1,0:T(8,128)(2,1)S(1)}, bf16[1024,128]{1,0:T(8,128)(2,1)}, u32[]{:S(2)}, u32[]{:S(2)}) collective-permute-start(bf16[1024,128]{1,0:T(8,128)(2,1)S(1)} %collective-permute-done.1.refs_3_), channel_id=1, source_target_pairs={{0,1},{1,0},{2,3},{3,2},{4,5},{5,4},{6,7},{7,6},{8,9},{9,8},{10,11... | collective-permute-start | bytes 786440 | tf_op jit(solution)/shard_map/ppermute | solution.py:211
  31.2 0.7 copy-done.6
  31.9 0.5 collective-permute-done.8.refs_7_
  32.5 2.1 %collective-permute-done.6.refs_10_ = bf16[1024,128]{1,0:T(8,128)(2,1)S(1)} collective-permute-done((bf16[1024,128]{1,0:T(8,128)(2,1)S(1)}, bf16[1024,128]{1,0:T(8,128)(2,1)S(1)}, u32[]{:S(2)}, u32[]{:S(2)}) %collective-permute-start.6) | collective-permute-done | bytes 262176 | tf_op jit(solution)/shard_map/ppermute | solution.py:220
  34.6 3.5 %collective-permute-done.7.refs_5_ = bf16[1024,128]{1,0:T(8,128)(2,1)S(1)} collective-permute-done((bf16[1024,128]{1,0:T(8,128)(2,1)S(1)}, bf16[1024,128]{1,0:T(8,128)(2,1)S(1)}, u32[]{:S(2)}, u32[]{:S(2)}) %collective-permute-start.7) | collective-permute-done | bytes 262176 | tf_op jit(solution)/shard_map/ppermute | solution.py:215
  38.1 0.0 collective-permute-done.4.refs_8_
  38.2 0.7 copy-done.10
  38.8 0.7 copy-done.12
  39.5 2.1 %mix_experts.1 = bf16[16,16,32,128]{3,2,1,0:T(8,128)(2,1)} custom-call(bf16[512,512]{1,0:T(8,128)(2,1)S(1)} %copy-done.1, bf16[16,16,32,128]{3,2,1,0:T(8,128)(2,1)S(1)} %bitcast.16), custom_call_target="tpu_custom_call" | custom-call | tf_op jit(solution)/shard_map/mix_experts/pallas_call | solution.py:98
  41.7 5.9 %all-to-all-start.1 = ((bf16[16,512,128]{2,1,0:T(8,128)(2,1)}), bf16[16,512,128]{2,1,0:T(8,128)(2,1)}, u32[]{:S(2)}, u32[]{:S(2)}) async-start(bf16[16,512,128]{2,1,0:T(8,128)(2,1)} %bitcast.13), calls=%async_computation.1 | async-start | bytes 4194304 | tf_op jit(solution)/shard_map/all_to_all | solution.py:224
  47.7 3.8 %collective-permute-start.9 = (bf16[1024,128]{1,0:T(8,128)(2,1)S(1)}, bf16[1024,128]{1,0:T(8,128)(2,1)S(1)}, u32[]{:S(2)}, u32[]{:S(2)}) collective-permute-start(bf16[1024,128]{1,0:T(8,128)(2,1)S(1)} %copy-done.13), channel_id=1, source_target_pairs={{0,18},{2,16},{16,2},{18,0},{1,19},{3,17},{17,3},{19,1},{4,22},{6,... | collective-permute-start | bytes 786440 | tf_op jit(solution)/shard_map/ppermute | solution.py:215
  51.5 0.3 collective-permute-start.12
  51.8 3.9 %collective-permute-start.11 = (bf16[1024,128]{1,0:T(8,128)(2,1)S(1)}, bf16[1024,128]{1,0:T(8,128)(2,1)S(1)}, u32[]{:S(2)}, u32[]{:S(2)}) collective-permute-start(bf16[1024,128]{1,0:T(8,128)(2,1)S(1)} %copy-done.13), channel_id=1, source_target_pairs={{0,224},{32,0},{64,32},{96,64},{128,96},{160,128},{192,160},{224,1... | collective-permute-start | bytes 786440 | tf_op jit(solution)/shard_map/ppermute | solution.py:220
  55.7 0.2 collective-permute-start.10
  55.9 2.1 %collective-permute-done.9.refs_9_ = bf16[1024,128]{1,0:T(8,128)(2,1)S(1)} collective-permute-done((bf16[1024,128]{1,0:T(8,128)(2,1)S(1)}, bf16[1024,128]{1,0:T(8,128)(2,1)S(1)}, u32[]{:S(2)}, u32[]{:S(2)}) %collective-permute-start.9) | collective-permute-done | bytes 262176 | tf_op jit(solution)/shard_map/ppermute | solution.py:215
  58.0 4.4 %collective-permute-start.13 = (bf16[1024,128]{1,0:T(8,128)(2,1)S(1)}, bf16[1024,128]{1,0:T(8,128)(2,1)}, u32[]{:S(2)}, u32[]{:S(2)}) collective-permute-start(bf16[1024,128]{1,0:T(8,128)(2,1)S(1)} %collective-permute-done.9.refs_9_), channel_id=1, source_target_pairs={{0,224},{32,0},{64,32},{96,64},{128,96},{160,128},{192,160},{224,1... | collective-permute-start | bytes 786440 | tf_op jit(solution)/shard_map/ppermute | solution.py:220
  62.4 0.0 collective-permute-done.12.refs_14_
  62.4 0.0 collective-permute-start.15
  62.4 1.7 %collective-permute-done.10.refs_11_ = bf16[1024,128]{1,0:T(8,128)(2,1)S(1)} collective-permute-done((bf16[1024,128]{1,0:T(8,128)(2,1)S(1)}, bf16[1024,128]{1,0:T(8,128)(2,1)S(1)}, u32[]{:S(2)}, u32[]{:S(2)}) %collective-permute-start.10) | collective-permute-done | bytes 262176 | tf_op jit(solution)/shard_map/ppermute | solution.py:215
  64.1 1.6 %collective-permute-start.17 = (bf16[1024,128]{1,0:T(8,128)(2,1)S(1)}, bf16[1024,128]{1,0:T(8,128)(2,1)S(1)}, u32[]{:S(2)}, u32[]{:S(2)}) collective-permute-start(bf16[1024,128]{1,0:T(8,128)(2,1)S(1)} %copy-done.5), channel_id=1, source_target_pairs={{0,1},{1,0},{2,3},{3,2},{4,5},{5,4},{6,7},{7,6},{8,9},{9,8},{10,11... | collective-permute-start | bytes 786440 | tf_op jit(solution)/shard_map/ppermute | solution.py:211
  65.7 0.1 collective-permute-start.18
  65.8 0.4 collective-permute-start.19
  66.2 0.9 collective-permute-done.13.refs_13_
  67.1 1.8 %collective-permute-start.20 = (bf16[1024,128]{1,0:T(8,128)(2,1)S(1)}, bf16[1024,128]{1,0:T(8,128)(2,1)S(1)}, u32[]{:S(2)}, u32[]{:S(2)}) collective-permute-start(bf16[1024,128]{1,0:T(8,128)(2,1)S(1)} %copy-done.9), channel_id=1, source_target_pairs={{0,1},{1,0},{2,3},{3,2},{4,5},{5,4},{6,7},{7,6},{8,9},{9,8},{10,11... | collective-permute-start | bytes 786440 | tf_op jit(solution)/shard_map/ppermute | solution.py:211
  68.9 1.4 %collective-permute-done.15.refs_16_ = bf16[1024,128]{1,0:T(8,128)(2,1)} collective-permute-done((bf16[1024,128]{1,0:T(8,128)(2,1)S(1)}, bf16[1024,128]{1,0:T(8,128)(2,1)}, u32[]{:S(2)}, u32[]{:S(2)}) %collective-permute-start.15) | collective-permute-done | bytes 262176 | tf_op jit(solution)/shard_map/ppermute | solution.py:220
  70.3 2.1 %collective-permute-start.21 = (bf16[1024,128]{1,0:T(8,128)(2,1)S(1)}, bf16[1024,128]{1,0:T(8,128)(2,1)S(1)}, u32[]{:S(2)}, u32[]{:S(2)}) collective-permute-start(bf16[1024,128]{1,0:T(8,128)(2,1)S(1)} %copy-done.13), channel_id=1, source_target_pairs={{0,1},{1,0},{2,3},{3,2},{4,5},{5,4},{6,7},{7,6},{8,9},{9,8},{10,11... | collective-permute-start | bytes 786440 | tf_op jit(solution)/shard_map/ppermute | solution.py:211
  72.4 0.0 collective-permute-done.17.refs_20_
  72.4 0.1 collective-permute-start.22
  72.5 0.0 collective-permute-done.18.refs_21_
  72.5 0.4 collective-permute-start.23
  73.0 0.1 collective-permute-start.24
  73.1 0.0 collective-permute-done.20.refs_23_
  73.1 0.4 collective-permute-start.25
  73.5 0.1 collective-permute-done.21.refs_24_
  73.6 0.0 collective-permute-start.14
  73.6 0.4 collective-permute-done.22.refs_25_
  74.0 2.4 %collective-permute-start.16 = (bf16[1024,128]{1,0:T(8,128)(2,1)}, bf16[1024,128]{1,0:T(8,128)(2,1)}, u32[]{:S(2)}, u32[]{:S(2)}) collective-permute-start(bf16[1024,128]{1,0:T(8,128)(2,1)} %collective-permute-done.15.refs_16_), channel_id=1, source_target_pairs={{0,18},{2,16},{16,2},{18,0},{1,19},{3,17},{17,3},{19,1},{4,22},{6,... | collective-permute-start | bytes 786440 | tf_op jit(solution)/shard_map/ppermute | solution.py:215
  76.3 0.0 collective-permute-done.23.refs_26_
  76.3 0.7 collective-permute-start.27
  77.1 0.1 collective-permute-start.29
  77.2 0.5 collective-permute-start.26
  77.7 4.8 %collective-permute-done.14.refs_15_ = bf16[1024,128]{1,0:T(8,128)(2,1)} collective-permute-done((bf16[1024,128]{1,0:T(8,128)(2,1)S(1)}, bf16[1024,128]{1,0:T(8,128)(2,1)}, u32[]{:S(2)}, u32[]{:S(2)}) %collective-permute-start.14) | collective-permute-done | bytes 262176 | tf_op jit(solution)/shard_map/ppermute | solution.py:220
  82.4 1.2 %collective-permute-start.28 = (bf16[1024,128]{1,0:T(8,128)(2,1)}, bf16[1024,128]{1,0:T(8,128)(2,1)}, u32[]{:S(2)}, u32[]{:S(2)}) collective-permute-start(bf16[1024,128]{1,0:T(8,128)(2,1)} %collective-permute-done.14.refs_15_), channel_id=1, source_target_pairs={{0,1},{1,0},{2,3},{3,2},{4,5},{5,4},{6,7},{7,6},{8,9},{9,8},{10,11... | collective-permute-start | bytes 786440 | tf_op jit(solution)/shard_map/ppermute | solution.py:211
  83.7 0.9 collective-permute-start.30
  84.6 0.1 stack.43.refs_0_
  84.7 0.4 collective-permute-done.28.refs_31_
  85.1 0.9 collective-permute-done.30.refs_33_
  86.1 10.3 %model_rows.1 = f32[512,2048]{1,0:T(8,128)} custom-call(s32[10]{0:T(128)S(1)} %stack.43.refs_0_, bf16[16,512,128]{2,1,0:T(8,128)(2,1)} %all-to-all-done.1.refs_1_, bf16[1024,128]{1,0:T(8,128)(2,1)S(1)} %bitcast.21, bf16[1024,128]{1,0:T(8,128)(2,1)S(1)} %copy-done.7, bf16[1024,128]{1,0:T(8,128)(2,1)S(1)} %copy-done.5, bf16[1024,128]{1,0:T(8,128)(2,1)S(1)} %copy-done.11, ...), custom_call_target="tpu_custom_call" | custom-call | flops 4294967296 | bytes 18874368 | tf_op jit(solution)/shard_map/model_rows/pallas_call | solution.py:186
  (70 shorter events, 0.2 us)
Async XLA Ops:
  0.0 1.0 %copy-start = (bf16[128,2048]{1,0:T(8,128)(2,1)S(1)}, bf16[128,2048]{1,0:T(8,128)(2,1)}, u32[]{:S(2)}) copy-start(bf16[128,2048]{1,0:T(8,128)(2,1)} %param.6) | copy-start | bytes 1572868
  4.9 34.6 %copy-start.1 = (bf16[512,512]{1,0:T(8,128)(2,1)S(1)}, bf16[512,512]{1,0:T(8,128)(2,1)}, u32[]{:S(2)}) copy-start(bf16[512,512]{1,0:T(8,128)(2,1)} %root_ref.1) | copy-start | bytes 1572868
  4.9 34.6 %all-to-all-start = ((bf16[16,512,128]{2,1,0:T(8,128)(2,1)}), bf16[16,512,128]{2,1,0:T(8,128)(2,1)S(1)}, u32[]{:S(2)}, u32[]{:S(2)}) async-start(bf16[16,512,128]{2,1,0:T(8,128)(2,1)} %slice_columns.1), calls=%async_computation | async-start | bytes 4194304 | tf_op jit(solution)/shard_map/all_to_all | solution.py:224
  11.9 12.2 %collective-permute-start.5 = (bf16[1024,128]{1,0:T(8,128)(2,1)S(1)}, bf16[1024,128]{1,0:T(8,128)(2,1)S(1)}, u32[]{:S(2)}, u32[]{:S(2)}) collective-permute-start(bf16[1024,128]{1,0:T(8,128)(2,1)S(1)} %bitcast.17), channel_id=1, source_target_pairs={{0,32},{32,64},{64,96},{96,128},{128,160},{160,192},{192,224},{224... | collective-permute-start | bytes 786440 | tf_op jit(solution)/shard_map/ppermute | solution.py:220
  13.5 13.2 %collective-permute-start.3 = (bf16[1024,128]{1,0:T(8,128)(2,1)S(1)}, bf16[1024,128]{1,0:T(8,128)(2,1)S(1)}, u32[]{:S(2)}, u32[]{:S(2)}) collective-permute-start(bf16[1024,128]{1,0:T(8,128)(2,1)S(1)} %bitcast.18), channel_id=1, source_target_pairs={{0,224},{32,0},{64,32},{96,64},{128,96},{160,128},{192,160},{224,1... | collective-permute-start | bytes 786440 | tf_op jit(solution)/shard_map/ppermute | solution.py:220
  17.6 9.3 %collective-permute-start.1 = (bf16[1024,128]{1,0:T(8,128)(2,1)S(1)}, bf16[1024,128]{1,0:T(8,128)(2,1)S(1)}, u32[]{:S(2)}, u32[]{:S(2)}) collective-permute-start(bf16[1024,128]{1,0:T(8,128)(2,1)S(1)} %bitcast.19), channel_id=1, source_target_pairs={{0,18},{2,16},{16,2},{18,0},{1,19},{3,17},{17,3},{19,1},{4,22},{6,... | collective-permute-start | bytes 786440 | tf_op jit(solution)/shard_map/ppermute | solution.py:215
  20.4 9.1 %collective-permute-start = (bf16[1024,128]{1,0:T(8,128)(2,1)S(1)}, bf16[1024,128]{1,0:T(8,128)(2,1)S(1)}, u32[]{:S(2)}, u32[]{:S(2)}) collective-permute-start(bf16[1024,128]{1,0:T(8,128)(2,1)S(1)} %bitcast.20), channel_id=1, source_target_pairs={{0,1},{1,0},{2,3},{3,2},{4,5},{5,4},{6,7},{7,6},{8,9},{9,8},{10,11... | collective-permute-start | bytes 786440 | tf_op jit(solution)/shard_map/ppermute | solution.py:211
  24.1 14.0 %copy-start.2 = (bf16[1024,128]{1,0:T(8,128)(2,1)}, bf16[1024,128]{1,0:T(8,128)(2,1)S(1)}, u32[]{:S(2)}) copy-start(bf16[1024,128]{1,0:T(8,128)(2,1)S(1)} %collective-permute-done.5.refs_6_) | copy-start | bytes 786436
  24.1 8.4 %collective-permute-start.8 = (bf16[1024,128]{1,0:T(8,128)(2,1)S(1)}, bf16[1024,128]{1,0:T(8,128)(2,1)S(1)}, u32[]{:S(2)}, u32[]{:S(2)}) collective-permute-start(bf16[1024,128]{1,0:T(8,128)(2,1)S(1)} %collective-permute-done.5.refs_6_), channel_id=1, source_target_pairs={{0,18},{2,16},{16,2},{18,0},{1,19},{3,17},{17,3},{19,1},{4,22},{6,... | collective-permute-start | bytes 786440 | tf_op jit(solution)/shard_map/ppermute | solution.py:215
  26.7 7.9 %collective-permute-start.6 = (bf16[1024,128]{1,0:T(8,128)(2,1)S(1)}, bf16[1024,128]{1,0:T(8,128)(2,1)S(1)}, u32[]{:S(2)}, u32[]{:S(2)}) collective-permute-start(bf16[1024,128]{1,0:T(8,128)(2,1)S(1)} %collective-permute-done.5.refs_6_), channel_id=1, source_target_pairs={{0,32},{32,64},{64,96},{96,128},{128,160},{160,192},{192,224},{224... | collective-permute-start | bytes 786440 | tf_op jit(solution)/shard_map/ppermute | solution.py:220
  26.7 11.4 %copy-start.4 = (bf16[1024,128]{1,0:T(8,128)(2,1)}, bf16[1024,128]{1,0:T(8,128)(2,1)S(1)}, u32[]{:S(2)}) copy-start(bf16[1024,128]{1,0:T(8,128)(2,1)S(1)} %collective-permute-done.3.refs_4_) | copy-start | bytes 786436
  26.7 11.4 %collective-permute-start.7 = (bf16[1024,128]{1,0:T(8,128)(2,1)S(1)}, bf16[1024,128]{1,0:T(8,128)(2,1)S(1)}, u32[]{:S(2)}, u32[]{:S(2)}) collective-permute-start(bf16[1024,128]{1,0:T(8,128)(2,1)S(1)} %collective-permute-done.3.refs_4_), channel_id=1, source_target_pairs={{0,18},{2,16},{16,2},{18,0},{1,19},{3,17},{17,3},{19,1},{4,22},{6,... | collective-permute-start | bytes 786440 | tf_op jit(solution)/shard_map/ppermute | solution.py:215
  26.9 11.2 %collective-permute-start.4 = (bf16[1024,128]{1,0:T(8,128)(2,1)S(1)}, bf16[1024,128]{1,0:T(8,128)(2,1)S(1)}, u32[]{:S(2)}, u32[]{:S(2)}) collective-permute-start(bf16[1024,128]{1,0:T(8,128)(2,1)S(1)} %collective-permute-done.3.refs_4_), channel_id=1, source_target_pairs={{0,224},{32,0},{64,32},{96,64},{128,96},{160,128},{192,160},{224,1... | collective-permute-start | bytes 786440 | tf_op jit(solution)/shard_map/ppermute | solution.py:220
  29.5 8.7 %copy-start.14 = (bf16[1024,128]{1,0:T(8,128)(2,1)}, bf16[1024,128]{1,0:T(8,128)(2,1)S(1)}, u32[]{:S(2)}) copy-start(bf16[1024,128]{1,0:T(8,128)(2,1)S(1)} %collective-permute-done.refs_18_) | copy-start | bytes 786436
  29.5 10.0 %collective-permute-start.2 = (bf16[1024,128]{1,0:T(8,128)(2,1)S(1)}, bf16[1024,128]{1,0:T(8,128)(2,1)}, u32[]{:S(2)}, u32[]{:S(2)}) collective-permute-start(bf16[1024,128]{1,0:T(8,128)(2,1)S(1)} %collective-permute-done.1.refs_3_), channel_id=1, source_target_pairs={{0,1},{1,0},{2,3},{3,2},{4,5},{5,4},{6,7},{7,6},{8,9},{9,8},{10,11... | collective-permute-start | bytes 786440 | tf_op jit(solution)/shard_map/ppermute | solution.py:211
  31.2 0.7 copy-start.6
  32.5 5.7 %copy-start.8 = (bf16[1024,128]{1,0:T(8,128)(2,1)}, bf16[1024,128]{1,0:T(8,128)(2,1)S(1)}, u32[]{:S(2)}) copy-start(bf16[1024,128]{1,0:T(8,128)(2,1)S(1)} %collective-permute-done.8.refs_7_) | copy-start | bytes 786436
  34.6 3.6 %copy-start.15 = (bf16[1024,128]{1,0:T(8,128)(2,1)}, bf16[1024,128]{1,0:T(8,128)(2,1)S(1)}, u32[]{:S(2)}) copy-start(bf16[1024,128]{1,0:T(8,128)(2,1)S(1)} %collective-permute-done.6.refs_10_) | copy-start | bytes 786436
  38.1 0.7 copy-start.10
  38.8 0.7 copy-start.12
  41.7 6.0 %copy-start.13 = (bf16[1024,128]{1,0:T(8,128)(2,1)S(1)}, bf16[1024,128]{1,0:T(8,128)(2,1)}, u32[]{:S(2)}) copy-start(bf16[1024,128]{1,0:T(8,128)(2,1)} %copy-done.12) | copy-start | bytes 786436
  41.7 9.8 %copy-start.16 = (bf16[1024,128]{1,0:T(8,128)(2,1)S(1)}, bf16[1024,128]{1,0:T(8,128)(2,1)}, u32[]{:S(2)}) copy-start(bf16[1024,128]{1,0:T(8,128)(2,1)} %copy-done.15) | copy-start | bytes 786436
  41.7 22.4 %copy-start.5 = (bf16[1024,128]{1,0:T(8,128)(2,1)S(1)}, bf16[1024,128]{1,0:T(8,128)(2,1)}, u32[]{:S(2)}) copy-start(bf16[1024,128]{1,0:T(8,128)(2,1)} %copy-done.4) | copy-start | bytes 786436
  41.7 24.0 %copy-start.11 = (bf16[1024,128]{1,0:T(8,128)(2,1)S(1)}, bf16[1024,128]{1,0:T(8,128)(2,1)}, u32[]{:S(2)}) copy-start(bf16[1024,128]{1,0:T(8,128)(2,1)} %copy-done.10) | copy-start | bytes 786436
  41.7 24.1 %copy-start.3 = (bf16[1024,128]{1,0:T(8,128)(2,1)S(1)}, bf16[1024,128]{1,0:T(8,128)(2,1)}, u32[]{:S(2)}) copy-start(bf16[1024,128]{1,0:T(8,128)(2,1)} %copy-done.2) | copy-start | bytes 786436
  41.7 25.4 %copy-start.9 = (bf16[1024,128]{1,0:T(8,128)(2,1)S(1)}, bf16[1024,128]{1,0:T(8,128)(2,1)}, u32[]{:S(2)}) copy-start(bf16[1024,128]{1,0:T(8,128)(2,1)} %copy-done.8) | copy-start | bytes 786436
  41.7 44.4 %copy-start.7 = (bf16[1024,128]{1,0:T(8,128)(2,1)S(1)}, bf16[1024,128]{1,0:T(8,128)(2,1)}, u32[]{:S(2)}) copy-start(bf16[1024,128]{1,0:T(8,128)(2,1)} %copy-done.6) | copy-start | bytes 786436
  41.7 44.4 %all-to-all-start.1 = ((bf16[16,512,128]{2,1,0:T(8,128)(2,1)}), bf16[16,512,128]{2,1,0:T(8,128)(2,1)}, u32[]{:S(2)}, u32[]{:S(2)}) async-start(bf16[16,512,128]{2,1,0:T(8,128)(2,1)} %bitcast.13), calls=%async_computation.1 | async-start | bytes 4194304 | tf_op jit(solution)/shard_map/all_to_all | solution.py:224
  47.7 10.3 %collective-permute-start.9 = (bf16[1024,128]{1,0:T(8,128)(2,1)S(1)}, bf16[1024,128]{1,0:T(8,128)(2,1)S(1)}, u32[]{:S(2)}, u32[]{:S(2)}) collective-permute-start(bf16[1024,128]{1,0:T(8,128)(2,1)S(1)} %copy-done.13), channel_id=1, source_target_pairs={{0,18},{2,16},{16,2},{18,0},{1,19},{3,17},{17,3},{19,1},{4,22},{6,... | collective-permute-start | bytes 786440 | tf_op jit(solution)/shard_map/ppermute | solution.py:215
  51.5 10.9 %collective-permute-start.12 = (bf16[1024,128]{1,0:T(8,128)(2,1)S(1)}, bf16[1024,128]{1,0:T(8,128)(2,1)S(1)}, u32[]{:S(2)}, u32[]{:S(2)}) collective-permute-start(bf16[1024,128]{1,0:T(8,128)(2,1)S(1)} %copy-done.16), channel_id=1, source_target_pairs={{0,32},{32,64},{64,96},{96,128},{128,160},{160,192},{192,224},{224... | collective-permute-start | bytes 786440 | tf_op jit(solution)/shard_map/ppermute | solution.py:220
  51.8 10.6 %collective-permute-start.11 = (bf16[1024,128]{1,0:T(8,128)(2,1)S(1)}, bf16[1024,128]{1,0:T(8,128)(2,1)S(1)}, u32[]{:S(2)}, u32[]{:S(2)}) collective-permute-start(bf16[1024,128]{1,0:T(8,128)(2,1)S(1)} %copy-done.13), channel_id=1, source_target_pairs={{0,224},{32,0},{64,32},{96,64},{128,96},{160,128},{192,160},{224,1... | collective-permute-start | bytes 786440 | tf_op jit(solution)/shard_map/ppermute | solution.py:220
  55.7 8.4 %collective-permute-start.10 = (bf16[1024,128]{1,0:T(8,128)(2,1)S(1)}, bf16[1024,128]{1,0:T(8,128)(2,1)S(1)}, u32[]{:S(2)}, u32[]{:S(2)}) collective-permute-start(bf16[1024,128]{1,0:T(8,128)(2,1)S(1)} %copy-done.16), channel_id=1, source_target_pairs={{0,18},{2,16},{16,2},{18,0},{1,19},{3,17},{17,3},{19,1},{4,22},{6,... | collective-permute-start | bytes 786440 | tf_op jit(solution)/shard_map/ppermute | solution.py:215
  58.0 28.1 %copy-start.17 = (bf16[1024,128]{1,0:T(8,128)(2,1)}, bf16[1024,128]{1,0:T(8,128)(2,1)S(1)}, u32[]{:S(2)}) copy-start(bf16[1024,128]{1,0:T(8,128)(2,1)S(1)} %collective-permute-done.9.refs_9_) | copy-start | bytes 786436
  58.0 9.1 %collective-permute-start.13 = (bf16[1024,128]{1,0:T(8,128)(2,1)S(1)}, bf16[1024,128]{1,0:T(8,128)(2,1)}, u32[]{:S(2)}, u32[]{:S(2)}) collective-permute-start(bf16[1024,128]{1,0:T(8,128)(2,1)S(1)} %collective-permute-done.9.refs_9_), channel_id=1, source_target_pairs={{0,224},{32,0},{64,32},{96,64},{128,96},{160,128},{192,160},{224,1... | collective-permute-start | bytes 786440 | tf_op jit(solution)/shard_map/ppermute | solution.py:220
  62.4 23.7 %copy-start.18 = (bf16[1024,128]{1,0:T(8,128)(2,1)}, bf16[1024,128]{1,0:T(8,128)(2,1)S(1)}, u32[]{:S(2)}) copy-start(bf16[1024,128]{1,0:T(8,128)(2,1)S(1)} %collective-permute-done.12.refs_14_) | copy-start | bytes 786436
  62.4 7.9 %collective-permute-start.15 = (bf16[1024,128]{1,0:T(8,128)(2,1)S(1)}, bf16[1024,128]{1,0:T(8,128)(2,1)}, u32[]{:S(2)}, u32[]{:S(2)}) collective-permute-start(bf16[1024,128]{1,0:T(8,128)(2,1)S(1)} %collective-permute-done.12.refs_14_), channel_id=1, source_target_pairs={{0,32},{32,64},{64,96},{96,128},{128,160},{160,192},{192,224},{224... | collective-permute-start | bytes 786440 | tf_op jit(solution)/shard_map/ppermute | solution.py:220
  62.4 13.9 %copy-start.19 = (bf16[1024,128]{1,0:T(8,128)(2,1)}, bf16[1024,128]{1,0:T(8,128)(2,1)S(1)}, u32[]{:S(2)}) copy-start(bf16[1024,128]{1,0:T(8,128)(2,1)S(1)} %collective-permute-done.11.refs_12_) | copy-start | bytes 786436
  64.1 13.1 %copy-start.20 = (bf16[1024,128]{1,0:T(8,128)(2,1)}, bf16[1024,128]{1,0:T(8,128)(2,1)S(1)}, u32[]{:S(2)}) copy-start(bf16[1024,128]{1,0:T(8,128)(2,1)S(1)} %collective-permute-done.10.refs_11_) | copy-start | bytes 786436
  64.1 8.3 %collective-permute-start.17 = (bf16[1024,128]{1,0:T(8,128)(2,1)S(1)}, bf16[1024,128]{1,0:T(8,128)(2,1)S(1)}, u32[]{:S(2)}, u32[]{:S(2)}) collective-permute-start(bf16[1024,128]{1,0:T(8,128)(2,1)S(1)} %copy-done.5), channel_id=1, source_target_pairs={{0,1},{1,0},{2,3},{3,2},{4,5},{5,4},{6,7},{7,6},{8,9},{9,8},{10,11... | collective-permute-start | bytes 786440 | tf_op jit(solution)/shard_map/ppermute | solution.py:211
  65.7 6.9 %collective-permute-start.18 = (bf16[1024,128]{1,0:T(8,128)(2,1)S(1)}, bf16[1024,128]{1,0:T(8,128)(2,1)S(1)}, u32[]{:S(2)}, u32[]{:S(2)}) collective-permute-start(bf16[1024,128]{1,0:T(8,128)(2,1)S(1)} %copy-done.11), channel_id=1, source_target_pairs={{0,1},{1,0},{2,3},{3,2},{4,5},{5,4},{6,7},{7,6},{8,9},{9,8},{10,11... | collective-permute-start | bytes 786440 | tf_op jit(solution)/shard_map/ppermute | solution.py:211
  65.8 7.2 %collective-permute-start.19 = (bf16[1024,128]{1,0:T(8,128)(2,1)S(1)}, bf16[1024,128]{1,0:T(8,128)(2,1)S(1)}, u32[]{:S(2)}, u32[]{:S(2)}) collective-permute-start(bf16[1024,128]{1,0:T(8,128)(2,1)S(1)} %copy-done.3), channel_id=1, source_target_pairs={{0,1},{1,0},{2,3},{3,2},{4,5},{5,4},{6,7},{7,6},{8,9},{9,8},{10,11... | collective-permute-start | bytes 786440 | tf_op jit(solution)/shard_map/ppermute | solution.py:211
  67.1 6.0 %collective-permute-start.20 = (bf16[1024,128]{1,0:T(8,128)(2,1)S(1)}, bf16[1024,128]{1,0:T(8,128)(2,1)S(1)}, u32[]{:S(2)}, u32[]{:S(2)}) collective-permute-start(bf16[1024,128]{1,0:T(8,128)(2,1)S(1)} %copy-done.9), channel_id=1, source_target_pairs={{0,1},{1,0},{2,3},{3,2},{4,5},{5,4},{6,7},{7,6},{8,9},{9,8},{10,11... | collective-permute-start | bytes 786440 | tf_op jit(solution)/shard_map/ppermute | solution.py:211
  70.3 3.3 %collective-permute-start.21 = (bf16[1024,128]{1,0:T(8,128)(2,1)S(1)}, bf16[1024,128]{1,0:T(8,128)(2,1)S(1)}, u32[]{:S(2)}, u32[]{:S(2)}) collective-permute-start(bf16[1024,128]{1,0:T(8,128)(2,1)S(1)} %copy-done.13), channel_id=1, source_target_pairs={{0,1},{1,0},{2,3},{3,2},{4,5},{5,4},{6,7},{7,6},{8,9},{9,8},{10,11... | collective-permute-start | bytes 786440 | tf_op jit(solution)/shard_map/ppermute | solution.py:211
  72.4 10.0 %copy-start.21 = (bf16[1024,128]{1,0:T(8,128)(2,1)}, bf16[1024,128]{1,0:T(8,128)(2,1)S(1)}, u32[]{:S(2)}) copy-start(bf16[1024,128]{1,0:T(8,128)(2,1)S(1)} %collective-permute-done.17.refs_20_) | copy-start | bytes 786436
  72.4 1.5 %collective-permute-start.22 = (bf16[1024,128]{1,0:T(8,128)(2,1)S(1)}, bf16[1024,128]{1,0:T(8,128)(2,1)S(1)}, u32[]{:S(2)}, u32[]{:S(2)}) collective-permute-start(bf16[1024,128]{1,0:T(8,128)(2,1)S(1)} %collective-permute-done.9.refs_9_), channel_id=1, source_target_pairs={{0,1},{1,0},{2,3},{3,2},{4,5},{5,4},{6,7},{7,6},{8,9},{9,8},{10,11... | collective-permute-start | bytes 786440 | tf_op jit(solution)/shard_map/ppermute | solution.py:211
  72.5 11.1 %copy-start.22 = (bf16[1024,128]{1,0:T(8,128)(2,1)}, bf16[1024,128]{1,0:T(8,128)(2,1)S(1)}, u32[]{:S(2)}) copy-start(bf16[1024,128]{1,0:T(8,128)(2,1)S(1)} %collective-permute-done.18.refs_21_) | copy-start | bytes 786436
  72.5 3.8 %collective-permute-start.23 = (bf16[1024,128]{1,0:T(8,128)(2,1)S(1)}, bf16[1024,128]{1,0:T(8,128)(2,1)S(1)}, u32[]{:S(2)}, u32[]{:S(2)}) collective-permute-start(bf16[1024,128]{1,0:T(8,128)(2,1)S(1)} %copy-done.16), channel_id=1, source_target_pairs={{0,1},{1,0},{2,3},{3,2},{4,5},{5,4},{6,7},{7,6},{8,9},{9,8},{10,11... | collective-permute-start | bytes 786440 | tf_op jit(solution)/shard_map/ppermute | solution.py:211
  73.0 10.7 %copy-start.23 = (bf16[1024,128]{1,0:T(8,128)(2,1)}, bf16[1024,128]{1,0:T(8,128)(2,1)S(1)}, u32[]{:S(2)}) copy-start(bf16[1024,128]{1,0:T(8,128)(2,1)S(1)} %collective-permute-done.19.refs_22_) | copy-start | bytes 786436
  73.0 4.1 %collective-permute-start.24 = (bf16[1024,128]{1,0:T(8,128)(2,1)S(1)}, bf16[1024,128]{1,0:T(8,128)(2,1)S(1)}, u32[]{:S(2)}, u32[]{:S(2)}) collective-permute-start(bf16[1024,128]{1,0:T(8,128)(2,1)S(1)} %collective-permute-done.10.refs_11_), channel_id=1, source_target_pairs={{0,1},{1,0},{2,3},{3,2},{4,5},{5,4},{6,7},{7,6},{8,9},{9,8},{10,11... | collective-permute-start | bytes 786440 | tf_op jit(solution)/shard_map/ppermute | solution.py:211
  73.1 10.6 %copy-start.24 = (bf16[1024,128]{1,0:T(8,128)(2,1)}, bf16[1024,128]{1,0:T(8,128)(2,1)S(1)}, u32[]{:S(2)}) copy-start(bf16[1024,128]{1,0:T(8,128)(2,1)S(1)} %collective-permute-done.20.refs_23_) | copy-start | bytes 786436
  73.1 4.1 %collective-permute-start.25 = (bf16[1024,128]{1,0:T(8,128)(2,1)S(1)}, bf16[1024,128]{1,0:T(8,128)(2,1)S(1)}, u32[]{:S(2)}, u32[]{:S(2)}) collective-permute-start(bf16[1024,128]{1,0:T(8,128)(2,1)S(1)} %collective-permute-done.11.refs_12_), channel_id=1, source_target_pairs={{0,1},{1,0},{2,3},{3,2},{4,5},{5,4},{6,7},{7,6},{8,9},{9,8},{10,11... | collective-permute-start | bytes 786440 | tf_op jit(solution)/shard_map/ppermute | solution.py:211
  73.6 10.1 %copy-start.25 = (bf16[1024,128]{1,0:T(8,128)(2,1)}, bf16[1024,128]{1,0:T(8,128)(2,1)S(1)}, u32[]{:S(2)}) copy-start(bf16[1024,128]{1,0:T(8,128)(2,1)S(1)} %collective-permute-done.21.refs_24_) | copy-start | bytes 786436
  73.6 8.8 %collective-permute-start.14 = (bf16[1024,128]{1,0:T(8,128)(2,1)S(1)}, bf16[1024,128]{1,0:T(8,128)(2,1)}, u32[]{:S(2)}, u32[]{:S(2)}) collective-permute-start(bf16[1024,128]{1,0:T(8,128)(2,1)S(1)} %collective-permute-done.10.refs_11_), channel_id=1, source_target_pairs={{0,32},{32,64},{64,96},{96,128},{128,160},{160,192},{192,224},{224... | collective-permute-start | bytes 786440 | tf_op jit(solution)/shard_map/ppermute | solution.py:220
  74.0 9.7 %copy-start.26 = (bf16[1024,128]{1,0:T(8,128)(2,1)}, bf16[1024,128]{1,0:T(8,128)(2,1)S(1)}, u32[]{:S(2)}) copy-start(bf16[1024,128]{1,0:T(8,128)(2,1)S(1)} %collective-permute-done.22.refs_25_) | copy-start | bytes 786436
  74.0 9.7 %collective-permute-start.16 = (bf16[1024,128]{1,0:T(8,128)(2,1)}, bf16[1024,128]{1,0:T(8,128)(2,1)}, u32[]{:S(2)}, u32[]{:S(2)}) collective-permute-start(bf16[1024,128]{1,0:T(8,128)(2,1)} %collective-permute-done.15.refs_16_), channel_id=1, source_target_pairs={{0,18},{2,16},{16,2},{18,0},{1,19},{3,17},{17,3},{19,1},{4,22},{6,... | collective-permute-start | bytes 786440 | tf_op jit(solution)/shard_map/ppermute | solution.py:215
  76.3 7.3 %copy-start.27 = (bf16[1024,128]{1,0:T(8,128)(2,1)}, bf16[1024,128]{1,0:T(8,128)(2,1)S(1)}, u32[]{:S(2)}) copy-start(bf16[1024,128]{1,0:T(8,128)(2,1)S(1)} %collective-permute-done.23.refs_26_) | copy-start | bytes 786436
  76.3 8.3 %collective-permute-start.27 = (bf16[1024,128]{1,0:T(8,128)(2,1)S(1)}, bf16[1024,128]{1,0:T(8,128)(2,1)S(1)}, u32[]{:S(2)}, u32[]{:S(2)}) collective-permute-start(bf16[1024,128]{1,0:T(8,128)(2,1)S(1)} %collective-permute-done.12.refs_14_), channel_id=1, source_target_pairs={{0,1},{1,0},{2,3},{3,2},{4,5},{5,4},{6,7},{7,6},{8,9},{9,8},{10,11... | collective-permute-start | bytes 786440 | tf_op jit(solution)/shard_map/ppermute | solution.py:211
  77.1 6.6 %copy-start.28 = (bf16[1024,128]{1,0:T(8,128)(2,1)}, bf16[1024,128]{1,0:T(8,128)(2,1)S(1)}, u32[]{:S(2)}) copy-start(bf16[1024,128]{1,0:T(8,128)(2,1)S(1)} %collective-permute-done.24.refs_27_) | copy-start | bytes 786436
  77.1 7.6 %collective-permute-start.29 = (bf16[1024,128]{1,0:T(8,128)(2,1)}, bf16[1024,128]{1,0:T(8,128)(2,1)}, u32[]{:S(2)}, u32[]{:S(2)}) collective-permute-start(bf16[1024,128]{1,0:T(8,128)(2,1)} %collective-permute-done.15.refs_16_), channel_id=1, source_target_pairs={{0,1},{1,0},{2,3},{3,2},{4,5},{5,4},{6,7},{7,6},{8,9},{9,8},{10,11... | collective-permute-start | bytes 786440 | tf_op jit(solution)/shard_map/ppermute | solution.py:211
  77.2 6.5 %copy-start.29 = (bf16[1024,128]{1,0:T(8,128)(2,1)}, bf16[1024,128]{1,0:T(8,128)(2,1)S(1)}, u32[]{:S(2)}) copy-start(bf16[1024,128]{1,0:T(8,128)(2,1)S(1)} %collective-permute-done.25.refs_28_) | copy-start | bytes 786436
  77.2 7.5 %collective-permute-start.26 = (bf16[1024,128]{1,0:T(8,128)(2,1)}, bf16[1024,128]{1,0:T(8,128)(2,1)}, u32[]{:S(2)}, u32[]{:S(2)}) collective-permute-start(bf16[1024,128]{1,0:T(8,128)(2,1)} %collective-permute-done.13.refs_13_), channel_id=1, source_target_pairs={{0,1},{1,0},{2,3},{3,2},{4,5},{5,4},{6,7},{7,6},{8,9},{9,8},{10,11... | collective-permute-start | bytes 786440 | tf_op jit(solution)/shard_map/ppermute | solution.py:211
  82.4 2.7 %collective-permute-start.28 = (bf16[1024,128]{1,0:T(8,128)(2,1)}, bf16[1024,128]{1,0:T(8,128)(2,1)}, u32[]{:S(2)}, u32[]{:S(2)}) collective-permute-start(bf16[1024,128]{1,0:T(8,128)(2,1)} %collective-permute-done.14.refs_15_), channel_id=1, source_target_pairs={{0,1},{1,0},{2,3},{3,2},{4,5},{5,4},{6,7},{7,6},{8,9},{9,8},{10,11... | collective-permute-start | bytes 786440 | tf_op jit(solution)/shard_map/ppermute | solution.py:211
  83.7 2.4 %collective-permute-start.30 = (bf16[1024,128]{1,0:T(8,128)(2,1)}, bf16[1024,128]{1,0:T(8,128)(2,1)}, u32[]{:S(2)}, u32[]{:S(2)}) collective-permute-start(bf16[1024,128]{1,0:T(8,128)(2,1)} %collective-permute-done.16.refs_17_), channel_id=1, source_target_pairs={{0,1},{1,0},{2,3},{3,2},{4,5},{5,4},{6,7},{7,6},{8,9},{9,8},{10,11... | collective-permute-start | bytes 786440 | tf_op jit(solution)/shard_map/ppermute | solution.py:211
  84.7 1.4 %copy-start.30 = (bf16[1024,128]{1,0:T(8,128)(2,1)}, bf16[1024,128]{1,0:T(8,128)(2,1)S(1)}, u32[]{:S(2)}) copy-start(bf16[1024,128]{1,0:T(8,128)(2,1)S(1)} %collective-permute-done.27.refs_30_) | copy-start | bytes 786436

commit v6 on v5

--- a/solution.py
+++ b/solution.py
@@ -249,8 +249,9 @@
     spread(near, 2)
     cross(1, -1)
     others = {0: [swap(near[0], "core"), swap(far[0], "core")]}
-    held, others, near[2], near[-2], far[1], far[-1] = lax.optimization_barrier(
-        (held, others, near[2], near[-2], far[1], far[-1])
+    side = [swap(near[place], "core") for place in (1, -1)]
+    held, others, side, near[2], near[-2], far[1], far[-1] = lax.optimization_barrier(
+        (held, others, side, near[2], near[-2], far[1], far[-1])
     )
 
     blended = mixed_experts(expert_root, held.reshape(PARTS, hidden, experts, LANES))
@@ -262,10 +263,13 @@
     early = [shares[place] for place in OFFSETS[1:5] for shares in (near, far)]
     near[4] = along_z(near[-3], 1)
     spread(far, 3)
-    cross(4)
+    far[4] = along_z(far[3], -1)
     early, near[3], near[-3] = lax.optimization_barrier((early, near[3], near[-3]))
     for index, place in enumerate(OFFSETS[1:5]):
-        others[place] = [swap(piece, "core") for piece in early[2 * index : 2 * index + 2]]
+        others[place] = [
+            side[index] if index < 2 else swap(early[2 * index], "core"),
+            swap(early[2 * index + 1], "core"),
+        ]
     for place in OFFSETS[5:]:
         others[place] = [swap(shares[place], "core") for shares in (near, far)]
     own = [shares[place] for place in OFFSETS for shares in (near, far)]

time: 96.8 us -> 96.1 us (level)
  waiting for transfers between devices: 21.7 us -> 17.6 us
  starting transfers between devices: 54.9 us -> 56.6 us
  local copies, waits for them, and re-layouts: 3.48 us -> 5.02 us
    ppermute x9 -> x10, starting transfers between devices: 17 us -> 19.6 us  [along_z(): return lax.ppermute(value, 'z', [(i, (i + step) % n) for i in range(n)])]
    ppermute x6 -> x5, waiting for transfers between devices: 7.83 us -> 5.49 us  [across(): lax.ppermute(value, ('yh', 'yl'), [(place, 3 - place) for place in range(...]
    ppermute x6 -> x5, starting transfers between devices: 11.9 us -> 9.66 us  [across(): lax.ppermute(value, ('yh', 'yl'), [(place, 3 - place) for place in range(...]
    ppermute x9 -> x10, waiting for transfers between devices: 11.9 us -> 10.3 us  [along_z(): return lax.ppermute(value, 'z', [(i, (i + step) % n) for i in range(n)])]
    unnamed x63 -> x61, local copies, waits for them, and re-layouts: 3.38 us -> 4.91 us
    ppermute x16, starting transfers between devices: 13.1 us -> 14.4 us  [swap(): return lax.ppermute(value, axis, [(0, 1), (1, 0)])]
  transfers between devices with their start and end apart: 33 -> 33, of which waited for: 13 -> 10; matrix products, arithmetic and copies ran while one was open for 0% -> 0% of each run, Pallas kernels for 0% -> 0%
where the time goes in v6:
time: 96.1 us; the launch traced here: 95.8 us
  starting transfers between devices  56.6 us (59%)
  waiting for transfers between devices  17.6 us (18%)
  Pallas kernels  16.1 us (17%)
  local copies, waits for them, and re-layouts  5.02 us (5%)
    ppermute x10, starting transfers between devices, along_z(): return lax.ppermute(value, 'z', [(i, (i + step) % n) for i in range(n)])  19.6 us
    ppermute x16, starting transfers between devices, swap(): return lax.ppermute(value, axis, [(0, 1), (1, 0)])  14.4 us
    all_to_all x2, starting transfers between devices, exchange(): return lax.all_to_all(value, EXP, split_axis=0, concat_axis=0, tiled=True)  12.9 us
    ppermute x10, waiting for transfers between devices, along_z(): return lax.ppermute(value, 'z', [(i, (i + step) % n) for i in range(n)])  10.3 us
    pallas_call x1, Pallas kernels, finished(): pl.pallas_call(lambda *refs: finish_kernel(experts, hidden, pieces, *refs...  10.3 us
    ppermute x5, starting transfers between devices, across(): lax.ppermute(value, ('yh', 'yl'), [(place, 3 - place) for place in range(...  9.66 us
    ppermute x5, waiting for transfers between devices, across(): lax.ppermute(value, ('yh', 'yl'), [(place, 3 - place) for place in range(...  5.49 us
    unnamed x61, local copies, waits for them, and re-layouts  4.91 us
  transfers between devices with their start and end apart: 33, of which 10 were waited for; matrix products, arithmetic and copies ran while one was open for 0% of the time, Pallas kernels for 0%

profile of v6, /device:TPU:1, one launch (start us, length us, event | category | flops | bytes accessed | tf_op | source)
XLA Modules:
  0.0 95.8 jit_solution(16894423573092280910)
XLA Ops:
  0.0 1.0 %copy-done = bf16[128,2048]{1,0:T(8,128)(2,1)S(1)} copy-done((bf16[128,2048]{1,0:T(8,128)(2,1)S(1)}, bf16[128,2048]{1,0:T(8,128)(2,1)}, u32[]{:S(2)}) %copy-start) | copy-done | bytes 524312
  1.1 0.2 copy.6
  1.2 3.7 %slice_columns.1 = bf16[16,512,128]{2,1,0:T(8,128)(2,1)} custom-call(bf16[512,2048]{1,0:T(8,128)(2,1)} %bitcast.23), custom_call_target="tpu_custom_call" | custom-call | flops 1073741824 | bytes 4194304 | tf_op jit(solution)/shard_map/slice_columns/pallas_call | solution.py:56
  4.9 0.0 copy-start.1
  4.9 7.0 %all-to-all-start = ((bf16[16,512,128]{2,1,0:T(8,128)(2,1)}), bf16[16,512,128]{2,1,0:T(8,128)(2,1)S(1)}, u32[]{:S(2)}, u32[]{:S(2)}) async-start(bf16[16,512,128]{2,1,0:T(8,128)(2,1)} %slice_columns.1), calls=%async_computation | async-start | bytes 4194304 | tf_op jit(solution)/shard_map/all_to_all | solution.py:224
  11.9 1.6 %collective-permute-start.5 = (bf16[1024,128]{1,0:T(8,128)(2,1)S(1)}, bf16[1024,128]{1,0:T(8,128)(2,1)S(1)}, u32[]{:S(2)}, u32[]{:S(2)}) collective-permute-start(bf16[1024,128]{1,0:T(8,128)(2,1)S(1)} %bitcast.17), channel_id=1, source_target_pairs={{0,32},{32,64},{64,96},{96,128},{128,160},{160,192},{192,224},{224... | collective-permute-start | bytes 786440 | tf_op jit(solution)/shard_map/ppermute | solution.py:220
  13.5 4.0 %collective-permute-start.3 = (bf16[1024,128]{1,0:T(8,128)(2,1)S(1)}, bf16[1024,128]{1,0:T(8,128)(2,1)S(1)}, u32[]{:S(2)}, u32[]{:S(2)}) collective-permute-start(bf16[1024,128]{1,0:T(8,128)(2,1)S(1)} %bitcast.18), channel_id=1, source_target_pairs={{0,224},{32,0},{64,32},{96,64},{128,96},{160,128},{192,160},{224,1... | collective-permute-start | bytes 786440 | tf_op jit(solution)/shard_map/ppermute | solution.py:220
  17.6 2.8 %collective-permute-start.1 = (bf16[1024,128]{1,0:T(8,128)(2,1)S(1)}, bf16[1024,128]{1,0:T(8,128)(2,1)S(1)}, u32[]{:S(2)}, u32[]{:S(2)}) collective-permute-start(bf16[1024,128]{1,0:T(8,128)(2,1)S(1)} %bitcast.19), channel_id=1, source_target_pairs={{0,18},{2,16},{16,2},{18,0},{1,19},{3,17},{17,3},{19,1},{4,22},{6,... | collective-permute-start | bytes 786440 | tf_op jit(solution)/shard_map/ppermute | solution.py:215
  20.4 0.9 collective-permute-start
  21.3 2.8 %collective-permute-done.5.refs_6_ = bf16[1024,128]{1,0:T(8,128)(2,1)S(1)} collective-permute-done((bf16[1024,128]{1,0:T(8,128)(2,1)S(1)}, bf16[1024,128]{1,0:T(8,128)(2,1)S(1)}, u32[]{:S(2)}, u32[]{:S(2)}) %collective-permute-start.5) | collective-permute-done | bytes 262176 | tf_op jit(solution)/shard_map/ppermute | solution.py:220
  24.1 2.6 %collective-permute-start.10 = (bf16[1024,128]{1,0:T(8,128)(2,1)S(1)}, bf16[1024,128]{1,0:T(8,128)(2,1)S(1)}, u32[]{:S(2)}, u32[]{:S(2)}) collective-permute-start(bf16[1024,128]{1,0:T(8,128)(2,1)S(1)} %collective-permute-done.5.refs_6_), channel_id=1, source_target_pairs={{0,18},{2,16},{16,2},{18,0},{1,19},{3,17},{17,3},{19,1},{4,22},{6,... | collective-permute-start | bytes 786440 | tf_op jit(solution)/shard_map/ppermute | solution.py:215
  26.7 0.0 collective-permute-start.8
  26.7 1.2 %collective-permute-start.6 = (bf16[1024,128]{1,0:T(8,128)(2,1)S(1)}, bf16[1024,128]{1,0:T(8,128)(2,1)S(1)}, u32[]{:S(2)}, u32[]{:S(2)}) collective-permute-start(bf16[1024,128]{1,0:T(8,128)(2,1)S(1)} %collective-permute-done.5.refs_6_), channel_id=1, source_target_pairs={{0,1},{1,0},{2,3},{3,2},{4,5},{5,4},{6,7},{7,6},{8,9},{9,8},{10,11... | collective-permute-start | bytes 786440 | tf_op jit(solution)/shard_map/ppermute | solution.py:211
  27.9 0.7 copy-done.2
  28.6 0.0 collective-permute-done.1.refs_3_
  28.6 0.3 collective-permute-start.9
  28.8 2.8 %collective-permute-start.7 = (bf16[1024,128]{1,0:T(8,128)(2,1)S(1)}, bf16[1024,128]{1,0:T(8,128)(2,1)S(1)}, u32[]{:S(2)}, u32[]{:S(2)}) collective-permute-start(bf16[1024,128]{1,0:T(8,128)(2,1)S(1)} %collective-permute-done.3.refs_4_), channel_id=1, source_target_pairs={{0,224},{32,0},{64,32},{96,64},{128,96},{160,128},{192,160},{224,1... | collective-permute-start | bytes 786440 | tf_op jit(solution)/shard_map/ppermute | solution.py:220
  31.6 0.9 collective-permute-done.10.refs_7_
  32.5 2.7 %collective-permute-start.4 = (bf16[1024,128]{1,0:T(8,128)(2,1)S(1)}, bf16[1024,128]{1,0:T(8,128)(2,1)S(1)}, u32[]{:S(2)}, u32[]{:S(2)}) collective-permute-start(bf16[1024,128]{1,0:T(8,128)(2,1)S(1)} %collective-permute-done.3.refs_4_), channel_id=1, source_target_pairs={{0,1},{1,0},{2,3},{3,2},{4,5},{5,4},{6,7},{7,6},{8,9},{9,8},{10,11... | collective-permute-start | bytes 786440 | tf_op jit(solution)/shard_map/ppermute | solution.py:211
  35.2 0.7 copy-done.4
  35.9 0.8 collective-permute-start.2
  36.6 0.7 copy-done.6
  37.3 0.0 collective-permute-done.6.refs_22_
  37.3 0.8 collective-permute-done.9.refs_5_
  38.1 0.7 copy-done.10
  38.8 0.1 copy-done.12
  38.9 0.7 copy-done.17
  39.6 0.0 collective-permute-done.2.refs_19_
  39.7 2.1 %mix_experts.1 = bf16[16,16,32,128]{3,2,1,0:T(8,128)(2,1)} custom-call(bf16[512,512]{1,0:T(8,128)(2,1)S(1)} %copy-done.1, bf16[16,16,32,128]{3,2,1,0:T(8,128)(2,1)S(1)} %bitcast.16), custom_call_target="tpu_custom_call" | custom-call | tf_op jit(solution)/shard_map/mix_experts/pallas_call | solution.py:98
  41.9 5.9 %all-to-all-start.1 = ((bf16[16,512,128]{2,1,0:T(8,128)(2,1)}), bf16[16,512,128]{2,1,0:T(8,128)(2,1)}, u32[]{:S(2)}, u32[]{:S(2)}) async-start(bf16[16,512,128]{2,1,0:T(8,128)(2,1)} %bitcast.13), calls=%async_computation.1 | async-start | bytes 4194304 | tf_op jit(solution)/shard_map/all_to_all | solution.py:224
  47.8 3.8 %collective-permute-start.11 = (bf16[1024,128]{1,0:T(8,128)(2,1)S(1)}, bf16[1024,128]{1,0:T(8,128)(2,1)S(1)}, u32[]{:S(2)}, u32[]{:S(2)}) collective-permute-start(bf16[1024,128]{1,0:T(8,128)(2,1)S(1)} %copy-done.13), channel_id=1, source_target_pairs={{0,18},{2,16},{16,2},{18,0},{1,19},{3,17},{17,3},{19,1},{4,22},{6,... | collective-permute-start | bytes 786440 | tf_op jit(solution)/shard_map/ppermute | solution.py:215
  51.6 0.2 collective-permute-start.14
  51.8 3.9 %collective-permute-start.13 = (bf16[1024,128]{1,0:T(8,128)(2,1)S(1)}, bf16[1024,128]{1,0:T(8,128)(2,1)S(1)}, u32[]{:S(2)}, u32[]{:S(2)}) collective-permute-start(bf16[1024,128]{1,0:T(8,128)(2,1)S(1)} %copy-done.13), channel_id=1, source_target_pairs={{0,224},{32,0},{64,32},{96,64},{128,96},{160,128},{192,160},{224,1... | collective-permute-start | bytes 786440 | tf_op jit(solution)/shard_map/ppermute | solution.py:220
  55.7 0.2 collective-permute-start.12
  55.9 2.2 %collective-permute-done.11.refs_9_ = bf16[1024,128]{1,0:T(8,128)(2,1)S(1)} collective-permute-done((bf16[1024,128]{1,0:T(8,128)(2,1)S(1)}, bf16[1024,128]{1,0:T(8,128)(2,1)S(1)}, u32[]{:S(2)}, u32[]{:S(2)}) %collective-permute-start.11) | collective-permute-done | bytes 262176 | tf_op jit(solution)/shard_map/ppermute | solution.py:215
  58.1 4.3 %collective-permute-start.15 = (bf16[1024,128]{1,0:T(8,128)(2,1)S(1)}, bf16[1024,128]{1,0:T(8,128)(2,1)}, u32[]{:S(2)}, u32[]{:S(2)}) collective-permute-start(bf16[1024,128]{1,0:T(8,128)(2,1)S(1)} %collective-permute-done.11.refs_9_), channel_id=1, source_target_pairs={{0,224},{32,0},{64,32},{96,64},{128,96},{160,128},{192,160},{224,1... | collective-permute-start | bytes 786440 | tf_op jit(solution)/shard_map/ppermute | solution.py:220
  62.4 0.0 collective-permute-done.14.refs_14_
  62.4 0.0 collective-permute-start.17
  62.5 1.7 %collective-permute-done.12.refs_11_ = bf16[1024,128]{1,0:T(8,128)(2,1)S(1)} collective-permute-done((bf16[1024,128]{1,0:T(8,128)(2,1)S(1)}, bf16[1024,128]{1,0:T(8,128)(2,1)S(1)}, u32[]{:S(2)}, u32[]{:S(2)}) %collective-permute-start.12) | collective-permute-done | bytes 262176 | tf_op jit(solution)/shard_map/ppermute | solution.py:215
  64.1 1.5 %collective-permute-start.19 = (bf16[1024,128]{1,0:T(8,128)(2,1)S(1)}, bf16[1024,128]{1,0:T(8,128)(2,1)S(1)}, u32[]{:S(2)}, u32[]{:S(2)}) collective-permute-start(bf16[1024,128]{1,0:T(8,128)(2,1)S(1)} %copy-done.11), channel_id=1, source_target_pairs={{0,1},{1,0},{2,3},{3,2},{4,5},{5,4},{6,7},{7,6},{8,9},{9,8},{10,11... | collective-permute-start | bytes 786440 | tf_op jit(solution)/shard_map/ppermute | solution.py:211
  65.7 0.1 collective-permute-start.20
  65.8 0.4 collective-permute-start.21
  66.2 1.0 %collective-permute-done.15.refs_13_ = bf16[1024,128]{1,0:T(8,128)(2,1)} collective-permute-done((bf16[1024,128]{1,0:T(8,128)(2,1)S(1)}, bf16[1024,128]{1,0:T(8,128)(2,1)}, u32[]{:S(2)}, u32[]{:S(2)}) %collective-permute-start.15) | collective-permute-done | bytes 262176 | tf_op jit(solution)/shard_map/ppermute | solution.py:220
  67.2 1.8 %collective-permute-start.22 = (bf16[1024,128]{1,0:T(8,128)(2,1)S(1)}, bf16[1024,128]{1,0:T(8,128)(2,1)S(1)}, u32[]{:S(2)}, u32[]{:S(2)}) collective-permute-start(bf16[1024,128]{1,0:T(8,128)(2,1)S(1)} %collective-permute-done.11.refs_9_), channel_id=1, source_target_pairs={{0,1},{1,0},{2,3},{3,2},{4,5},{5,4},{6,7},{7,6},{8,9},{9,8},{10,11... | collective-permute-start | bytes 786440 | tf_op jit(solution)/shard_map/ppermute | solution.py:211
  68.9 1.4 %collective-permute-done.17.refs_16_ = bf16[1024,128]{1,0:T(8,128)(2,1)} collective-permute-done((bf16[1024,128]{1,0:T(8,128)(2,1)S(1)}, bf16[1024,128]{1,0:T(8,128)(2,1)}, u32[]{:S(2)}, u32[]{:S(2)}) %collective-permute-start.17) | collective-permute-done | bytes 262176 | tf_op jit(solution)/shard_map/ppermute | solution.py:220
  70.4 2.1 %collective-permute-start.23 = (bf16[1024,128]{1,0:T(8,128)(2,1)S(1)}, bf16[1024,128]{1,0:T(8,128)(2,1)S(1)}, u32[]{:S(2)}, u32[]{:S(2)}) collective-permute-start(bf16[1024,128]{1,0:T(8,128)(2,1)S(1)} %copy-done.15), channel_id=1, source_target_pairs={{0,1},{1,0},{2,3},{3,2},{4,5},{5,4},{6,7},{7,6},{8,9},{9,8},{10,11... | collective-permute-start | bytes 786440 | tf_op jit(solution)/shard_map/ppermute | solution.py:211
  72.5 0.0 collective-permute-done.19.refs_21_
  72.5 0.1 collective-permute-start.24
  72.6 0.0 collective-permute-done.20.refs_23_
  72.6 0.4 collective-permute-start.25
  73.0 0.0 collective-permute-start.16
  73.0 0.0 collective-permute-done.22.refs_25_
  73.0 2.7 %collective-permute-start.18 = (bf16[1024,128]{1,0:T(8,128)(2,1)}, bf16[1024,128]{1,0:T(8,128)(2,1)}, u32[]{:S(2)}, u32[]{:S(2)}) collective-permute-start(bf16[1024,128]{1,0:T(8,128)(2,1)} %collective-permute-done.15.refs_13_), channel_id=1, source_target_pairs={{0,224},{32,0},{64,32},{96,64},{128,96},{160,128},{192,160},{224,1... | collective-permute-start | bytes 786440 | tf_op jit(solution)/shard_map/ppermute | solution.py:220
  75.7 0.0 collective-permute-done.23.refs_26_
  75.7 0.7 collective-permute-start.27
  76.4 0.1 collective-permute-start.26
  76.6 0.5 collective-permute-start.29
  77.0 5.1 %collective-permute-done.16.refs_15_ = bf16[1024,128]{1,0:T(8,128)(2,1)} collective-permute-done((bf16[1024,128]{1,0:T(8,128)(2,1)S(1)}, bf16[1024,128]{1,0:T(8,128)(2,1)}, u32[]{:S(2)}, u32[]{:S(2)}) %collective-permute-start.16) | collective-permute-done | bytes 262176 | tf_op jit(solution)/shard_map/ppermute | solution.py:220
  82.2 0.9 collective-permute-start.28
  83.1 0.3 collective-permute-start.30
  83.4 0.1 stack.43.refs_0_
  83.6 1.0 %collective-permute-done.28.refs_31_ = bf16[1024,128]{1,0:T(8,128)(2,1)} collective-permute-done((bf16[1024,128]{1,0:T(8,128)(2,1)}, bf16[1024,128]{1,0:T(8,128)(2,1)}, u32[]{:S(2)}, u32[]{:S(2)}) %collective-permute-start.28) | collective-permute-done | bytes 262176 | tf_op jit(solution)/shard_map/ppermute | solution.py:211
  84.6 0.7 collective-permute-done.30.refs_33_
  85.3 10.3 %model_rows.1 = f32[512,2048]{1,0:T(8,128)} custom-call(s32[10]{0:T(128)S(1)} %stack.43.refs_0_, bf16[16,512,128]{2,1,0:T(8,128)(2,1)} %all-to-all-done.1.refs_1_, bf16[1024,128]{1,0:T(8,128)(2,1)S(1)} %bitcast.21, bf16[1024,128]{1,0:T(8,128)(2,1)S(1)} %copy-done.7, bf16[1024,128]{1,0:T(8,128)(2,1)S(1)} %copy-done.5, bf16[1024,128]{1,0:T(8,128)(2,1)S(1)} %copy-done.11, ...), custom_call_target="tpu_custom_call" | custom-call | flops 4294967296 | bytes 18874368 | tf_op jit(solution)/shard_map/model_rows/pallas_call | solution.py:186
  (68 shorter events, 0.2 us)
Async XLA Ops:
  0.0 1.0 %copy-start = (bf16[128,2048]{1,0:T(8,128)(2,1)S(1)}, bf16[128,2048]{1,0:T(8,128)(2,1)}, u32[]{:S(2)}) copy-start(bf16[128,2048]{1,0:T(8,128)(2,1)} %param.6) | copy-start | bytes 1572868
  4.9 34.7 %copy-start.1 = (bf16[512,512]{1,0:T(8,128)(2,1)S(1)}, bf16[512,512]{1,0:T(8,128)(2,1)}, u32[]{:S(2)}) copy-start(bf16[512,512]{1,0:T(8,128)(2,1)} %root_ref.1) | copy-start | bytes 1572868
  4.9 34.7 %all-to-all-start = ((bf16[16,512,128]{2,1,0:T(8,128)(2,1)}), bf16[16,512,128]{2,1,0:T(8,128)(2,1)S(1)}, u32[]{:S(2)}, u32[]{:S(2)}) async-start(bf16[16,512,128]{2,1,0:T(8,128)(2,1)} %slice_columns.1), calls=%async_computation | async-start | bytes 4194304 | tf_op jit(solution)/shard_map/all_to_all | solution.py:224
  11.9 12.2 %collective-permute-start.5 = (bf16[1024,128]{1,0:T(8,128)(2,1)S(1)}, bf16[1024,128]{1,0:T(8,128)(2,1)S(1)}, u32[]{:S(2)}, u32[]{:S(2)}) collective-permute-start(bf16[1024,128]{1,0:T(8,128)(2,1)S(1)} %bitcast.17), channel_id=1, source_target_pairs={{0,32},{32,64},{64,96},{96,128},{128,160},{160,192},{192,224},{224... | collective-permute-start | bytes 786440 | tf_op jit(solution)/shard_map/ppermute | solution.py:220
  13.5 13.2 %collective-permute-start.3 = (bf16[1024,128]{1,0:T(8,128)(2,1)S(1)}, bf16[1024,128]{1,0:T(8,128)(2,1)S(1)}, u32[]{:S(2)}, u32[]{:S(2)}) collective-permute-start(bf16[1024,128]{1,0:T(8,128)(2,1)S(1)} %bitcast.18), channel_id=1, source_target_pairs={{0,224},{32,0},{64,32},{96,64},{128,96},{160,128},{192,160},{224,1... | collective-permute-start | bytes 786440 | tf_op jit(solution)/shard_map/ppermute | solution.py:220
  17.6 11.0 %collective-permute-start.1 = (bf16[1024,128]{1,0:T(8,128)(2,1)S(1)}, bf16[1024,128]{1,0:T(8,128)(2,1)S(1)}, u32[]{:S(2)}, u32[]{:S(2)}) collective-permute-start(bf16[1024,128]{1,0:T(8,128)(2,1)S(1)} %bitcast.19), channel_id=1, source_target_pairs={{0,18},{2,16},{16,2},{18,0},{1,19},{3,17},{17,3},{19,1},{4,22},{6,... | collective-permute-start | bytes 786440 | tf_op jit(solution)/shard_map/ppermute | solution.py:215
  20.4 8.4 %collective-permute-start = (bf16[1024,128]{1,0:T(8,128)(2,1)S(1)}, bf16[1024,128]{1,0:T(8,128)(2,1)}, u32[]{:S(2)}, u32[]{:S(2)}) collective-permute-start(bf16[1024,128]{1,0:T(8,128)(2,1)S(1)} %bitcast.20), channel_id=1, source_target_pairs={{0,1},{1,0},{2,3},{3,2},{4,5},{5,4},{6,7},{7,6},{8,9},{9,8},{10,11... | collective-permute-start | bytes 786440 | tf_op jit(solution)/shard_map/ppermute | solution.py:211
  24.1 8.4 %collective-permute-start.10 = (bf16[1024,128]{1,0:T(8,128)(2,1)S(1)}, bf16[1024,128]{1,0:T(8,128)(2,1)S(1)}, u32[]{:S(2)}, u32[]{:S(2)}) collective-permute-start(bf16[1024,128]{1,0:T(8,128)(2,1)S(1)} %collective-permute-done.5.refs_6_), channel_id=1, source_target_pairs={{0,18},{2,16},{16,2},{18,0},{1,19},{3,17},{17,3},{19,1},{4,22},{6,... | collective-permute-start | bytes 786440 | tf_op jit(solution)/shard_map/ppermute | solution.py:215
  26.7 9.2 %collective-permute-start.8 = (bf16[1024,128]{1,0:T(8,128)(2,1)S(1)}, bf16[1024,128]{1,0:T(8,128)(2,1)S(1)}, u32[]{:S(2)}, u32[]{:S(2)}) collective-permute-start(bf16[1024,128]{1,0:T(8,128)(2,1)S(1)} %collective-permute-done.5.refs_6_), channel_id=1, source_target_pairs={{0,32},{32,64},{64,96},{96,128},{128,160},{160,192},{192,224},{224... | collective-permute-start | bytes 786440 | tf_op jit(solution)/shard_map/ppermute | solution.py:220
  26.7 10.6 %collective-permute-start.6 = (bf16[1024,128]{1,0:T(8,128)(2,1)S(1)}, bf16[1024,128]{1,0:T(8,128)(2,1)S(1)}, u32[]{:S(2)}, u32[]{:S(2)}) collective-permute-start(bf16[1024,128]{1,0:T(8,128)(2,1)S(1)} %collective-permute-done.5.refs_6_), channel_id=1, source_target_pairs={{0,1},{1,0},{2,3},{3,2},{4,5},{5,4},{6,7},{7,6},{8,9},{9,8},{10,11... | collective-permute-start | bytes 786440 | tf_op jit(solution)/shard_map/ppermute | solution.py:211
  27.9 0.7 copy-start.2
  28.6 9.5 %collective-permute-start.9 = (bf16[1024,128]{1,0:T(8,128)(2,1)S(1)}, bf16[1024,128]{1,0:T(8,128)(2,1)S(1)}, u32[]{:S(2)}, u32[]{:S(2)}) collective-permute-start(bf16[1024,128]{1,0:T(8,128)(2,1)S(1)} %collective-permute-done.3.refs_4_), channel_id=1, source_target_pairs={{0,18},{2,16},{16,2},{18,0},{1,19},{3,17},{17,3},{19,1},{4,22},{6,... | collective-permute-start | bytes 786440 | tf_op jit(solution)/shard_map/ppermute | solution.py:215
  28.8 9.3 %collective-permute-start.7 = (bf16[1024,128]{1,0:T(8,128)(2,1)S(1)}, bf16[1024,128]{1,0:T(8,128)(2,1)S(1)}, u32[]{:S(2)}, u32[]{:S(2)}) collective-permute-start(bf16[1024,128]{1,0:T(8,128)(2,1)S(1)} %collective-permute-done.3.refs_4_), channel_id=1, source_target_pairs={{0,224},{32,0},{64,32},{96,64},{128,96},{160,128},{192,160},{224,1... | collective-permute-start | bytes 786440 | tf_op jit(solution)/shard_map/ppermute | solution.py:220
  32.5 5.6 %copy-start.8 = (bf16[1024,128]{1,0:T(8,128)(2,1)}, bf16[1024,128]{1,0:T(8,128)(2,1)S(1)}, u32[]{:S(2)}) copy-start(bf16[1024,128]{1,0:T(8,128)(2,1)S(1)} %collective-permute-done.10.refs_7_) | copy-start | bytes 786436
  32.5 5.6 %collective-permute-start.4 = (bf16[1024,128]{1,0:T(8,128)(2,1)S(1)}, bf16[1024,128]{1,0:T(8,128)(2,1)S(1)}, u32[]{:S(2)}, u32[]{:S(2)}) collective-permute-start(bf16[1024,128]{1,0:T(8,128)(2,1)S(1)} %collective-permute-done.3.refs_4_), channel_id=1, source_target_pairs={{0,1},{1,0},{2,3},{3,2},{4,5},{5,4},{6,7},{7,6},{8,9},{9,8},{10,11... | collective-permute-start | bytes 786440 | tf_op jit(solution)/shard_map/ppermute | solution.py:211
  35.2 0.7 copy-start.4
  35.9 2.3 %copy-start.14 = (bf16[1024,128]{1,0:T(8,128)(2,1)}, bf16[1024,128]{1,0:T(8,128)(2,1)S(1)}, u32[]{:S(2)}) copy-start(bf16[1024,128]{1,0:T(8,128)(2,1)S(1)} %collective-permute-done.8.refs_10_) | copy-start | bytes 786436
  35.9 3.8 %collective-permute-start.2 = (bf16[1024,128]{1,0:T(8,128)(2,1)S(1)}, bf16[1024,128]{1,0:T(8,128)(2,1)}, u32[]{:S(2)}, u32[]{:S(2)}) collective-permute-start(bf16[1024,128]{1,0:T(8,128)(2,1)S(1)} %collective-permute-done.1.refs_3_), channel_id=1, source_target_pairs={{0,1},{1,0},{2,3},{3,2},{4,5},{5,4},{6,7},{7,6},{8,9},{9,8},{10,11... | collective-permute-start | bytes 786440 | tf_op jit(solution)/shard_map/ppermute | solution.py:211
  36.6 0.7 copy-start.6
  37.3 0.8 copy-start.16
  38.1 0.7 copy-start.10
  38.1 0.8 copy-start.12
  38.9 0.7 copy-start.17
  41.8 6.0 %copy-start.13 = (bf16[1024,128]{1,0:T(8,128)(2,1)S(1)}, bf16[1024,128]{1,0:T(8,128)(2,1)}, u32[]{:S(2)}) copy-start(bf16[1024,128]{1,0:T(8,128)(2,1)} %copy-done.12) | copy-start | bytes 786436
  41.8 9.8 %copy-start.15 = (bf16[1024,128]{1,0:T(8,128)(2,1)S(1)}, bf16[1024,128]{1,0:T(8,128)(2,1)}, u32[]{:S(2)}) copy-start(bf16[1024,128]{1,0:T(8,128)(2,1)} %copy-done.14) | copy-start | bytes 786436
  41.8 22.3 %copy-start.11 = (bf16[1024,128]{1,0:T(8,128)(2,1)S(1)}, bf16[1024,128]{1,0:T(8,128)(2,1)}, u32[]{:S(2)}) copy-start(bf16[1024,128]{1,0:T(8,128)(2,1)} %copy-done.10) | copy-start | bytes 786436
  41.8 23.9 %copy-start.9 = (bf16[1024,128]{1,0:T(8,128)(2,1)S(1)}, bf16[1024,128]{1,0:T(8,128)(2,1)}, u32[]{:S(2)}) copy-start(bf16[1024,128]{1,0:T(8,128)(2,1)} %copy-done.8) | copy-start | bytes 786436
  41.8 43.5 %copy-start.3 = (bf16[1024,128]{1,0:T(8,128)(2,1)S(1)}, bf16[1024,128]{1,0:T(8,128)(2,1)}, u32[]{:S(2)}) copy-start(bf16[1024,128]{1,0:T(8,128)(2,1)} %copy-done.2) | copy-start | bytes 786436
  41.8 43.5 %copy-start.5 = (bf16[1024,128]{1,0:T(8,128)(2,1)S(1)}, bf16[1024,128]{1,0:T(8,128)(2,1)}, u32[]{:S(2)}) copy-start(bf16[1024,128]{1,0:T(8,128)(2,1)} %copy-done.4) | copy-start | bytes 786436
  41.9 43.5 %copy-start.7 = (bf16[1024,128]{1,0:T(8,128)(2,1)S(1)}, bf16[1024,128]{1,0:T(8,128)(2,1)}, u32[]{:S(2)}) copy-start(bf16[1024,128]{1,0:T(8,128)(2,1)} %copy-done.6) | copy-start | bytes 786436
  41.9 43.4 %all-to-all-start.1 = ((bf16[16,512,128]{2,1,0:T(8,128)(2,1)}), bf16[16,512,128]{2,1,0:T(8,128)(2,1)}, u32[]{:S(2)}, u32[]{:S(2)}) async-start(bf16[16,512,128]{2,1,0:T(8,128)(2,1)} %bitcast.13), calls=%async_computation.1 | async-start | bytes 4194304 | tf_op jit(solution)/shard_map/all_to_all | solution.py:224
  47.8 10.3 %collective-permute-start.11 = (bf16[1024,128]{1,0:T(8,128)(2,1)S(1)}, bf16[1024,128]{1,0:T(8,128)(2,1)S(1)}, u32[]{:S(2)}, u32[]{:S(2)}) collective-permute-start(bf16[1024,128]{1,0:T(8,128)(2,1)S(1)} %copy-done.13), channel_id=1, source_target_pairs={{0,18},{2,16},{16,2},{18,0},{1,19},{3,17},{17,3},{19,1},{4,22},{6,... | collective-permute-start | bytes 786440 | tf_op jit(solution)/shard_map/ppermute | solution.py:215
  51.6 10.8 %collective-permute-start.14 = (bf16[1024,128]{1,0:T(8,128)(2,1)S(1)}, bf16[1024,128]{1,0:T(8,128)(2,1)S(1)}, u32[]{:S(2)}, u32[]{:S(2)}) collective-permute-start(bf16[1024,128]{1,0:T(8,128)(2,1)S(1)} %copy-done.15), channel_id=1, source_target_pairs={{0,32},{32,64},{64,96},{96,128},{128,160},{160,192},{192,224},{224... | collective-permute-start | bytes 786440 | tf_op jit(solution)/shard_map/ppermute | solution.py:220
  51.8 10.6 %collective-permute-start.13 = (bf16[1024,128]{1,0:T(8,128)(2,1)S(1)}, bf16[1024,128]{1,0:T(8,128)(2,1)S(1)}, u32[]{:S(2)}, u32[]{:S(2)}) collective-permute-start(bf16[1024,128]{1,0:T(8,128)(2,1)S(1)} %copy-done.13), channel_id=1, source_target_pairs={{0,224},{32,0},{64,32},{96,64},{128,96},{160,128},{192,160},{224,1... | collective-permute-start | bytes 786440 | tf_op jit(solution)/shard_map/ppermute | solution.py:220
  55.7 8.4 %collective-permute-start.12 = (bf16[1024,128]{1,0:T(8,128)(2,1)S(1)}, bf16[1024,128]{1,0:T(8,128)(2,1)S(1)}, u32[]{:S(2)}, u32[]{:S(2)}) collective-permute-start(bf16[1024,128]{1,0:T(8,128)(2,1)S(1)} %copy-done.15), channel_id=1, source_target_pairs={{0,18},{2,16},{16,2},{18,0},{1,19},{3,17},{17,3},{19,1},{4,22},{6,... | collective-permute-start | bytes 786440 | tf_op jit(solution)/shard_map/ppermute | solution.py:215
  58.1 27.2 %copy-start.18 = (bf16[1024,128]{1,0:T(8,128)(2,1)}, bf16[1024,128]{1,0:T(8,128)(2,1)S(1)}, u32[]{:S(2)}) copy-start(bf16[1024,128]{1,0:T(8,128)(2,1)S(1)} %collective-permute-done.11.refs_9_) | copy-start | bytes 786436
  58.1 9.1 %collective-permute-start.15 = (bf16[1024,128]{1,0:T(8,128)(2,1)S(1)}, bf16[1024,128]{1,0:T(8,128)(2,1)}, u32[]{:S(2)}, u32[]{:S(2)}) collective-permute-start(bf16[1024,128]{1,0:T(8,128)(2,1)S(1)} %collective-permute-done.11.refs_9_), channel_id=1, source_target_pairs={{0,224},{32,0},{64,32},{96,64},{128,96},{160,128},{192,160},{224,1... | collective-permute-start | bytes 786440 | tf_op jit(solution)/shard_map/ppermute | solution.py:220
  62.4 22.9 %copy-start.19 = (bf16[1024,128]{1,0:T(8,128)(2,1)}, bf16[1024,128]{1,0:T(8,128)(2,1)S(1)}, u32[]{:S(2)}) copy-start(bf16[1024,128]{1,0:T(8,128)(2,1)S(1)} %collective-permute-done.14.refs_14_) | copy-start | bytes 786436
  62.4 8.0 %collective-permute-start.17 = (bf16[1024,128]{1,0:T(8,128)(2,1)S(1)}, bf16[1024,128]{1,0:T(8,128)(2,1)}, u32[]{:S(2)}, u32[]{:S(2)}) collective-permute-start(bf16[1024,128]{1,0:T(8,128)(2,1)S(1)} %collective-permute-done.14.refs_14_), channel_id=1, source_target_pairs={{0,32},{32,64},{64,96},{96,128},{128,160},{160,192},{192,224},{224... | collective-permute-start | bytes 786440 | tf_op jit(solution)/shard_map/ppermute | solution.py:220
  62.4 13.3 %copy-start.20 = (bf16[1024,128]{1,0:T(8,128)(2,1)}, bf16[1024,128]{1,0:T(8,128)(2,1)S(1)}, u32[]{:S(2)}) copy-start(bf16[1024,128]{1,0:T(8,128)(2,1)S(1)} %collective-permute-done.13.refs_12_) | copy-start | bytes 786436
  64.1 12.4 %copy-start.21 = (bf16[1024,128]{1,0:T(8,128)(2,1)}, bf16[1024,128]{1,0:T(8,128)(2,1)S(1)}, u32[]{:S(2)}) copy-start(bf16[1024,128]{1,0:T(8,128)(2,1)S(1)} %collective-permute-done.12.refs_11_) | copy-start | bytes 786436
  64.1 8.3 %collective-permute-start.19 = (bf16[1024,128]{1,0:T(8,128)(2,1)S(1)}, bf16[1024,128]{1,0:T(8,128)(2,1)S(1)}, u32[]{:S(2)}, u32[]{:S(2)}) collective-permute-start(bf16[1024,128]{1,0:T(8,128)(2,1)S(1)} %copy-done.11), channel_id=1, source_target_pairs={{0,1},{1,0},{2,3},{3,2},{4,5},{5,4},{6,7},{7,6},{8,9},{9,8},{10,11... | collective-permute-start | bytes 786440 | tf_op jit(solution)/shard_map/ppermute | solution.py:211
  65.7 6.9 %collective-permute-start.20 = (bf16[1024,128]{1,0:T(8,128)(2,1)S(1)}, bf16[1024,128]{1,0:T(8,128)(2,1)S(1)}, u32[]{:S(2)}, u32[]{:S(2)}) collective-permute-start(bf16[1024,128]{1,0:T(8,128)(2,1)S(1)} %copy-done.9), channel_id=1, source_target_pairs={{0,1},{1,0},{2,3},{3,2},{4,5},{5,4},{6,7},{7,6},{8,9},{9,8},{10,11... | collective-permute-start | bytes 786440 | tf_op jit(solution)/shard_map/ppermute | solution.py:211
  65.8 7.2 %collective-permute-start.21 = (bf16[1024,128]{1,0:T(8,128)(2,1)S(1)}, bf16[1024,128]{1,0:T(8,128)(2,1)S(1)}, u32[]{:S(2)}, u32[]{:S(2)}) collective-permute-start(bf16[1024,128]{1,0:T(8,128)(2,1)S(1)} %copy-done.13), channel_id=1, source_target_pairs={{0,1},{1,0},{2,3},{3,2},{4,5},{5,4},{6,7},{7,6},{8,9},{9,8},{10,11... | collective-permute-start | bytes 786440 | tf_op jit(solution)/shard_map/ppermute | solution.py:211
  67.2 5.8 %collective-permute-start.22 = (bf16[1024,128]{1,0:T(8,128)(2,1)S(1)}, bf16[1024,128]{1,0:T(8,128)(2,1)S(1)}, u32[]{:S(2)}, u32[]{:S(2)}) collective-permute-start(bf16[1024,128]{1,0:T(8,128)(2,1)S(1)} %collective-permute-done.11.refs_9_), channel_id=1, source_target_pairs={{0,1},{1,0},{2,3},{3,2},{4,5},{5,4},{6,7},{7,6},{8,9},{9,8},{10,11... | collective-permute-start | bytes 786440 | tf_op jit(solution)/shard_map/ppermute | solution.py:211
  70.4 5.3 %collective-permute-start.23 = (bf16[1024,128]{1,0:T(8,128)(2,1)S(1)}, bf16[1024,128]{1,0:T(8,128)(2,1)S(1)}, u32[]{:S(2)}, u32[]{:S(2)}) collective-permute-start(bf16[1024,128]{1,0:T(8,128)(2,1)S(1)} %copy-done.15), channel_id=1, source_target_pairs={{0,1},{1,0},{2,3},{3,2},{4,5},{5,4},{6,7},{7,6},{8,9},{9,8},{10,11... | collective-permute-start | bytes 786440 | tf_op jit(solution)/shard_map/ppermute | solution.py:211
  72.5 9.7 %copy-start.22 = (bf16[1024,128]{1,0:T(8,128)(2,1)}, bf16[1024,128]{1,0:T(8,128)(2,1)S(1)}, u32[]{:S(2)}) copy-start(bf16[1024,128]{1,0:T(8,128)(2,1)S(1)} %collective-permute-done.19.refs_21_) | copy-start | bytes 786436
  72.5 4.0 %collective-permute-start.24 = (bf16[1024,128]{1,0:T(8,128)(2,1)S(1)}, bf16[1024,128]{1,0:T(8,128)(2,1)S(1)}, u32[]{:S(2)}, u32[]{:S(2)}) collective-permute-start(bf16[1024,128]{1,0:T(8,128)(2,1)S(1)} %collective-permute-done.12.refs_11_), channel_id=1, source_target_pairs={{0,1},{1,0},{2,3},{3,2},{4,5},{5,4},{6,7},{7,6},{8,9},{9,8},{10,11... | collective-permute-start | bytes 786440 | tf_op jit(solution)/shard_map/ppermute | solution.py:211
  72.6 10.5 %copy-start.23 = (bf16[1024,128]{1,0:T(8,128)(2,1)}, bf16[1024,128]{1,0:T(8,128)(2,1)S(1)}, u32[]{:S(2)}) copy-start(bf16[1024,128]{1,0:T(8,128)(2,1)S(1)} %collective-permute-done.20.refs_23_) | copy-start | bytes 786436
  72.6 4.0 %collective-permute-start.25 = (bf16[1024,128]{1,0:T(8,128)(2,1)S(1)}, bf16[1024,128]{1,0:T(8,128)(2,1)S(1)}, u32[]{:S(2)}, u32[]{:S(2)}) collective-permute-start(bf16[1024,128]{1,0:T(8,128)(2,1)S(1)} %collective-permute-done.13.refs_12_), channel_id=1, source_target_pairs={{0,1},{1,0},{2,3},{3,2},{4,5},{5,4},{6,7},{7,6},{8,9},{9,8},{10,11... | collective-permute-start | bytes 786440 | tf_op jit(solution)/shard_map/ppermute | solution.py:211
  73.0 10.1 %copy-start.24 = (bf16[1024,128]{1,0:T(8,128)(2,1)}, bf16[1024,128]{1,0:T(8,128)(2,1)S(1)}, u32[]{:S(2)}) copy-start(bf16[1024,128]{1,0:T(8,128)(2,1)S(1)} %collective-permute-done.21.refs_24_) | copy-start | bytes 786436
  73.0 9.2 %collective-permute-start.16 = (bf16[1024,128]{1,0:T(8,128)(2,1)S(1)}, bf16[1024,128]{1,0:T(8,128)(2,1)}, u32[]{:S(2)}, u32[]{:S(2)}) collective-permute-start(bf16[1024,128]{1,0:T(8,128)(2,1)S(1)} %collective-permute-done.12.refs_11_), channel_id=1, source_target_pairs={{0,32},{32,64},{64,96},{96,128},{128,160},{160,192},{192,224},{224... | collective-permute-start | bytes 786440 | tf_op jit(solution)/shard_map/ppermute | solution.py:220
  73.0 10.1 %copy-start.25 = (bf16[1024,128]{1,0:T(8,128)(2,1)}, bf16[1024,128]{1,0:T(8,128)(2,1)S(1)}, u32[]{:S(2)}) copy-start(bf16[1024,128]{1,0:T(8,128)(2,1)S(1)} %collective-permute-done.22.refs_25_) | copy-start | bytes 786436
  73.0 10.0 %collective-permute-start.18 = (bf16[1024,128]{1,0:T(8,128)(2,1)}, bf16[1024,128]{1,0:T(8,128)(2,1)}, u32[]{:S(2)}, u32[]{:S(2)}) collective-permute-start(bf16[1024,128]{1,0:T(8,128)(2,1)} %collective-permute-done.15.refs_13_), channel_id=1, source_target_pairs={{0,224},{32,0},{64,32},{96,64},{128,96},{160,128},{192,160},{224,1... | collective-permute-start | bytes 786440 | tf_op jit(solution)/shard_map/ppermute | solution.py:220
  75.7 7.4 %copy-start.26 = (bf16[1024,128]{1,0:T(8,128)(2,1)}, bf16[1024,128]{1,0:T(8,128)(2,1)S(1)}, u32[]{:S(2)}) copy-start(bf16[1024,128]{1,0:T(8,128)(2,1)S(1)} %collective-permute-done.23.refs_26_) | copy-start | bytes 786436
  75.7 7.8 %collective-permute-start.27 = (bf16[1024,128]{1,0:T(8,128)(2,1)S(1)}, bf16[1024,128]{1,0:T(8,128)(2,1)S(1)}, u32[]{:S(2)}, u32[]{:S(2)}) collective-permute-start(bf16[1024,128]{1,0:T(8,128)(2,1)S(1)} %collective-permute-done.14.refs_14_), channel_id=1, source_target_pairs={{0,1},{1,0},{2,3},{3,2},{4,5},{5,4},{6,7},{7,6},{8,9},{9,8},{10,11... | collective-permute-start | bytes 786440 | tf_op jit(solution)/shard_map/ppermute | solution.py:211
  76.4 6.7 %copy-start.27 = (bf16[1024,128]{1,0:T(8,128)(2,1)}, bf16[1024,128]{1,0:T(8,128)(2,1)S(1)}, u32[]{:S(2)}) copy-start(bf16[1024,128]{1,0:T(8,128)(2,1)S(1)} %collective-permute-done.24.refs_27_) | copy-start | bytes 786436
  76.4 7.1 %collective-permute-start.26 = (bf16[1024,128]{1,0:T(8,128)(2,1)}, bf16[1024,128]{1,0:T(8,128)(2,1)}, u32[]{:S(2)}, u32[]{:S(2)}) collective-permute-start(bf16[1024,128]{1,0:T(8,128)(2,1)} %collective-permute-done.15.refs_13_), channel_id=1, source_target_pairs={{0,1},{1,0},{2,3},{3,2},{4,5},{5,4},{6,7},{7,6},{8,9},{9,8},{10,11... | collective-permute-start | bytes 786440 | tf_op jit(solution)/shard_map/ppermute | solution.py:211
  76.6 6.5 %copy-start.28 = (bf16[1024,128]{1,0:T(8,128)(2,1)}, bf16[1024,128]{1,0:T(8,128)(2,1)S(1)}, u32[]{:S(2)}) copy-start(bf16[1024,128]{1,0:T(8,128)(2,1)S(1)} %collective-permute-done.25.refs_28_) | copy-start | bytes 786436
  76.6 7.0 %collective-permute-start.29 = (bf16[1024,128]{1,0:T(8,128)(2,1)}, bf16[1024,128]{1,0:T(8,128)(2,1)}, u32[]{:S(2)}, u32[]{:S(2)}) collective-permute-start(bf16[1024,128]{1,0:T(8,128)(2,1)} %collective-permute-done.17.refs_16_), channel_id=1, source_target_pairs={{0,1},{1,0},{2,3},{3,2},{4,5},{5,4},{6,7},{7,6},{8,9},{9,8},{10,11... | collective-permute-start | bytes 786440 | tf_op jit(solution)/shard_map/ppermute | solution.py:211
  82.2 2.4 %collective-permute-start.28 = (bf16[1024,128]{1,0:T(8,128)(2,1)}, bf16[1024,128]{1,0:T(8,128)(2,1)}, u32[]{:S(2)}, u32[]{:S(2)}) collective-permute-start(bf16[1024,128]{1,0:T(8,128)(2,1)} %collective-permute-done.16.refs_15_), channel_id=1, source_target_pairs={{0,1},{1,0},{2,3},{3,2},{4,5},{5,4},{6,7},{7,6},{8,9},{9,8},{10,11... | collective-permute-start | bytes 786440 | tf_op jit(solution)/shard_map/ppermute | solution.py:211
  83.1 2.2 %collective-permute-start.30 = (bf16[1024,128]{1,0:T(8,128)(2,1)}, bf16[1024,128]{1,0:T(8,128)(2,1)}, u32[]{:S(2)}, u32[]{:S(2)}) collective-permute-start(bf16[1024,128]{1,0:T(8,128)(2,1)} %collective-permute-done.18.refs_17_), channel_id=1, source_target_pairs={{0,1},{1,0},{2,3},{3,2},{4,5},{5,4},{6,7},{7,6},{8,9},{9,8},{10,11... | collective-permute-start | bytes 786440 | tf_op jit(solution)/shard_map/ppermute | solution.py:211
  83.5 1.8 %copy-start.29 = (bf16[1024,128]{1,0:T(8,128)(2,1)}, bf16[1024,128]{1,0:T(8,128)(2,1)S(1)}, u32[]{:S(2)}) copy-start(bf16[1024,128]{1,0:T(8,128)(2,1)S(1)} %collective-permute-done.27.refs_30_) | copy-start | bytes 786436

commit v7 on v6

--- a/solution.py
+++ b/solution.py
@@ -136,14 +136,18 @@
     def departure(step):
         return pltpu.make_async_copy(out.at[step], block(out_ref, step), out_sems.at[step])
 
-    held_arrival = pltpu.make_async_copy(held_ref, held, held_sem)
-    held_arrival.start()
+    def held_arrival(part):
+        there = pl.ds(part, GROUP)
+        return pltpu.make_async_copy(held_ref.at[there], held.at[there], held_sem.at[part // GROUP])
+
+    for part in range(0, PARTS, GROUP):
+        held_arrival(part).start()
     for step in range(steps):
         for copy in (*root_arrivals(0, step), *root_arrivals(1, step), momentum_arrival(step)):
             copy.start()
     order = order_matrix(rows, hidden, experts)
-    held_arrival.wait()
     for part in range(0, PARTS, GROUP):
+        held_arrival(part).wait()
         some = jnp.concatenate([held[part + k] for k in range(GROUP)], axis=1)
         moved = jnp.dot(order, some, preferred_element_type=jnp.float32).astype(jnp.bfloat16)
         at = (part % per_half) * LANES
@@ -194,7 +198,7 @@
             pltpu.VMEM((2, steps, 2, *own[0].shape), jnp.bfloat16),
             pltpu.VMEM((steps, rows, columns), jnp.float32),
             pltpu.VMEM((steps, rows, columns), jnp.float32),
-            pltpu.SemaphoreType.DMA,
+            pltpu.SemaphoreType.DMA((PARTS // GROUP,)),
             pltpu.SemaphoreType.DMA((2, pieces)),
             pltpu.SemaphoreType.DMA((steps,)),
             pltpu.SemaphoreType.DMA((steps,)),

time: 96.1 us -> 96 us (level)
  no operation moved by 1% of the time
where the time goes in v7:
time: 96 us; the launch traced here: 95.8 us
  starting transfers between devices  56.6 us (59%)
  waiting for transfers between devices  17.6 us (18%)
  Pallas kernels  16.1 us (17%)
  local copies, waits for them, and re-layouts  5.02 us (5%)
    ppermute x10, starting transfers between devices, along_z(): return lax.ppermute(value, 'z', [(i, (i + step) % n) for i in range(n)])  19.6 us
    ppermute x16, starting transfers between devices, swap(): return lax.ppermute(value, axis, [(0, 1), (1, 0)])  14.4 us
    all_to_all x2, starting transfers between devices, exchange(): return lax.all_to_all(value, EXP, split_axis=0, concat_axis=0, tiled=True)  12.9 us
    ppermute x10, waiting for transfers between devices, along_z(): return lax.ppermute(value, 'z', [(i, (i + step) % n) for i in range(n)])  10.3 us
    pallas_call x1, Pallas kernels, finished(): pl.pallas_call(lambda *refs: finish_kernel(experts, hidden, pieces, *refs...  10.3 us
    ppermute x5, starting transfers between devices, across(): lax.ppermute(value, ('yh', 'yl'), [(place, 3 - place) for place in range(...  9.66 us
    ppermute x5, waiting for transfers between devices, across(): lax.ppermute(value, ('yh', 'yl'), [(place, 3 - place) for place in range(...  5.49 us
    unnamed x61, local copies, waits for them, and re-layouts  4.91 us
  transfers between devices with their start and end apart: 33, of which 10 were waited for; matrix products, arithmetic and copies ran while one was open for 0% of the time, Pallas kernels for 0%

profile of v7, /device:TPU:1, one launch (start us, length us, event | category | flops | bytes accessed | tf_op | source)
XLA Modules:
  0.0 95.8 jit_solution(6754958138558920196)
XLA Ops:
  0.0 1.0 %copy-done = bf16[128,2048]{1,0:T(8,128)(2,1)S(1)} copy-done((bf16[128,2048]{1,0:T(8,128)(2,1)S(1)}, bf16[128,2048]{1,0:T(8,128)(2,1)}, u32[]{:S(2)}) %copy-start) | copy-done | bytes 524312
  1.1 0.2 copy.6
  1.2 3.7 %slice_columns.1 = bf16[16,512,128]{2,1,0:T(8,128)(2,1)} custom-call(bf16[512,2048]{1,0:T(8,128)(2,1)} %bitcast.23), custom_call_target="tpu_custom_call" | custom-call | flops 1073741824 | bytes 4194304 | tf_op jit(solution)/shard_map/slice_columns/pallas_call | solution.py:56
  4.9 0.0 copy-start.1
  4.9 7.0 %all-to-all-start = ((bf16[16,512,128]{2,1,0:T(8,128)(2,1)}), bf16[16,512,128]{2,1,0:T(8,128)(2,1)S(1)}, u32[]{:S(2)}, u32[]{:S(2)}) async-start(bf16[16,512,128]{2,1,0:T(8,128)(2,1)} %slice_columns.1), calls=%async_computation | async-start | bytes 4194304 | tf_op jit(solution)/shard_map/all_to_all | solution.py:228
  11.9 1.6 %collective-permute-start.5 = (bf16[1024,128]{1,0:T(8,128)(2,1)S(1)}, bf16[1024,128]{1,0:T(8,128)(2,1)S(1)}, u32[]{:S(2)}, u32[]{:S(2)}) collective-permute-start(bf16[1024,128]{1,0:T(8,128)(2,1)S(1)} %bitcast.17), channel_id=1, source_target_pairs={{0,32},{32,64},{64,96},{96,128},{128,160},{160,192},{192,224},{224... | collective-permute-start | bytes 786440 | tf_op jit(solution)/shard_map/ppermute | solution.py:224
  13.5 4.0 %collective-permute-start.3 = (bf16[1024,128]{1,0:T(8,128)(2,1)S(1)}, bf16[1024,128]{1,0:T(8,128)(2,1)S(1)}, u32[]{:S(2)}, u32[]{:S(2)}) collective-permute-start(bf16[1024,128]{1,0:T(8,128)(2,1)S(1)} %bitcast.18), channel_id=1, source_target_pairs={{0,224},{32,0},{64,32},{96,64},{128,96},{160,128},{192,160},{224,1... | collective-permute-start | bytes 786440 | tf_op jit(solution)/shard_map/ppermute | solution.py:224
  17.6 2.8 %collective-permute-start.1 = (bf16[1024,128]{1,0:T(8,128)(2,1)S(1)}, bf16[1024,128]{1,0:T(8,128)(2,1)S(1)}, u32[]{:S(2)}, u32[]{:S(2)}) collective-permute-start(bf16[1024,128]{1,0:T(8,128)(2,1)S(1)} %bitcast.19), channel_id=1, source_target_pairs={{0,18},{2,16},{16,2},{18,0},{1,19},{3,17},{17,3},{19,1},{4,22},{6,... | collective-permute-start | bytes 786440 | tf_op jit(solution)/shard_map/ppermute | solution.py:219
  20.4 0.9 collective-permute-start
  21.3 2.8 %collective-permute-done.5.refs_6_ = bf16[1024,128]{1,0:T(8,128)(2,1)S(1)} collective-permute-done((bf16[1024,128]{1,0:T(8,128)(2,1)S(1)}, bf16[1024,128]{1,0:T(8,128)(2,1)S(1)}, u32[]{:S(2)}, u32[]{:S(2)}) %collective-permute-start.5) | collective-permute-done | bytes 262176 | tf_op jit(solution)/shard_map/ppermute | solution.py:224
  24.1 2.6 %collective-permute-start.10 = (bf16[1024,128]{1,0:T(8,128)(2,1)S(1)}, bf16[1024,128]{1,0:T(8,128)(2,1)S(1)}, u32[]{:S(2)}, u32[]{:S(2)}) collective-permute-start(bf16[1024,128]{1,0:T(8,128)(2,1)S(1)} %collective-permute-done.5.refs_6_), channel_id=1, source_target_pairs={{0,18},{2,16},{16,2},{18,0},{1,19},{3,17},{17,3},{19,1},{4,22},{6,... | collective-permute-start | bytes 786440 | tf_op jit(solution)/shard_map/ppermute | solution.py:219
  26.7 0.0 collective-permute-start.8
  26.7 0.0 collective-permute-done.3.refs_4_
  26.7 1.2 %collective-permute-start.6 = (bf16[1024,128]{1,0:T(8,128)(2,1)S(1)}, bf16[1024,128]{1,0:T(8,128)(2,1)S(1)}, u32[]{:S(2)}, u32[]{:S(2)}) collective-permute-start(bf16[1024,128]{1,0:T(8,128)(2,1)S(1)} %collective-permute-done.5.refs_6_), channel_id=1, source_target_pairs={{0,1},{1,0},{2,3},{3,2},{4,5},{5,4},{6,7},{7,6},{8,9},{9,8},{10,11... | collective-permute-start | bytes 786440 | tf_op jit(solution)/shard_map/ppermute | solution.py:215
  27.9 0.7 copy-done.2
  28.6 0.0 collective-permute-done.1.refs_3_
  28.6 0.3 collective-permute-start.9
  28.8 2.8 %collective-permute-start.7 = (bf16[1024,128]{1,0:T(8,128)(2,1)S(1)}, bf16[1024,128]{1,0:T(8,128)(2,1)S(1)}, u32[]{:S(2)}, u32[]{:S(2)}) collective-permute-start(bf16[1024,128]{1,0:T(8,128)(2,1)S(1)} %collective-permute-done.3.refs_4_), channel_id=1, source_target_pairs={{0,224},{32,0},{64,32},{96,64},{128,96},{160,128},{192,160},{224,1... | collective-permute-start | bytes 786440 | tf_op jit(solution)/shard_map/ppermute | solution.py:224
  31.6 0.9 collective-permute-done.10.refs_7_
  32.5 2.7 %collective-permute-start.4 = (bf16[1024,128]{1,0:T(8,128)(2,1)S(1)}, bf16[1024,128]{1,0:T(8,128)(2,1)S(1)}, u32[]{:S(2)}, u32[]{:S(2)}) collective-permute-start(bf16[1024,128]{1,0:T(8,128)(2,1)S(1)} %collective-permute-done.3.refs_4_), channel_id=1, source_target_pairs={{0,1},{1,0},{2,3},{3,2},{4,5},{5,4},{6,7},{7,6},{8,9},{9,8},{10,11... | collective-permute-start | bytes 786440 | tf_op jit(solution)/shard_map/ppermute | solution.py:215
  35.2 0.7 copy-done.4
  35.9 0.8 collective-permute-start.2
  36.6 0.7 copy-done.6
  37.3 0.8 collective-permute-done.9.refs_5_
  38.1 0.0 collective-permute-done.7.refs_8_
  38.1 0.7 copy-done.10
  38.8 0.1 copy-done.12
  38.9 0.7 copy-done.17
  39.7 2.1 %mix_experts.1 = bf16[16,16,32,128]{3,2,1,0:T(8,128)(2,1)} custom-call(bf16[512,512]{1,0:T(8,128)(2,1)S(1)} %copy-done.1, bf16[16,16,32,128]{3,2,1,0:T(8,128)(2,1)S(1)} %bitcast.16), custom_call_target="tpu_custom_call" | custom-call | tf_op jit(solution)/shard_map/mix_experts/pallas_call | solution.py:98
  41.9 5.9 %all-to-all-start.1 = ((bf16[16,512,128]{2,1,0:T(8,128)(2,1)}), bf16[16,512,128]{2,1,0:T(8,128)(2,1)}, u32[]{:S(2)}, u32[]{:S(2)}) async-start(bf16[16,512,128]{2,1,0:T(8,128)(2,1)} %bitcast.13), calls=%async_computation.1 | async-start | bytes 4194304 | tf_op jit(solution)/shard_map/all_to_all | solution.py:228
  47.8 3.8 %collective-permute-start.11 = (bf16[1024,128]{1,0:T(8,128)(2,1)S(1)}, bf16[1024,128]{1,0:T(8,128)(2,1)S(1)}, u32[]{:S(2)}, u32[]{:S(2)}) collective-permute-start(bf16[1024,128]{1,0:T(8,128)(2,1)S(1)} %copy-done.13), channel_id=1, source_target_pairs={{0,18},{2,16},{16,2},{18,0},{1,19},{3,17},{17,3},{19,1},{4,22},{6,... | collective-permute-start | bytes 786440 | tf_op jit(solution)/shard_map/ppermute | solution.py:219
  51.6 0.2 collective-permute-start.14
  51.8 3.9 %collective-permute-start.13 = (bf16[1024,128]{1,0:T(8,128)(2,1)S(1)}, bf16[1024,128]{1,0:T(8,128)(2,1)S(1)}, u32[]{:S(2)}, u32[]{:S(2)}) collective-permute-start(bf16[1024,128]{1,0:T(8,128)(2,1)S(1)} %copy-done.13), channel_id=1, source_target_pairs={{0,224},{32,0},{64,32},{96,64},{128,96},{160,128},{192,160},{224,1... | collective-permute-start | bytes 786440 | tf_op jit(solution)/shard_map/ppermute | solution.py:224
  55.7 0.2 collective-permute-start.12
  55.9 2.2 %collective-permute-done.11.refs_9_ = bf16[1024,128]{1,0:T(8,128)(2,1)S(1)} collective-permute-done((bf16[1024,128]{1,0:T(8,128)(2,1)S(1)}, bf16[1024,128]{1,0:T(8,128)(2,1)S(1)}, u32[]{:S(2)}, u32[]{:S(2)}) %collective-permute-start.11) | collective-permute-done | bytes 262176 | tf_op jit(solution)/shard_map/ppermute | solution.py:219
  58.1 4.3 %collective-permute-start.15 = (bf16[1024,128]{1,0:T(8,128)(2,1)S(1)}, bf16[1024,128]{1,0:T(8,128)(2,1)}, u32[]{:S(2)}, u32[]{:S(2)}) collective-permute-start(bf16[1024,128]{1,0:T(8,128)(2,1)S(1)} %collective-permute-done.11.refs_9_), channel_id=1, source_target_pairs={{0,224},{32,0},{64,32},{96,64},{128,96},{160,128},{192,160},{224,1... | collective-permute-start | bytes 786440 | tf_op jit(solution)/shard_map/ppermute | solution.py:224
  62.4 0.0 collective-permute-done.13.refs_12_
  62.5 1.7 %collective-permute-done.12.refs_11_ = bf16[1024,128]{1,0:T(8,128)(2,1)S(1)} collective-permute-done((bf16[1024,128]{1,0:T(8,128)(2,1)S(1)}, bf16[1024,128]{1,0:T(8,128)(2,1)S(1)}, u32[]{:S(2)}, u32[]{:S(2)}) %collective-permute-start.12) | collective-permute-done | bytes 262176 | tf_op jit(solution)/shard_map/ppermute | solution.py:219
  64.1 1.5 %collective-permute-start.19 = (bf16[1024,128]{1,0:T(8,128)(2,1)S(1)}, bf16[1024,128]{1,0:T(8,128)(2,1)S(1)}, u32[]{:S(2)}, u32[]{:S(2)}) collective-permute-start(bf16[1024,128]{1,0:T(8,128)(2,1)S(1)} %copy-done.11), channel_id=1, source_target_pairs={{0,1},{1,0},{2,3},{3,2},{4,5},{5,4},{6,7},{7,6},{8,9},{9,8},{10,11... | collective-permute-start | bytes 786440 | tf_op jit(solution)/shard_map/ppermute | solution.py:215
  65.7 0.1 collective-permute-start.20
  65.8 0.4 collective-permute-start.21
  66.2 1.0 %collective-permute-done.15.refs_13_ = bf16[1024,128]{1,0:T(8,128)(2,1)} collective-permute-done((bf16[1024,128]{1,0:T(8,128)(2,1)S(1)}, bf16[1024,128]{1,0:T(8,128)(2,1)}, u32[]{:S(2)}, u32[]{:S(2)}) %collective-permute-start.15) | collective-permute-done | bytes 262176 | tf_op jit(solution)/shard_map/ppermute | solution.py:224
  67.2 1.8 %collective-permute-start.22 = (bf16[1024,128]{1,0:T(8,128)(2,1)S(1)}, bf16[1024,128]{1,0:T(8,128)(2,1)S(1)}, u32[]{:S(2)}, u32[]{:S(2)}) collective-permute-start(bf16[1024,128]{1,0:T(8,128)(2,1)S(1)} %collective-permute-done.11.refs_9_), channel_id=1, source_target_pairs={{0,1},{1,0},{2,3},{3,2},{4,5},{5,4},{6,7},{7,6},{8,9},{9,8},{10,11... | collective-permute-start | bytes 786440 | tf_op jit(solution)/shard_map/ppermute | solution.py:215
  68.9 1.4 %collective-permute-done.17.refs_16_ = bf16[1024,128]{1,0:T(8,128)(2,1)} collective-permute-done((bf16[1024,128]{1,0:T(8,128)(2,1)S(1)}, bf16[1024,128]{1,0:T(8,128)(2,1)}, u32[]{:S(2)}, u32[]{:S(2)}) %collective-permute-start.17) | collective-permute-done | bytes 262176 | tf_op jit(solution)/shard_map/ppermute | solution.py:224
  70.4 2.1 %collective-permute-start.23 = (bf16[1024,128]{1,0:T(8,128)(2,1)S(1)}, bf16[1024,128]{1,0:T(8,128)(2,1)S(1)}, u32[]{:S(2)}, u32[]{:S(2)}) collective-permute-start(bf16[1024,128]{1,0:T(8,128)(2,1)S(1)} %copy-done.15), channel_id=1, source_target_pairs={{0,1},{1,0},{2,3},{3,2},{4,5},{5,4},{6,7},{7,6},{8,9},{9,8},{10,11... | collective-permute-start | bytes 786440 | tf_op jit(solution)/shard_map/ppermute | solution.py:215
  72.5 0.0 collective-permute-done.19.refs_21_
  72.5 0.1 collective-permute-start.24
  72.6 0.4 collective-permute-start.25
  73.0 0.0 collective-permute-done.22.refs_25_
  73.0 2.7 %collective-permute-start.18 = (bf16[1024,128]{1,0:T(8,128)(2,1)}, bf16[1024,128]{1,0:T(8,128)(2,1)}, u32[]{:S(2)}, u32[]{:S(2)}) collective-permute-start(bf16[1024,128]{1,0:T(8,128)(2,1)} %collective-permute-done.15.refs_13_), channel_id=1, source_target_pairs={{0,224},{32,0},{64,32},{96,64},{128,96},{160,128},{192,160},{224,1... | collective-permute-start | bytes 786440 | tf_op jit(solution)/shard_map/ppermute | solution.py:224
  75.7 0.0 collective-permute-done.23.refs_26_
  75.7 0.7 collective-permute-start.27
  76.4 0.0 collective-permute-done.24.refs_27_
  76.4 0.1 collective-permute-start.26
  76.6 0.5 collective-permute-start.29
  77.0 5.1 %collective-permute-done.16.refs_15_ = bf16[1024,128]{1,0:T(8,128)(2,1)} collective-permute-done((bf16[1024,128]{1,0:T(8,128)(2,1)S(1)}, bf16[1024,128]{1,0:T(8,128)(2,1)}, u32[]{:S(2)}, u32[]{:S(2)}) %collective-permute-start.16) | collective-permute-done | bytes 262176 | tf_op jit(solution)/shard_map/ppermute | solution.py:224
  82.2 0.9 collective-permute-start.28
  83.1 0.0 collective-permute-done.18.refs_17_
  83.1 0.3 collective-permute-start.30
  83.4 0.1 stack.43.refs_0_
  83.6 0.0 collective-permute-done.29.refs_32_
  83.6 1.0 %collective-permute-done.28.refs_31_ = bf16[1024,128]{1,0:T(8,128)(2,1)} collective-permute-done((bf16[1024,128]{1,0:T(8,128)(2,1)}, bf16[1024,128]{1,0:T(8,128)(2,1)}, u32[]{:S(2)}, u32[]{:S(2)}) %collective-permute-start.28) | collective-permute-done | bytes 262176 | tf_op jit(solution)/shard_map/ppermute | solution.py:215
  84.6 0.7 collective-permute-done.30.refs_33_
  85.3 10.3 %model_rows.1 = f32[512,2048]{1,0:T(8,128)} custom-call(s32[10]{0:T(128)S(1)} %stack.43.refs_0_, bf16[16,512,128]{2,1,0:T(8,128)(2,1)} %all-to-all-done.1.refs_1_, bf16[1024,128]{1,0:T(8,128)(2,1)S(1)} %bitcast.21, bf16[1024,128]{1,0:T(8,128)(2,1)S(1)} %copy-done.7, bf16[1024,128]{1,0:T(8,128)(2,1)S(1)} %copy-done.5, bf16[1024,128]{1,0:T(8,128)(2,1)S(1)} %copy-done.11, ...), custom_call_target="tpu_custom_call" | custom-call | flops 4294967296 | bytes 18874368 | tf_op jit(solution)/shard_map/model_rows/pallas_call | solution.py:190
  (68 shorter events, 0.2 us)
Async XLA Ops:
  0.0 1.0 %copy-start = (bf16[128,2048]{1,0:T(8,128)(2,1)S(1)}, bf16[128,2048]{1,0:T(8,128)(2,1)}, u32[]{:S(2)}) copy-start(bf16[128,2048]{1,0:T(8,128)(2,1)} %param.6) | copy-start | bytes 1572868
  4.9 34.7 %copy-start.1 = (bf16[512,512]{1,0:T(8,128)(2,1)S(1)}, bf16[512,512]{1,0:T(8,128)(2,1)}, u32[]{:S(2)}) copy-start(bf16[512,512]{1,0:T(8,128)(2,1)} %root_ref.1) | copy-start | bytes 1572868
  4.9 34.7 %all-to-all-start = ((bf16[16,512,128]{2,1,0:T(8,128)(2,1)}), bf16[16,512,128]{2,1,0:T(8,128)(2,1)S(1)}, u32[]{:S(2)}, u32[]{:S(2)}) async-start(bf16[16,512,128]{2,1,0:T(8,128)(2,1)} %slice_columns.1), calls=%async_computation | async-start | bytes 4194304 | tf_op jit(solution)/shard_map/all_to_all | solution.py:228
  11.9 12.2 %collective-permute-start.5 = (bf16[1024,128]{1,0:T(8,128)(2,1)S(1)}, bf16[1024,128]{1,0:T(8,128)(2,1)S(1)}, u32[]{:S(2)}, u32[]{:S(2)}) collective-permute-start(bf16[1024,128]{1,0:T(8,128)(2,1)S(1)} %bitcast.17), channel_id=1, source_target_pairs={{0,32},{32,64},{64,96},{96,128},{128,160},{160,192},{192,224},{224... | collective-permute-start | bytes 786440 | tf_op jit(solution)/shard_map/ppermute | solution.py:224
  13.5 13.2 %collective-permute-start.3 = (bf16[1024,128]{1,0:T(8,128)(2,1)S(1)}, bf16[1024,128]{1,0:T(8,128)(2,1)S(1)}, u32[]{:S(2)}, u32[]{:S(2)}) collective-permute-start(bf16[1024,128]{1,0:T(8,128)(2,1)S(1)} %bitcast.18), channel_id=1, source_target_pairs={{0,224},{32,0},{64,32},{96,64},{128,96},{160,128},{192,160},{224,1... | collective-permute-start | bytes 786440 | tf_op jit(solution)/shard_map/ppermute | solution.py:224
  17.6 11.0 %collective-permute-start.1 = (bf16[1024,128]{1,0:T(8,128)(2,1)S(1)}, bf16[1024,128]{1,0:T(8,128)(2,1)S(1)}, u32[]{:S(2)}, u32[]{:S(2)}) collective-permute-start(bf16[1024,128]{1,0:T(8,128)(2,1)S(1)} %bitcast.19), channel_id=1, source_target_pairs={{0,18},{2,16},{16,2},{18,0},{1,19},{3,17},{17,3},{19,1},{4,22},{6,... | collective-permute-start | bytes 786440 | tf_op jit(solution)/shard_map/ppermute | solution.py:219
  20.4 8.4 %collective-permute-start = (bf16[1024,128]{1,0:T(8,128)(2,1)S(1)}, bf16[1024,128]{1,0:T(8,128)(2,1)}, u32[]{:S(2)}, u32[]{:S(2)}) collective-permute-start(bf16[1024,128]{1,0:T(8,128)(2,1)S(1)} %bitcast.20), channel_id=1, source_target_pairs={{0,1},{1,0},{2,3},{3,2},{4,5},{5,4},{6,7},{7,6},{8,9},{9,8},{10,11... | collective-permute-start | bytes 786440 | tf_op jit(solution)/shard_map/ppermute | solution.py:215
  24.1 8.4 %collective-permute-start.10 = (bf16[1024,128]{1,0:T(8,128)(2,1)S(1)}, bf16[1024,128]{1,0:T(8,128)(2,1)S(1)}, u32[]{:S(2)}, u32[]{:S(2)}) collective-permute-start(bf16[1024,128]{1,0:T(8,128)(2,1)S(1)} %collective-permute-done.5.refs_6_), channel_id=1, source_target_pairs={{0,18},{2,16},{16,2},{18,0},{1,19},{3,17},{17,3},{19,1},{4,22},{6,... | collective-permute-start | bytes 786440 | tf_op jit(solution)/shard_map/ppermute | solution.py:219
  26.7 9.2 %collective-permute-start.8 = (bf16[1024,128]{1,0:T(8,128)(2,1)S(1)}, bf16[1024,128]{1,0:T(8,128)(2,1)S(1)}, u32[]{:S(2)}, u32[]{:S(2)}) collective-permute-start(bf16[1024,128]{1,0:T(8,128)(2,1)S(1)} %collective-permute-done.5.refs_6_), channel_id=1, source_target_pairs={{0,32},{32,64},{64,96},{96,128},{128,160},{160,192},{192,224},{224... | collective-permute-start | bytes 786440 | tf_op jit(solution)/shard_map/ppermute | solution.py:224
  26.7 10.6 %collective-permute-start.6 = (bf16[1024,128]{1,0:T(8,128)(2,1)S(1)}, bf16[1024,128]{1,0:T(8,128)(2,1)S(1)}, u32[]{:S(2)}, u32[]{:S(2)}) collective-permute-start(bf16[1024,128]{1,0:T(8,128)(2,1)S(1)} %collective-permute-done.5.refs_6_), channel_id=1, source_target_pairs={{0,1},{1,0},{2,3},{3,2},{4,5},{5,4},{6,7},{7,6},{8,9},{9,8},{10,11... | collective-permute-start | bytes 786440 | tf_op jit(solution)/shard_map/ppermute | solution.py:215
  27.9 0.7 copy-start.2
  28.6 9.5 %collective-permute-start.9 = (bf16[1024,128]{1,0:T(8,128)(2,1)S(1)}, bf16[1024,128]{1,0:T(8,128)(2,1)S(1)}, u32[]{:S(2)}, u32[]{:S(2)}) collective-permute-start(bf16[1024,128]{1,0:T(8,128)(2,1)S(1)} %collective-permute-done.3.refs_4_), channel_id=1, source_target_pairs={{0,18},{2,16},{16,2},{18,0},{1,19},{3,17},{17,3},{19,1},{4,22},{6,... | collective-permute-start | bytes 786440 | tf_op jit(solution)/shard_map/ppermute | solution.py:219
  28.8 9.3 %collective-permute-start.7 = (bf16[1024,128]{1,0:T(8,128)(2,1)S(1)}, bf16[1024,128]{1,0:T(8,128)(2,1)S(1)}, u32[]{:S(2)}, u32[]{:S(2)}) collective-permute-start(bf16[1024,128]{1,0:T(8,128)(2,1)S(1)} %collective-permute-done.3.refs_4_), channel_id=1, source_target_pairs={{0,224},{32,0},{64,32},{96,64},{128,96},{160,128},{192,160},{224,1... | collective-permute-start | bytes 786440 | tf_op jit(solution)/shard_map/ppermute | solution.py:224
  32.5 5.6 %copy-start.8 = (bf16[1024,128]{1,0:T(8,128)(2,1)}, bf16[1024,128]{1,0:T(8,128)(2,1)S(1)}, u32[]{:S(2)}) copy-start(bf16[1024,128]{1,0:T(8,128)(2,1)S(1)} %collective-permute-done.10.refs_7_) | copy-start | bytes 786436
  32.5 5.6 %collective-permute-start.4 = (bf16[1024,128]{1,0:T(8,128)(2,1)S(1)}, bf16[1024,128]{1,0:T(8,128)(2,1)S(1)}, u32[]{:S(2)}, u32[]{:S(2)}) collective-permute-start(bf16[1024,128]{1,0:T(8,128)(2,1)S(1)} %collective-permute-done.3.refs_4_), channel_id=1, source_target_pairs={{0,1},{1,0},{2,3},{3,2},{4,5},{5,4},{6,7},{7,6},{8,9},{9,8},{10,11... | collective-permute-start | bytes 786440 | tf_op jit(solution)/shard_map/ppermute | solution.py:215
  35.2 0.7 copy-start.4
  35.9 2.3 %copy-start.14 = (bf16[1024,128]{1,0:T(8,128)(2,1)}, bf16[1024,128]{1,0:T(8,128)(2,1)S(1)}, u32[]{:S(2)}) copy-start(bf16[1024,128]{1,0:T(8,128)(2,1)S(1)} %collective-permute-done.8.refs_10_) | copy-start | bytes 786436
  35.9 3.8 %collective-permute-start.2 = (bf16[1024,128]{1,0:T(8,128)(2,1)S(1)}, bf16[1024,128]{1,0:T(8,128)(2,1)}, u32[]{:S(2)}, u32[]{:S(2)}) collective-permute-start(bf16[1024,128]{1,0:T(8,128)(2,1)S(1)} %collective-permute-done.1.refs_3_), channel_id=1, source_target_pairs={{0,1},{1,0},{2,3},{3,2},{4,5},{5,4},{6,7},{7,6},{8,9},{9,8},{10,11... | collective-permute-start | bytes 786440 | tf_op jit(solution)/shard_map/ppermute | solution.py:215
  36.6 0.7 copy-start.6
  37.3 0.8 copy-start.16
  38.1 0.7 copy-start.10
  38.1 0.8 copy-start.12
  38.9 0.7 copy-start.17
  41.8 6.0 %copy-start.13 = (bf16[1024,128]{1,0:T(8,128)(2,1)S(1)}, bf16[1024,128]{1,0:T(8,128)(2,1)}, u32[]{:S(2)}) copy-start(bf16[1024,128]{1,0:T(8,128)(2,1)} %copy-done.12) | copy-start | bytes 786436
  41.8 9.8 %copy-start.15 = (bf16[1024,128]{1,0:T(8,128)(2,1)S(1)}, bf16[1024,128]{1,0:T(8,128)(2,1)}, u32[]{:S(2)}) copy-start(bf16[1024,128]{1,0:T(8,128)(2,1)} %copy-done.14) | copy-start | bytes 786436
  41.8 22.3 %copy-start.11 = (bf16[1024,128]{1,0:T(8,128)(2,1)S(1)}, bf16[1024,128]{1,0:T(8,128)(2,1)}, u32[]{:S(2)}) copy-start(bf16[1024,128]{1,0:T(8,128)(2,1)} %copy-done.10) | copy-start | bytes 786436
  41.8 23.9 %copy-start.9 = (bf16[1024,128]{1,0:T(8,128)(2,1)S(1)}, bf16[1024,128]{1,0:T(8,128)(2,1)}, u32[]{:S(2)}) copy-start(bf16[1024,128]{1,0:T(8,128)(2,1)} %copy-done.8) | copy-start | bytes 786436
  41.8 43.5 %copy-start.3 = (bf16[1024,128]{1,0:T(8,128)(2,1)S(1)}, bf16[1024,128]{1,0:T(8,128)(2,1)}, u32[]{:S(2)}) copy-start(bf16[1024,128]{1,0:T(8,128)(2,1)} %copy-done.2) | copy-start | bytes 786436
  41.8 43.5 %copy-start.5 = (bf16[1024,128]{1,0:T(8,128)(2,1)S(1)}, bf16[1024,128]{1,0:T(8,128)(2,1)}, u32[]{:S(2)}) copy-start(bf16[1024,128]{1,0:T(8,128)(2,1)} %copy-done.4) | copy-start | bytes 786436
  41.9 43.5 %copy-start.7 = (bf16[1024,128]{1,0:T(8,128)(2,1)S(1)}, bf16[1024,128]{1,0:T(8,128)(2,1)}, u32[]{:S(2)}) copy-start(bf16[1024,128]{1,0:T(8,128)(2,1)} %copy-done.6) | copy-start | bytes 786436
  41.9 43.4 %all-to-all-start.1 = ((bf16[16,512,128]{2,1,0:T(8,128)(2,1)}), bf16[16,512,128]{2,1,0:T(8,128)(2,1)}, u32[]{:S(2)}, u32[]{:S(2)}) async-start(bf16[16,512,128]{2,1,0:T(8,128)(2,1)} %bitcast.13), calls=%async_computation.1 | async-start | bytes 4194304 | tf_op jit(solution)/shard_map/all_to_all | solution.py:228
  47.8 10.3 %collective-permute-start.11 = (bf16[1024,128]{1,0:T(8,128)(2,1)S(1)}, bf16[1024,128]{1,0:T(8,128)(2,1)S(1)}, u32[]{:S(2)}, u32[]{:S(2)}) collective-permute-start(bf16[1024,128]{1,0:T(8,128)(2,1)S(1)} %copy-done.13), channel_id=1, source_target_pairs={{0,18},{2,16},{16,2},{18,0},{1,19},{3,17},{17,3},{19,1},{4,22},{6,... | collective-permute-start | bytes 786440 | tf_op jit(solution)/shard_map/ppermute | solution.py:219
  51.6 10.8 %collective-permute-start.14 = (bf16[1024,128]{1,0:T(8,128)(2,1)S(1)}, bf16[1024,128]{1,0:T(8,128)(2,1)S(1)}, u32[]{:S(2)}, u32[]{:S(2)}) collective-permute-start(bf16[1024,128]{1,0:T(8,128)(2,1)S(1)} %copy-done.15), channel_id=1, source_target_pairs={{0,32},{32,64},{64,96},{96,128},{128,160},{160,192},{192,224},{224... | collective-permute-start | bytes 786440 | tf_op jit(solution)/shard_map/ppermute | solution.py:224
  51.8 10.6 %collective-permute-start.13 = (bf16[1024,128]{1,0:T(8,128)(2,1)S(1)}, bf16[1024,128]{1,0:T(8,128)(2,1)S(1)}, u32[]{:S(2)}, u32[]{:S(2)}) collective-permute-start(bf16[1024,128]{1,0:T(8,128)(2,1)S(1)} %copy-done.13), channel_id=1, source_target_pairs={{0,224},{32,0},{64,32},{96,64},{128,96},{160,128},{192,160},{224,1... | collective-permute-start | bytes 786440 | tf_op jit(solution)/shard_map/ppermute | solution.py:224
  55.7 8.4 %collective-permute-start.12 = (bf16[1024,128]{1,0:T(8,128)(2,1)S(1)}, bf16[1024,128]{1,0:T(8,128)(2,1)S(1)}, u32[]{:S(2)}, u32[]{:S(2)}) collective-permute-start(bf16[1024,128]{1,0:T(8,128)(2,1)S(1)} %copy-done.15), channel_id=1, source_target_pairs={{0,18},{2,16},{16,2},{18,0},{1,19},{3,17},{17,3},{19,1},{4,22},{6,... | collective-permute-start | bytes 786440 | tf_op jit(solution)/shard_map/ppermute | solution.py:219
  58.1 27.2 %copy-start.18 = (bf16[1024,128]{1,0:T(8,128)(2,1)}, bf16[1024,128]{1,0:T(8,128)(2,1)S(1)}, u32[]{:S(2)}) copy-start(bf16[1024,128]{1,0:T(8,128)(2,1)S(1)} %collective-permute-done.11.refs_9_) | copy-start | bytes 786436
  58.1 9.1 %collective-permute-start.15 = (bf16[1024,128]{1,0:T(8,128)(2,1)S(1)}, bf16[1024,128]{1,0:T(8,128)(2,1)}, u32[]{:S(2)}, u32[]{:S(2)}) collective-permute-start(bf16[1024,128]{1,0:T(8,128)(2,1)S(1)} %collective-permute-done.11.refs_9_), channel_id=1, source_target_pairs={{0,224},{32,0},{64,32},{96,64},{128,96},{160,128},{192,160},{224,1... | collective-permute-start | bytes 786440 | tf_op jit(solution)/shard_map/ppermute | solution.py:224
  62.4 22.9 %copy-start.19 = (bf16[1024,128]{1,0:T(8,128)(2,1)}, bf16[1024,128]{1,0:T(8,128)(2,1)S(1)}, u32[]{:S(2)}) copy-start(bf16[1024,128]{1,0:T(8,128)(2,1)S(1)} %collective-permute-done.14.refs_14_) | copy-start | bytes 786436
  62.4 8.0 %collective-permute-start.17 = (bf16[1024,128]{1,0:T(8,128)(2,1)S(1)}, bf16[1024,128]{1,0:T(8,128)(2,1)}, u32[]{:S(2)}, u32[]{:S(2)}) collective-permute-start(bf16[1024,128]{1,0:T(8,128)(2,1)S(1)} %collective-permute-done.14.refs_14_), channel_id=1, source_target_pairs={{0,32},{32,64},{64,96},{96,128},{128,160},{160,192},{192,224},{224... | collective-permute-start | bytes 786440 | tf_op jit(solution)/shard_map/ppermute | solution.py:224
  62.4 13.3 %copy-start.20 = (bf16[1024,128]{1,0:T(8,128)(2,1)}, bf16[1024,128]{1,0:T(8,128)(2,1)S(1)}, u32[]{:S(2)}) copy-start(bf16[1024,128]{1,0:T(8,128)(2,1)S(1)} %collective-permute-done.13.refs_12_) | copy-start | bytes 786436
  64.1 12.4 %copy-start.21 = (bf16[1024,128]{1,0:T(8,128)(2,1)}, bf16[1024,128]{1,0:T(8,128)(2,1)S(1)}, u32[]{:S(2)}) copy-start(bf16[1024,128]{1,0:T(8,128)(2,1)S(1)} %collective-permute-done.12.refs_11_) | copy-start | bytes 786436
  64.1 8.3 %collective-permute-start.19 = (bf16[1024,128]{1,0:T(8,128)(2,1)S(1)}, bf16[1024,128]{1,0:T(8,128)(2,1)S(1)}, u32[]{:S(2)}, u32[]{:S(2)}) collective-permute-start(bf16[1024,128]{1,0:T(8,128)(2,1)S(1)} %copy-done.11), channel_id=1, source_target_pairs={{0,1},{1,0},{2,3},{3,2},{4,5},{5,4},{6,7},{7,6},{8,9},{9,8},{10,11... | collective-permute-start | bytes 786440 | tf_op jit(solution)/shard_map/ppermute | solution.py:215
  65.7 6.9 %collective-permute-start.20 = (bf16[1024,128]{1,0:T(8,128)(2,1)S(1)}, bf16[1024,128]{1,0:T(8,128)(2,1)S(1)}, u32[]{:S(2)}, u32[]{:S(2)}) collective-permute-start(bf16[1024,128]{1,0:T(8,128)(2,1)S(1)} %copy-done.9), channel_id=1, source_target_pairs={{0,1},{1,0},{2,3},{3,2},{4,5},{5,4},{6,7},{7,6},{8,9},{9,8},{10,11... | collective-permute-start | bytes 786440 | tf_op jit(solution)/shard_map/ppermute | solution.py:215
  65.8 7.2 %collective-permute-start.21 = (bf16[1024,128]{1,0:T(8,128)(2,1)S(1)}, bf16[1024,128]{1,0:T(8,128)(2,1)S(1)}, u32[]{:S(2)}, u32[]{:S(2)}) collective-permute-start(bf16[1024,128]{1,0:T(8,128)(2,1)S(1)} %copy-done.13), channel_id=1, source_target_pairs={{0,1},{1,0},{2,3},{3,2},{4,5},{5,4},{6,7},{7,6},{8,9},{9,8},{10,11... | collective-permute-start | bytes 786440 | tf_op jit(solution)/shard_map/ppermute | solution.py:215
  67.2 5.8 %collective-permute-start.22 = (bf16[1024,128]{1,0:T(8,128)(2,1)S(1)}, bf16[1024,128]{1,0:T(8,128)(2,1)S(1)}, u32[]{:S(2)}, u32[]{:S(2)}) collective-permute-start(bf16[1024,128]{1,0:T(8,128)(2,1)S(1)} %collective-permute-done.11.refs_9_), channel_id=1, source_target_pairs={{0,1},{1,0},{2,3},{3,2},{4,5},{5,4},{6,7},{7,6},{8,9},{9,8},{10,11... | collective-permute-start | bytes 786440 | tf_op jit(solution)/shard_map/ppermute | solution.py:215
  70.4 5.3 %collective-permute-start.23 = (bf16[1024,128]{1,0:T(8,128)(2,1)S(1)}, bf16[1024,128]{1,0:T(8,128)(2,1)S(1)}, u32[]{:S(2)}, u32[]{:S(2)}) collective-permute-start(bf16[1024,128]{1,0:T(8,128)(2,1)S(1)} %copy-done.15), channel_id=1, source_target_pairs={{0,1},{1,0},{2,3},{3,2},{4,5},{5,4},{6,7},{7,6},{8,9},{9,8},{10,11... | collective-permute-start | bytes 786440 | tf_op jit(solution)/shard_map/ppermute | solution.py:215
  72.5 9.7 %copy-start.22 = (bf16[1024,128]{1,0:T(8,128)(2,1)}, bf16[1024,128]{1,0:T(8,128)(2,1)S(1)}, u32[]{:S(2)}) copy-start(bf16[1024,128]{1,0:T(8,128)(2,1)S(1)} %collective-permute-done.19.refs_21_) | copy-start | bytes 786436
  72.5 4.0 %collective-permute-start.24 = (bf16[1024,128]{1,0:T(8,128)(2,1)S(1)}, bf16[1024,128]{1,0:T(8,128)(2,1)S(1)}, u32[]{:S(2)}, u32[]{:S(2)}) collective-permute-start(bf16[1024,128]{1,0:T(8,128)(2,1)S(1)} %collective-permute-done.12.refs_11_), channel_id=1, source_target_pairs={{0,1},{1,0},{2,3},{3,2},{4,5},{5,4},{6,7},{7,6},{8,9},{9,8},{10,11... | collective-permute-start | bytes 786440 | tf_op jit(solution)/shard_map/ppermute | solution.py:215
  72.6 10.5 %copy-start.23 = (bf16[1024,128]{1,0:T(8,128)(2,1)}, bf16[1024,128]{1,0:T(8,128)(2,1)S(1)}, u32[]{:S(2)}) copy-start(bf16[1024,128]{1,0:T(8,128)(2,1)S(1)} %collective-permute-done.20.refs_23_) | copy-start | bytes 786436
  72.6 4.0 %collective-permute-start.25 = (bf16[1024,128]{1,0:T(8,128)(2,1)S(1)}, bf16[1024,128]{1,0:T(8,128)(2,1)S(1)}, u32[]{:S(2)}, u32[]{:S(2)}) collective-permute-start(bf16[1024,128]{1,0:T(8,128)(2,1)S(1)} %collective-permute-done.13.refs_12_), channel_id=1, source_target_pairs={{0,1},{1,0},{2,3},{3,2},{4,5},{5,4},{6,7},{7,6},{8,9},{9,8},{10,11... | collective-permute-start | bytes 786440 | tf_op jit(solution)/shard_map/ppermute | solution.py:215
  73.0 10.1 %copy-start.24 = (bf16[1024,128]{1,0:T(8,128)(2,1)}, bf16[1024,128]{1,0:T(8,128)(2,1)S(1)}, u32[]{:S(2)}) copy-start(bf16[1024,128]{1,0:T(8,128)(2,1)S(1)} %collective-permute-done.21.refs_24_) | copy-start | bytes 786436
  73.0 9.2 %collective-permute-start.16 = (bf16[1024,128]{1,0:T(8,128)(2,1)S(1)}, bf16[1024,128]{1,0:T(8,128)(2,1)}, u32[]{:S(2)}, u32[]{:S(2)}) collective-permute-start(bf16[1024,128]{1,0:T(8,128)(2,1)S(1)} %collective-permute-done.12.refs_11_), channel_id=1, source_target_pairs={{0,32},{32,64},{64,96},{96,128},{128,160},{160,192},{192,224},{224... | collective-permute-start | bytes 786440 | tf_op jit(solution)/shard_map/ppermute | solution.py:224
  73.0 10.1 %copy-start.25 = (bf16[1024,128]{1,0:T(8,128)(2,1)}, bf16[1024,128]{1,0:T(8,128)(2,1)S(1)}, u32[]{:S(2)}) copy-start(bf16[1024,128]{1,0:T(8,128)(2,1)S(1)} %collective-permute-done.22.refs_25_) | copy-start | bytes 786436
  73.0 10.0 %collective-permute-start.18 = (bf16[1024,128]{1,0:T(8,128)(2,1)}, bf16[1024,128]{1,0:T(8,128)(2,1)}, u32[]{:S(2)}, u32[]{:S(2)}) collective-permute-start(bf16[1024,128]{1,0:T(8,128)(2,1)} %collective-permute-done.15.refs_13_), channel_id=1, source_target_pairs={{0,224},{32,0},{64,32},{96,64},{128,96},{160,128},{192,160},{224,1... | collective-permute-start | bytes 786440 | tf_op jit(solution)/shard_map/ppermute | solution.py:224
  75.7 7.4 %copy-start.26 = (bf16[1024,128]{1,0:T(8,128)(2,1)}, bf16[1024,128]{1,0:T(8,128)(2,1)S(1)}, u32[]{:S(2)}) copy-start(bf16[1024,128]{1,0:T(8,128)(2,1)S(1)} %collective-permute-done.23.refs_26_) | copy-start | bytes 786436
  75.7 7.8 %collective-permute-start.27 = (bf16[1024,128]{1,0:T(8,128)(2,1)S(1)}, bf16[1024,128]{1,0:T(8,128)(2,1)S(1)}, u32[]{:S(2)}, u32[]{:S(2)}) collective-permute-start(bf16[1024,128]{1,0:T(8,128)(2,1)S(1)} %collective-permute-done.14.refs_14_), channel_id=1, source_target_pairs={{0,1},{1,0},{2,3},{3,2},{4,5},{5,4},{6,7},{7,6},{8,9},{9,8},{10,11... | collective-permute-start | bytes 786440 | tf_op jit(solution)/shard_map/ppermute | solution.py:215
  76.4 6.7 %copy-start.27 = (bf16[1024,128]{1,0:T(8,128)(2,1)}, bf16[1024,128]{1,0:T(8,128)(2,1)S(1)}, u32[]{:S(2)}) copy-start(bf16[1024,128]{1,0:T(8,128)(2,1)S(1)} %collective-permute-done.24.refs_27_) | copy-start | bytes 786436
  76.4 7.1 %collective-permute-start.26 = (bf16[1024,128]{1,0:T(8,128)(2,1)}, bf16[1024,128]{1,0:T(8,128)(2,1)}, u32[]{:S(2)}, u32[]{:S(2)}) collective-permute-start(bf16[1024,128]{1,0:T(8,128)(2,1)} %collective-permute-done.15.refs_13_), channel_id=1, source_target_pairs={{0,1},{1,0},{2,3},{3,2},{4,5},{5,4},{6,7},{7,6},{8,9},{9,8},{10,11... | collective-permute-start | bytes 786440 | tf_op jit(solution)/shard_map/ppermute | solution.py:215
  76.6 6.5 %copy-start.28 = (bf16[1024,128]{1,0:T(8,128)(2,1)}, bf16[1024,128]{1,0:T(8,128)(2,1)S(1)}, u32[]{:S(2)}) copy-start(bf16[1024,128]{1,0:T(8,128)(2,1)S(1)} %collective-permute-done.25.refs_28_) | copy-start | bytes 786436
  76.6 7.0 %collective-permute-start.29 = (bf16[1024,128]{1,0:T(8,128)(2,1)}, bf16[1024,128]{1,0:T(8,128)(2,1)}, u32[]{:S(2)}, u32[]{:S(2)}) collective-permute-start(bf16[1024,128]{1,0:T(8,128)(2,1)} %collective-permute-done.17.refs_16_), channel_id=1, source_target_pairs={{0,1},{1,0},{2,3},{3,2},{4,5},{5,4},{6,7},{7,6},{8,9},{9,8},{10,11... | collective-permute-start | bytes 786440 | tf_op jit(solution)/shard_map/ppermute | solution.py:215
  82.2 2.4 %collective-permute-start.28 = (bf16[1024,128]{1,0:T(8,128)(2,1)}, bf16[1024,128]{1,0:T(8,128)(2,1)}, u32[]{:S(2)}, u32[]{:S(2)}) collective-permute-start(bf16[1024,128]{1,0:T(8,128)(2,1)} %collective-permute-done.16.refs_15_), channel_id=1, source_target_pairs={{0,1},{1,0},{2,3},{3,2},{4,5},{5,4},{6,7},{7,6},{8,9},{9,8},{10,11... | collective-permute-start | bytes 786440 | tf_op jit(solution)/shard_map/ppermute | solution.py:215
  83.1 2.2 %collective-permute-start.30 = (bf16[1024,128]{1,0:T(8,128)(2,1)}, bf16[1024,128]{1,0:T(8,128)(2,1)}, u32[]{:S(2)}, u32[]{:S(2)}) collective-permute-start(bf16[1024,128]{1,0:T(8,128)(2,1)} %collective-permute-done.18.refs_17_), channel_id=1, source_target_pairs={{0,1},{1,0},{2,3},{3,2},{4,5},{5,4},{6,7},{7,6},{8,9},{9,8},{10,11... | collective-permute-start | bytes 786440 | tf_op jit(solution)/shard_map/ppermute | solution.py:215
  83.5 1.8 %copy-start.29 = (bf16[1024,128]{1,0:T(8,128)(2,1)}, bf16[1024,128]{1,0:T(8,128)(2,1)S(1)}, u32[]{:S(2)}) copy-start(bf16[1024,128]{1,0:T(8,128)(2,1)S(1)} %collective-permute-done.27.refs_30_) | copy-start | bytes 786436
